TPU v7x, 32 devices: a whole 2x2x4 slice. The times are simulated.
32 devices in a mesh: groups: 2 (over x), gx: 16 (over z, y, core).
Axes of the slice: x: 2, y: 2, z: 4, core: 2. Of those that a mesh axis runs over, the one named last changes fastest.
Arguments:
- tokens: bfloat16 [1024, 16384], P('groups', 'gx'), parts along dimension 0, may hold values from -6 to 6
- token_scale: float32 [1024, 128], P('groups', 'gx'), parts along dimension 0, may hold values from 0.25 to 4
- gate_tiles: bfloat16 [16, 8192, 832], P('gx'), may hold values from -0.046875 to 0.046875
- up_tiles: bfloat16 [16, 8192, 832], P('gx'), may hold values from -0.046875 to 0.046875
- gate_scale: float32 [128, 52], replicated, may hold values from 0.25 to 4
- up_scale: float32 [128, 52], replicated, may hold values from 0.25 to 4
- down_tiles: bfloat16 [16, 832, 8192], P('gx'), may hold values from -0.078125 to 0.078125
- down_scale: float32 [52, 128], replicated, may hold values from 0.25 to 4
Outputs:
- mixed: bfloat16 [1024, 16384], P('groups', 'gx'), parts along dimension 0
There are 2 independent parts, one for each index of `groups`. A program takes and returns all parts, laid end to end along the dimension named above; an argument that names none is the same for every part. Nothing has to cross between parts.
All inputs are finite; a program needn't handle non-finite values.
Results may differ from a plain program's by a relative error of at most 0.0081.
Values may be sent and summed in bfloat16 or wider, within the bound.
A program may use at most 256 MiB of HBM per device.

v0:
```python
import jax
import jax.numpy as jnp
from jax import lax
from jax.sharding import PartitionSpec as P

BLK = 128
RO = 8


def partner(shard, axis, stride):
    return lax.ppermute(shard, axis, [(i, i ^ 1 << stride) for i in range(lax.axis_size(axis))])


def from_behind(shard, axis, by):
    devices = lax.axis_size(axis)
    return lax.ppermute(shard, axis, [(i, (i + by) % devices) for i in range(devices)])


def scale_by_columns(stored, blocks, row_start, col_start):
    height, width = stored.shape
    row_scales = lax.dynamic_slice_in_dim(blocks, row_start // BLK, height // BLK, 0)
    owner = (col_start + jnp.arange(width, dtype=jnp.int32)) // BLK
    select = (jnp.arange(blocks.shape[1], dtype=jnp.int32)[:, None] == owner[None, :]).astype(
        jnp.float32
    )
    factors = jnp.dot(row_scales, select, precision=lax.Precision.HIGHEST)
    scaled = stored.astype(jnp.float32).reshape(height // BLK, BLK, width) * factors[:, None, :]
    return scaled.reshape(height, width).astype(jnp.bfloat16)


def scale_by_rows(stored, blocks, row_start, col_start):
    height, width = stored.shape
    col_scales = lax.dynamic_slice_in_dim(blocks, col_start // BLK, width // BLK, 1)
    owner = (row_start + jnp.arange(height, dtype=jnp.int32)) // BLK
    select = (owner[:, None] == jnp.arange(blocks.shape[0], dtype=jnp.int32)[None, :]).astype(
        jnp.float32
    )
    factors = jnp.dot(select, col_scales, precision=lax.Precision.HIGHEST)
    scaled = stored.astype(jnp.float32).reshape(height, width // BLK, BLK) * factors[:, :, None]
    return scaled.reshape(height, width).astype(jnp.bfloat16)


def body(tokens, token_scale, gate_tiles, up_tiles, gate_scale, up_scale, down_tiles, down_scale):
    position = lax.axis_index("gx")
    devices = lax.axis_size("gx")
    row_groups = devices // RO
    levels = RO.bit_length() - 1
    col_slot = position % RO
    row_slot = position // RO
    token_count, slice_width = tokens.shape
    tile_rows = gate_tiles.shape[1]
    tile_cols = gate_tiles.shape[2]
    piece_cols = tile_cols // row_groups
    tokens_eff = (
        tokens.astype(jnp.float32).reshape(token_count, slice_width // BLK, BLK)
        * token_scale[:, :, None]
    )
    tokens_eff = tokens_eff.reshape(token_count, slice_width).astype(jnp.bfloat16)
    gate_eff = scale_by_columns(
        gate_tiles[0], gate_scale, row_slot * tile_rows, col_slot * tile_cols
    )
    up_eff = scale_by_columns(up_tiles[0], up_scale, row_slot * tile_rows, col_slot * tile_cols)
    joined = jnp.concatenate((gate_eff, up_eff), 1)
    gathered = tokens_eff
    for level in range(levels):
        other = partner(gathered, "gx", level)
        upper = col_slot // 2**level % 2 == 1
        first = jnp.where(upper, other, gathered)
        second = jnp.where(upper, gathered, other)
        gathered = jnp.concatenate((first, second), 1)
    partial_value = jnp.dot(gathered, joined, preferred_element_type=jnp.float32)
    stacked = jnp.stack((partial_value[:, :tile_cols], partial_value[:, tile_cols:]), 0)

    def share(target):
        return lax.dynamic_slice_in_dim(stacked, target * piece_cols, piece_cols, 2)

    summed = share((row_slot - 1) % row_groups)
    for step in range(1, row_groups):
        summed = from_behind(summed, "gx", RO)
        summed = summed + share((row_slot - 1 - step) % row_groups)
    hidden_piece = (jax.nn.silu(summed[0]) * summed[1]).astype(jnp.bfloat16)
    hidden_full = jnp.zeros((token_count, tile_cols), jnp.bfloat16)
    hidden_full = lax.dynamic_update_slice_in_dim(
        hidden_full, hidden_piece, row_slot * piece_cols, 1
    )
    current_hidden = hidden_piece
    for step in range(1, row_groups):
        current_hidden = from_behind(current_hidden, "gx", RO)
        source = (row_slot - step) % row_groups
        hidden_full = lax.dynamic_update_slice_in_dim(
            hidden_full, current_hidden, source * piece_cols, 1
        )
    down_eff = scale_by_rows(down_tiles[0], down_scale, col_slot * tile_cols, row_slot * tile_rows)
    result = jnp.dot(hidden_full, down_eff, preferred_element_type=jnp.float32)
    for level in reversed(range(levels)):
        half = result.shape[1] // 2
        lower_half = result[:, :half]
        upper_half = result[:, half:]
        upper = col_slot // 2**level % 2 == 1
        outgoing = jnp.where(upper, lower_half, upper_half)
        kept = jnp.where(upper, upper_half, lower_half)
        result = kept + partner(outgoing, "gx", level)
    return result.astype(jnp.bfloat16)


def solution(mesh):
    return jax.shard_map(
        body,
        mesh=mesh,
        in_specs=(
            P("groups", "gx"),
            P("groups", "gx"),
            P("gx", None, None),
            P("gx", None, None),
            P(),
            P(),
            P("gx", None, None),
            P(),
        ),
        out_specs=P("groups", "gx"),
        check_vma=False,
    )
```

profile of v0, /device:TPU:0, one launch (start us, length us, event | category | flops | bytes accessed | tf_op | source)
XLA Modules:
  0.0 668.5 jit_solution(9761176060917316105)
XLA Ops:
  0.0 0.0 copy-start
  0.0 0.8 copy.13
  0.9 0.6 mul.71
  1.5 1.8 fusion.16
  3.3 0.5 collective-permute-start
  3.8 2.4 collective-permute-done
  6.2 1.4 broadcast_select_fusion.5
  7.6 1.5 pad_maximum_fusion.1
  9.1 2.9 collective-permute-start.1
  12.0 0.0 copy-done
  12.0 0.6 fusion.21
  12.6 0.0 copy-done.3
  12.6 0.6 fusion.22
  13.2 45.1 %collective-permute-done.1 = bf16[512,2048]{1,0:T(8,128)(2,1)} collective-permute-done((bf16[512,2048]{1,0:T(8,128)(2,1)}, bf16[512,2048]{1,0:T(8,128)(2,1)}, u32[]{:S(2)}, u32[]{:S(2)}) %collective-permute-start.1) | collective-permute-done | bytes 2097184 | tf_op jit(solution)/shard_map/ppermute | solution.py:11
  58.3 2.7 broadcast_select_fusion.3
  61.0 2.3 pad_maximum_fusion
  63.3 1.8 collective-permute-start.2
  65.1 11.1 %mul.79 = f32[64,128,832]{1,0,2:T(8,128)} broadcast(f32[64,832]{0,1:T(8,128)S(1)} %fusion.21), dimensions={0,2} | broadcast | bytes 27475968 | tf_op jit(solution)/shard_map/mul | solution.py:27
  76.2 10.8 %mul.76 = f32[64,128,832]{1,0,2:T(8,128)} broadcast(f32[64,832]{0,1:T(8,128)S(1)} %fusion.22), dimensions={0,2} | broadcast | bytes 27475968 | tf_op jit(solution)/shard_map/mul | solution.py:27
  87.0 0.0 slice-done.4
  87.0 0.0 slice-done.5
  87.0 0.0 slice-done.6
  87.0 0.0 slice-done.7
  87.0 50.1 %fusion.1 = (bf16[8192,832]{0,1:T(8,128)(2,1)}, bf16[8192,832]{0,1:T(8,128)(2,1)}) fusion(f32[104,8,64,128]{3,2,1,0:T(8,128)} %bitcast.53, bf16[1,8192,832]{1,2,0:T(8,128)(2,1)S(1)} %bitcast.58, f32[104,8,64,128]{3,2,1,0:T(8,128)} %bitcast.54, bf16[1,8192,832]{1,2,0:T(8,128)(2,1)} %param.10), kind=kLoop, calls=%fused_computation.3 | loop fusion | flops 40894464 | bytes 109051904 | tf_op jit(solution)/shard_map/convert_element_type | solution.py:28
  137.2 18.5 %collective-permute-done.2 = bf16[512,4096]{1,0:T(8,128)(2,1)} collective-permute-done((bf16[512,4096]{1,0:T(8,128)(2,1)}, bf16[512,4096]{1,0:T(8,128)(2,1)}, u32[]{:S(2)}, u32[]{:S(2)}) %collective-permute-start.2) | collective-permute-done | bytes 4194336 | tf_op jit(solution)/shard_map/ppermute | solution.py:11
  155.7 4.4 broadcast_select_fusion.1
  160.1 21.9 %fusion.3 = f32[512,1664]{1,0:T(8,128)} fusion(bf16[8192,832]{0,1:T(8,128)(2,1)} %get-tuple-element.13, bf16[8192,832]{0,1:T(8,128)(2,1)} %get-tuple-element.14, bf16[512,4096]{1,0:T(8,128)(2,1)} %get-tuple-element.6, bf16[512,4096]{1,0:T(8,128)(2,1)S(1)} %get-tuple-element.5), kind=kOutput, calls=%fused_computation.6 | convolution fusion | flops 14029946880 | bytes 39059456 | tf_op jit(solution)/shard_map/dot_general | solution.py:71
  182.0 2.6 slice_bitcast_fusion
  184.6 0.0 copy-start.2
  184.6 1.2 copy-done.2
  185.9 2.0 fusion.15
  187.9 2.8 copy.16
  190.6 2.5 collective-permute-start.3
  193.1 73.1 %collective-permute-done.3 = f32[2,512,416]{1,2,0:T(8,128)} collective-permute-done((f32[2,512,416]{1,2,0:T(8,128)}, f32[2,512,416]{1,2,0:T(8,128)}, u32[]{:S(2)}, u32[]{:S(2)}) %collective-permute-start.3) | collective-permute-done | bytes 1703968 | tf_op jit(solution)/shard_map/ppermute | solution.py:16
  266.2 2.8 copy.17
  269.1 2.6 fusion.14
  271.7 0.0 slice-start
  271.7 0.3 fusion.18
  272.0 0.1 collective-permute-start.4
  272.1 0.0 copy-done.4
  272.1 0.4 fusion.19
  272.5 0.1 broadcast_in_dim.2
  272.6 4.3 dynamic_update_slice.6
  276.9 20.5 %collective-permute-done.4 = bf16[512,416]{1,0:T(8,128)(2,1)S(1)} collective-permute-done((bf16[512,416]{1,0:T(8,128)(2,1)S(1)}, bf16[512,416]{1,0:T(8,128)(2,1)S(1)}, u32[]{:S(2)}, u32[]{:S(2)}) %collective-permute-start.4) | collective-permute-done | bytes 426016 | tf_op jit(solution)/shard_map/ppermute | solution.py:16
  297.4 4.3 dynamic_update_slice.7
  301.7 0.0 slice-start.1
  301.7 0.0 slice-start.2
  301.7 0.0 slice-start.3
  301.7 12.6 %mul.87 = f32[832,64,128]{2,1,0:T(8,128)} broadcast(f32[832,64]{1,0:T(8,128)S(1)} %fusion.19), dimensions={0,1} | broadcast | bytes 27475968 | tf_op jit(solution)/shard_map/mul | solution.py:39
  314.3 0.0 slice-done.1
  314.3 54.3 %fusion.7 = f32[512,8192]{1,0:T(8,128)} fusion(bf16[512,832]{1,0:T(8,128)(2,1)S(1)} %dynamic_update_slice.7, f32[104,8,64,128]{3,2,1,0:T(8,128)} %bitcast.52, bf16[1,832,8192]{2,1,0:T(8,128)(2,1)S(1)} %bitcast.56), kind=kOutput, calls=%fused_computation.10 | convolution fusion | flops 6999769088 | bytes 58523648 | tf_op jit(solution)/shard_map/dot_general | solution.py:94
  368.6 11.2 %slice_select_fusion = f32[512,4096]{1,0:T(8,128)} fusion(f32[512,8192]{1,0:T(8,128)} %fusion.7, pred[]{:T(512)S(6)} %eq.58), kind=kLoop, calls=%fused_computation.16 | loop fusion | flops 2097152 | bytes 25165824 | tf_op jit(solution)/shard_map/jit(_where)/select_n | solution.py:100
  379.8 0.0 collective-permute-start.5
  379.8 181.6 %collective-permute-done.5 = f32[512,4096]{1,0:T(8,128)S(1)} collective-permute-done((f32[512,4096]{1,0:T(8,128)}, f32[512,4096]{1,0:T(8,128)S(1)}, u32[]{:S(2)}, u32[]{:S(2)}) %collective-permute-start.5) | collective-permute-done | bytes 8388640 | tf_op jit(solution)/shard_map/ppermute | solution.py:11
  561.4 6.9 %select_add_fusion = f32[512,4096]{1,0:T(8,128)S(1)} fusion(f32[512,4096]{1,0:T(8,128)S(1)} %collective-permute-done.5, f32[512,8192]{1,0:T(8,128)} %fusion.7, pred[]{:T(512)S(6)} %eq.58), kind=kLoop, calls=%fused_computation.15 | loop fusion | flops 4194304 | bytes 33554432 | tf_op jit(solution)/shard_map/add | solution.py:102
  568.4 1.1 slice_select_fusion.1
  569.4 0.1 collective-permute-start.6
  569.5 90.5 %collective-permute-done.6 = f32[512,2048]{1,0:T(8,128)S(1)} collective-permute-done((f32[512,2048]{1,0:T(8,128)S(1)}, f32[512,2048]{1,0:T(8,128)S(1)}, u32[]{:S(2)}, u32[]{:S(2)}) %collective-permute-start.6) | collective-permute-done | bytes 4194336 | tf_op jit(solution)/shard_map/ppermute | solution.py:11
  660.1 1.7 select_add_fusion.1
  661.8 0.0 copy-start.1
  661.8 0.4 slice_select_fusion.2
  662.2 0.1 collective-permute-start.7
  662.3 4.1 collective-permute-done.7
  666.5 1.6 add_convert_fusion
  (13 shorter events, 0.0 us)
Async XLA Ops:
  0.0 12.0 %copy-start = (f32[128,52]{0,1:T(8,128)S(1)}, f32[128,52]{0,1:T(8,128)}, u32[]{:S(2)}) copy-start(f32[128,52]{0,1:T(8,128)} %param.13) | copy-start | bytes 79876
  3.3 2.9 collective-permute-start
  3.8 8.8 %copy-start.3 = (f32[128,52]{0,1:T(8,128)S(1)}, f32[128,52]{0,1:T(8,128)}, u32[]{:S(2)}) copy-start(f32[128,52]{0,1:T(8,128)} %param.12) | copy-start | bytes 79876
  9.1 49.1 %collective-permute-start.1 = (bf16[512,2048]{1,0:T(8,128)(2,1)}, bf16[512,2048]{1,0:T(8,128)(2,1)}, u32[]{:S(2)}, u32[]{:S(2)}) collective-permute-start(bf16[512,2048]{1,0:T(8,128)(2,1)} %pad_maximum_fusion.1), channel_id=1, source_target_pairs={{0,2},{1,3},{2,0},{3,1},{4,6},{5,7},{6,4},{7,5},{8,10},{9,11},{10,... | collective-permute-start | bytes 6291464 | tf_op jit(solution)/shard_map/ppermute | solution.py:11
  63.3 92.4 %collective-permute-start.2 = (bf16[512,4096]{1,0:T(8,128)(2,1)}, bf16[512,4096]{1,0:T(8,128)(2,1)}, u32[]{:S(2)}, u32[]{:S(2)}) collective-permute-start(bf16[512,4096]{1,0:T(8,128)(2,1)} %pad_maximum_fusion), channel_id=1, source_target_pairs={{0,4},{1,5},{2,6},{3,7},{4,0},{5,1},{6,2},{7,3},{8,12},{9,13},{10,... | collective-permute-start | bytes 12582920 | tf_op jit(solution)/shard_map/ppermute | solution.py:11
  65.1 21.9 %slice-start.4 = ((s8[13631488]{0:T(1024)(128)(4,1)}), s8[4194304]{0:T(1024)(128)(4,1)S(1)}, s32[]{:S(2)}) async-start(s8[13631488]{0:T(1024)(128)(4,1)} %bitcast.57), calls=%async_computation.4 | async-start | bytes 8388608
  65.1 21.9 %slice-start.5 = ((s8[13631488]{0:T(1024)(128)(4,1)}), s8[4194304]{0:T(1024)(128)(4,1)S(1)}, s32[]{:S(2)}) async-start(s8[13631488]{0:T(1024)(128)(4,1)} %bitcast.57), calls=%async_computation.5 | async-start | bytes 8388608
  76.2 10.8 %slice-start.6 = ((s8[13631488]{0:T(1024)(128)(4,1)}), s8[4194304]{0:T(1024)(128)(4,1)S(1)}, s32[]{:S(2)}) async-start(s8[13631488]{0:T(1024)(128)(4,1)} %bitcast.57), calls=%async_computation.6 | async-start | bytes 8388608
  76.2 10.8 %slice-start.7 = ((s8[13631488]{0:T(1024)(128)(4,1)}), s8[1048576]{0:T(1024)(128)(4,1)S(1)}, s32[]{:S(2)}) async-start(s8[13631488]{0:T(1024)(128)(4,1)} %bitcast.57), calls=%async_computation.7 | async-start | bytes 2097152
  184.6 1.2 copy-start.2
  190.6 75.6 %collective-permute-start.3 = (f32[2,512,416]{1,2,0:T(8,128)}, f32[2,512,416]{1,2,0:T(8,128)}, u32[]{:S(2)}, u32[]{:S(2)}) collective-permute-start(f32[2,512,416]{1,2,0:T(8,128)} %copy.16), channel_id=1, source_target_pairs={{0,8},{1,9},{2,10},{3,11},{4,12},{5,13},{6,14},{7,15},{8,0},{9,1},... | collective-permute-start | bytes 5111816 | tf_op jit(solution)/shard_map/ppermute | solution.py:16
  269.1 3.0 copy-start.4
  271.7 42.7 %slice-start = ((s8[13631488]{0:T(1024)(128)(4,1)}), s8[1048576]{0:T(1024)(128)(4,1)S(1)}, s32[]{:S(2)}) async-start(s8[13631488]{0:T(1024)(128)(4,1)} %bitcast.55), calls=%async_computation | async-start | bytes 2097152
  272.0 25.4 %collective-permute-start.4 = (bf16[512,416]{1,0:T(8,128)(2,1)S(1)}, bf16[512,416]{1,0:T(8,128)(2,1)S(1)}, u32[]{:S(2)}, u32[]{:S(2)}) collective-permute-start(bf16[512,416]{1,0:T(8,128)(2,1)S(1)} %fusion.18), channel_id=1, source_target_pairs={{0,8},{1,9},{2,10},{3,11},{4,12},{5,13},{6,14},{7,15},{8,0},{9,1},... | collective-permute-start | bytes 1277960 | tf_op jit(solution)/shard_map/ppermute | solution.py:16
  301.7 12.6 %slice-start.1 = ((s8[13631488]{0:T(1024)(128)(4,1)}), s8[4194304]{0:T(1024)(128)(4,1)S(1)}, s32[]{:S(2)}) async-start(s8[13631488]{0:T(1024)(128)(4,1)} %bitcast.55), calls=%async_computation.1 | async-start | bytes 8388608
  301.7 12.6 %slice-start.2 = ((s8[13631488]{0:T(1024)(128)(4,1)}), s8[4194304]{0:T(1024)(128)(4,1)S(1)}, s32[]{:S(2)}) async-start(s8[13631488]{0:T(1024)(128)(4,1)} %bitcast.55), calls=%async_computation.2 | async-start | bytes 8388608
  301.7 12.6 %slice-start.3 = ((s8[13631488]{0:T(1024)(128)(4,1)}), s8[4194304]{0:T(1024)(128)(4,1)S(1)}, s32[]{:S(2)}) async-start(s8[13631488]{0:T(1024)(128)(4,1)} %bitcast.55), calls=%async_computation.3 | async-start | bytes 8388608
  379.8 181.6 %collective-permute-start.5 = (f32[512,4096]{1,0:T(8,128)}, f32[512,4096]{1,0:T(8,128)S(1)}, u32[]{:S(2)}, u32[]{:S(2)}) collective-permute-start(f32[512,4096]{1,0:T(8,128)} %slice_select_fusion), channel_id=1, source_target_pairs={{0,4},{1,5},{2,6},{3,7},{4,0},{5,1},{6,2},{7,3},{8,12},{9,13},{10,... | collective-permute-start | bytes 25165832 | tf_op jit(solution)/shard_map/ppermute | solution.py:11
  569.4 90.6 %collective-permute-start.6 = (f32[512,2048]{1,0:T(8,128)S(1)}, f32[512,2048]{1,0:T(8,128)S(1)}, u32[]{:S(2)}, u32[]{:S(2)}) collective-permute-start(f32[512,2048]{1,0:T(8,128)S(1)} %slice_select_fusion.1), channel_id=1, source_target_pairs={{0,2},{1,3},{2,0},{3,1},{4,6},{5,7},{6,4},{7,5},{8,10},{9,11},{10,... | collective-permute-start | bytes 12582920 | tf_op jit(solution)/shard_map/ppermute | solution.py:11
  661.8 6.2 copy-start.1
  662.2 4.2 collective-permute-start.7
where the time goes:
time: 677 us; the launch traced here: 668 us
  waiting for transfers between devices  436 us (64%)
  other arithmetic  92.1 us (14%)
  matrix products  77.7 us (11%)
  local copies, waits for them, and re-layouts  54.2 us (8%)
  starting transfers between devices  7.93 us (1%)
    ppermute x6, waiting for transfers between devices, partner(): lax.ppermute(shard, axis, [(i, i ^ 1 << stride) for i in range(lax.axis_s...  342 us
    ppermute x2, waiting for transfers between devices, from_behind(): lax.ppermute(shard, axis, [(i, (i + by) % devices) for i in range(devices)])  93.6 us
    dot_general x1, matrix products, body(): result = jnp.dot(hidden_full, down_eff, preferred_element_type=jnp.float32)  54.3 us
    convert_element_type x1, other arithmetic, scale_by_columns(): return scaled.reshape(height, width).astype(jnp.bfloat16)  50.1 us
    dot_general x1, matrix products, body(): jnp.dot(gathered, joined, preferred_element_type=jnp.float32)  21.9 us
    mul x2, local copies, waits for them, and re-layouts, scale_by_columns(): stored.astype(jnp.float32).reshape(height // BLK, BLK, width)  21.9 us
  transfers between devices with their start and end apart: 8, of which 8 were waited for; matrix products, arithmetic and copies ran while one was open for 12% of the time, Pallas kernels for 0%

commit v1 on v0

v1 whole, which is shorter than its diff:
```python
import jax
import jax.numpy as jnp
from jax import lax
from jax.sharding import PartitionSpec as P

BLK = 128
RO = 8
CHUNKS = 2


def partner(shard, mask):
    return lax.ppermute(shard, "gx", [(i, i ^ mask) for i in range(lax.axis_size("gx"))])


def from_behind(shard, by):
    devices = lax.axis_size("gx")
    return lax.ppermute(shard, "gx", [(i, (i + by) % devices) for i in range(devices)])


def scale_by_columns(stored, blocks, row_start, col_start):
    height, width = stored.shape
    row_scales = lax.dynamic_slice_in_dim(blocks, row_start // BLK, height // BLK, 0)
    owner = (col_start + jnp.arange(width, dtype=jnp.int32)) // BLK
    select = (jnp.arange(blocks.shape[1], dtype=jnp.int32)[:, None] == owner[None, :]).astype(
        jnp.float32
    )
    factors = jnp.dot(row_scales, select, precision=lax.Precision.HIGHEST)
    scaled = stored.astype(jnp.float32).reshape(height // BLK, BLK, width) * factors[:, None, :]
    return scaled.reshape(height, width).astype(jnp.bfloat16)


def scale_by_rows(stored, blocks, row_start, col_start):
    height, width = stored.shape
    col_scales = lax.dynamic_slice_in_dim(blocks, col_start // BLK, width // BLK, 1)
    owner = (row_start + jnp.arange(height, dtype=jnp.int32)) // BLK
    select = (owner[:, None] == jnp.arange(blocks.shape[0], dtype=jnp.int32)[None, :]).astype(
        jnp.float32
    )
    factors = jnp.dot(select, col_scales, precision=lax.Precision.HIGHEST)
    scaled = stored.astype(jnp.float32).reshape(height, width // BLK, BLK) * factors[:, :, None]
    return scaled.reshape(height, width).astype(jnp.bfloat16)


def gather_features(own, col_slot):
    width = own.shape[1]
    half = width // 2
    far = partner(own, 4)
    near = partner(own, 2)
    diagonal_a = partner(far[:, :half], 2)
    diagonal_b = partner(near[:, half:], 4)
    same = [
        (0, 0, own),
        (4, 0, far),
        (2, 0, near),
        (6, 0, diagonal_a),
        (6, half, diagonal_b),
    ]
    gathered = jnp.zeros((own.shape[0], width * RO), own.dtype)
    for mask, offset, block in same:
        gathered = lax.dynamic_update_slice_in_dim(
            gathered, block, (col_slot ^ mask) * width + offset, 1
        )
        gathered = lax.dynamic_update_slice_in_dim(
            gathered, partner(block, 1), (col_slot ^ mask ^ 1) * width + offset, 1
        )
    return gathered


def scatter_sum(result, col_slot):
    width = result.shape[1] // RO
    half = width // 2

    def piece(mask, offset, size):
        return lax.dynamic_slice_in_dim(result, (col_slot ^ mask) * width + offset, size, 1)

    def summed(mask, offset, size):
        sent = piece(mask ^ 1, offset, size).astype(jnp.bfloat16)
        return piece(mask, offset, size) + partner(sent, 1).astype(jnp.float32)

    def send(value, mask):
        return partner(value.astype(jnp.bfloat16), mask).astype(jnp.float32)

    diagonal_a = send(summed(6, 0, half), 2)
    diagonal_b = send(summed(6, half, half), 4)
    far_a = send(summed(4, 0, half) + diagonal_a, 4)
    far_b = send(summed(4, half, half), 4)
    near_a = send(summed(2, 0, half), 2)
    near_b = send(summed(2, half, half) + diagonal_b, 2)
    own_a = summed(0, 0, half) + far_a + near_a
    own_b = summed(0, half, half) + far_b + near_b
    return jnp.concatenate((own_a, own_b), 1).astype(jnp.bfloat16)


def body(tokens, token_scale, gate_tiles, up_tiles, gate_scale, up_scale, down_tiles, down_scale):
    position = lax.axis_index("gx")
    devices = lax.axis_size("gx")
    row_groups = devices // RO
    col_slot = position % RO
    row_slot = position // RO
    token_count, slice_width = tokens.shape
    tile_rows = gate_tiles.shape[1]
    tile_cols = gate_tiles.shape[2]
    piece_cols = tile_cols // row_groups
    tokens_eff = (
        tokens.astype(jnp.float32).reshape(token_count, slice_width // BLK, BLK)
        * token_scale[:, :, None]
    )
    tokens_eff = tokens_eff.reshape(token_count, slice_width).astype(jnp.bfloat16)
    gate_eff = scale_by_columns(
        gate_tiles[0], gate_scale, row_slot * tile_rows, col_slot * tile_cols
    )
    up_eff = scale_by_columns(up_tiles[0], up_scale, row_slot * tile_rows, col_slot * tile_cols)
    joined = jnp.concatenate((gate_eff, up_eff), 1)
    down_eff = scale_by_rows(down_tiles[0], down_scale, col_slot * tile_cols, row_slot * tile_rows)
    rows = token_count // CHUNKS

    def finish(gathered):
        partial_value = jnp.dot(gathered, joined, preferred_element_type=jnp.float32)

        def share(target):
            start = target * piece_cols
            return jnp.stack(
                (
                    lax.dynamic_slice_in_dim(partial_value, start, piece_cols, 1),
                    lax.dynamic_slice_in_dim(partial_value, tile_cols + start, piece_cols, 1),
                ),
                0,
            )

        summed = share((row_slot - 1) % row_groups)
        for step in range(1, row_groups):
            summed = from_behind(summed.astype(jnp.bfloat16), RO).astype(jnp.float32)
            summed = summed + share((row_slot - 1 - step) % row_groups)
        hidden_piece = (jax.nn.silu(summed[0]) * summed[1]).astype(jnp.bfloat16)
        hidden_full = jnp.zeros((rows, tile_cols), jnp.bfloat16)
        hidden_full = lax.dynamic_update_slice_in_dim(
            hidden_full, hidden_piece, row_slot * piece_cols, 1
        )
        current_hidden = hidden_piece
        for step in range(1, row_groups):
            current_hidden = from_behind(current_hidden, RO)
            source = (row_slot - step) % row_groups
            hidden_full = lax.dynamic_update_slice_in_dim(
                hidden_full, current_hidden, source * piece_cols, 1
            )
        result = jnp.dot(hidden_full, down_eff, preferred_element_type=jnp.float32)
        return scatter_sum(result, col_slot)

    outs = []
    for chunk in range(CHUNKS):
        own = tokens_eff[chunk * rows : (chunk + 1) * rows]
        outs.append(finish(gather_features(own, col_slot)))
    return jnp.concatenate(outs, 0)


def solution(mesh):
    return jax.shard_map(
        body,
        mesh=mesh,
        in_specs=(
            P("groups", "gx"),
            P("groups", "gx"),
            P("gx", None, None),
            P("gx", None, None),
            P(),
            P(),
            P("gx", None, None),
            P(),
        ),
        out_specs=P("groups", "gx"),
        check_vma=False,
    )
```

time: 677 us -> 352 us (0.52)
  waiting for transfers between devices: 436 us -> 67 us
  local copies, waits for them, and re-layouts: 54.2 us -> 82.5 us
  starting transfers between devices: 7.93 us -> 29.8 us
  other arithmetic: 92.1 us -> 71.4 us
  matrix products: 77.7 us -> 96.5 us
    ppermute x8 -> x50, waiting for transfers between devices: 436 us -> 67 us  [the longest x46 34.6 us: partner(): lax.ppermute(shard, 'gx', [(i, i ^ mask) for i in range(lax.axis_size('gx...]
    ppermute x8 -> x50, starting transfers between devices: 7.93 us -> 29.8 us  [the longest x46 24.1 us: partner(): lax.ppermute(shard, 'gx', [(i, i ^ mask) for i in range(lax.axis_size('gx...]
    select_n x6 -> x0, other arithmetic: 21.2 us -> none  [the longest x3 12.7 us: body(): outgoing = jnp.where(upper, lower_half, upper_half)]
    dot_general x2 -> x4, matrix products: 76.2 us -> 95 us  [the longest x2 64.4 us: finish(): result = jnp.dot(hidden_full, down_eff, preferred_element_type=jnp.float32)]
    dynamic_update_slice x2 -> x23, local copies, waits for them, and re-layouts: 8.56 us -> 27.3 us  [the longest x10 11.2 us: gather_features(): lax.dynamic_update_slice_in_dim(gathered, partner(block, 1), (col_slot ^...]
    add x3 -> x2, other arithmetic: 11.2 us -> 1.39 us  [finish(): summed = summed + share((row_slot - 1 - step) % row_groups)]
    convert_element_type x2 -> x8, other arithmetic: 1.88 us -> 8.89 us  [the longest x6 8.57 us: send(): return partner(value.astype(jnp.bfloat16), mask).astype(jnp.float32)]
  transfers between devices with their start and end apart: 8 -> 50, of which waited for: 8 -> 13; matrix products, arithmetic and copies ran while one was open for 12% -> 68% of each run, Pallas kernels for 0% -> 0%
where the time goes in v1:
time: 352 us; the launch traced here: 348 us
  matrix products  96.5 us (27%)
  local copies, waits for them, and re-layouts  82.5 us (23%)
  other arithmetic  71.4 us (20%)
  waiting for transfers between devices  67 us (19%)
  starting transfers between devices  29.8 us (8%)
    dot_general x2, matrix products, finish(): result = jnp.dot(hidden_full, down_eff, preferred_element_type=jnp.float32)  64.4 us
    convert_element_type x1, other arithmetic, scale_by_columns(): return scaled.reshape(height, width).astype(jnp.bfloat16)  50.2 us
    ppermute x46, waiting for transfers between devices, partner(): lax.ppermute(shard, 'gx', [(i, i ^ mask) for i in range(lax.axis_size('gx...  34.6 us
    ppermute x4, waiting for transfers between devices, from_behind(): lax.ppermute(shard, 'gx', [(i, (i + by) % devices) for i in range(devices)])  32.4 us
    dot_general x2, matrix products, finish(): jnp.dot(gathered, joined, preferred_element_type=jnp.float32)  30.6 us
    ppermute x46, starting transfers between devices, partner(): lax.ppermute(shard, 'gx', [(i, i ^ mask) for i in range(lax.axis_size('gx...  24.1 us
    mul x2, local copies, waits for them, and re-layouts, scale_by_columns(): stored.astype(jnp.float32).reshape(height // BLK, BLK, width)  21.9 us
    dynamic_update_slice x10, local copies, waits for them, and re-layouts, gather_features(): lax.dynamic_update_slice_in_dim(gathered, partner(block, 1), (col_slot ^...  11.2 us
  transfers between devices with their start and end apart: 50, of which 13 were waited for; matrix products, arithmetic and copies ran while one was open for 68% of the time, Pallas kernels for 0%

profile of v1, /device:TPU:0, one launch (start us, length us, event | category | flops | bytes accessed | tf_op | source)
XLA Modules:
  0.0 348.2 jit_solution(10801994312470629583)
XLA Ops:
  1.5 1.8 fusion.5
  3.3 2.5 broadcast.90.clone.1
  5.8 1.3 fusion.35
  7.5 2.6 collective-permute-start.1
  10.1 1.5 collective-permute-start.3
  13.2 11.1 %mul.84 = f32[64,128,832]{1,0,2:T(8,128)} broadcast(f32[64,832]{0,1:T(8,128)S(1)} %fusion.17), dimensions={0,2} | broadcast | bytes 27475968 | tf_op jit(solution)/shard_map/mul | solution.py:28
  24.3 10.8 %mul.171 = f32[64,128,832]{1,0,2:T(8,128)} broadcast(f32[64,832]{0,1:T(8,128)S(1)} %fusion.16), dimensions={0,2} | broadcast | bytes 27475968 | tf_op jit(solution)/shard_map/mul | solution.py:28
  35.1 50.2 %fusion.1 = (bf16[8192,832]{0,1:T(8,128)(2,1)}, bf16[8192,832]{0,1:T(8,128)(2,1)}) fusion(f32[104,8,64,128]{3,2,1,0:T(8,128)} %bitcast.80, bf16[1,8192,832]{1,2,0:T(8,128)(2,1)S(1)} %bitcast.82, f32[104,8,64,128]{3,2,1,0:T(8,128)} %bitcast.79, bf16[1,8192,832]{1,2,0:T(8,128)(2,1)} %param.10), kind=kLoop, calls=%fused_computation.3 | loop fusion | flops 40894464 | bytes 109051904 | tf_op jit(solution)/shard_map/convert_element_type | solution.py:29
  85.8 2.0 copy-done.2
  89.5 1.9 constant_dynamic-update-slice_fusion.18
  91.4 1.0 collective-permute-start.5
  93.5 1.9 constant_dynamic-update-slice_fusion.8
  95.4 1.7 collective-permute-start.7
  97.1 1.9 constant_dynamic-update-slice_fusion.7
  99.9 3.0 collective-permute-done.28
  104.1 4.3 %collective-permute-done.5 = bf16[256,512]{1,0:T(8,128)(2,1)S(1)} collective-permute-done((bf16[256,512]{1,0:T(8,128)(2,1)S(1)}, bf16[256,512]{1,0:T(8,128)(2,1)S(1)}, u32[]{:S(2)}, u32[]{:S(2)}) %collective-permute-start.5) | collective-permute-done | bytes 262176 | tf_op jit(solution)/shard_map/ppermute | solution.py:12
  108.4 1.6 collective-permute-start.32
  114.3 1.0 collective-permute-done.32
  118.2 15.6 %fusion.4 = f32[256,1664]{1,0:T(8,128)} fusion(bf16[256,8192]{1,0:T(8,128)(2,1)} %constant_dynamic-update-slice_fusion.10, bf16[8192,832]{0,1:T(8,128)(2,1)} %get-tuple-element.42, bf16[8192,832]{0,1:T(8,128)(2,1)} %get-tuple-element.43), kind=kOutput, calls=%fused_computation.8 | convolution fusion | flops 7033847808 | bytes 33161216 | tf_op jit(solution)/shard_map/dot_general | solution.py:118
  133.8 1.5 fusion.11
  136.1 2.6 collective-permute-start.9
  138.7 1.1 constant_dynamic-update-slice_fusion.6
  139.8 1.1 constant_dynamic-update-slice_fusion.5
  140.9 1.1 constant_dynamic-update-slice_fusion.4
  142.0 1.0 constant_dynamic-update-slice_fusion.3
  143.0 1.0 constant_dynamic-update-slice_fusion.2
  145.0 15.0 %fusion.3 = f32[256,1664]{1,0:T(8,128)} fusion(bf16[256,8192]{1,0:T(8,128)(2,1)S(1)} %constant_dynamic-update-slice_fusion, bf16[8192,832]{0,1:T(8,128)(2,1)} %get-tuple-element.42, bf16[8192,832]{0,1:T(8,128)(2,1)} %get-tuple-element.43), kind=kOutput, calls=%fused_computation.7 | convolution fusion | flops 7033847808 | bytes 33161216 | tf_op jit(solution)/shard_map/dot_general | solution.py:118
  160.0 1.6 fusion.13
  162.1 1.6 dynamic-slice_bitcast_fusion.3
  164.1 1.2 maximum_add_fusion
  165.5 2.6 collective-permute-start.10
  168.1 26.0 %collective-permute-done.34 = bf16[2,256,416]{2,1,0:T(8,128)(2,1)S(1)} collective-permute-done((bf16[2,256,416]{2,1,0:T(8,128)(2,1)S(1)}, bf16[2,256,416]{2,1,0:T(8,128)(2,1)S(1)}, u32[]{:S(2)}, u32[]{:S(2)}) %collective-permute-start.34) | collective-permute-done | bytes 426016 | tf_op jit(solution)/shard_map/ppermute | solution.py:17
  194.5 2.2 dynamic_update_slice.82
  196.7 2.2 dynamic_update_slice.94
  198.9 6.4 %collective-permute-done.10 = bf16[256,416]{1,0:T(8,128)(2,1)S(1)} collective-permute-done((bf16[256,416]{1,0:T(8,128)(2,1)S(1)}, bf16[256,416]{1,0:T(8,128)(2,1)S(1)}, u32[]{:S(2)}, u32[]{:S(2)}) %collective-permute-start.10) | collective-permute-done | bytes 213024 | tf_op jit(solution)/shard_map/ppermute | solution.py:17
  205.3 2.1 dynamic_update_slice.83
  207.4 10.8 %mul.179 = f32[832,64,128]{2,1,0:T(8,128)} broadcast(f32[832,64]{1,0:T(8,128)S(1)} %fusion.10), dimensions={0,1} | broadcast | bytes 27475968 | tf_op jit(solution)/shard_map/mul | solution.py:40
  218.2 32.1 %fusion.33 = f32[256,8192]{1,0:T(8,128)} fusion(bf16[256,832]{1,0:T(8,128)(2,1)S(1)} %dynamic_update_slice.83, f32[104,8,64,128]{3,2,1,0:T(8,128)} %bitcast.77, bf16[1,832,8192]{2,1,0:T(8,128)(2,1)} %param.14), kind=kOutput, calls=%fused_computation.114 | convolution fusion | flops 3510108160 | bytes 49709056 | tf_op jit(solution)/shard_map/dot_general | solution.py:146
  250.3 3.3 dynamic-slice_convert_fusion.17
  253.6 2.4 dynamic_update_slice.95
  256.1 32.3 %fusion.31 = f32[256,8192]{1,0:T(8,128)} fusion(bf16[256,832]{1,0:T(8,128)(2,1)S(1)} %dynamic_update_slice.95, f32[104,8,64,128]{3,2,1,0:T(8,128)} %bitcast.78, bf16[1,832,8192]{2,1,0:T(8,128)(2,1)} %param.14), kind=kOutput, calls=%fused_computation.113 | convolution fusion | flops 3510108160 | bytes 49709056 | tf_op jit(solution)/shard_map/dot_general | solution.py:146
  288.4 2.5 dynamic-slice_convert_fusion.7
  291.9 1.2 add_convert_fusion.15
  294.3 1.1 add_convert_fusion.7
  295.4 1.5 collective-permute-start.39
  296.9 5.4 %collective-permute-done.14 = bf16[256,512]{1,0:T(8,128)(2,1)S(1)} collective-permute-done((bf16[256,512]{1,0:T(8,128)(2,1)S(1)}, bf16[256,512]{1,0:T(8,128)(2,1)S(1)}, u32[]{:S(2)}, u32[]{:S(2)}) %collective-permute-start.14) | collective-permute-done | bytes 262176 | tf_op jit(solution)/shard_map/ppermute | solution.py:12
  302.3 2.3 add_convert_fusion.14
  306.0 1.2 collective-permute-done.39
  307.8 1.6 add_convert_fusion.6
  310.1 4.9 %collective-permute-done.15 = bf16[256,512]{1,0:T(8,128)(2,1)} collective-permute-done((bf16[256,512]{1,0:T(8,128)(2,1)}, bf16[256,512]{1,0:T(8,128)(2,1)}, u32[]{:S(2)}, u32[]{:S(2)}) %collective-permute-start.15) | collective-permute-done | bytes 262176 | tf_op jit(solution)/shard_map/ppermute | solution.py:12
  316.0 2.1 add_convert_fusion.12
  318.7 1.7 collective-permute-start.23
  320.4 3.9 %collective-permute-done.40 = bf16[256,512]{1,0:T(8,128)(2,1)S(1)} collective-permute-done((bf16[256,512]{1,0:T(8,128)(2,1)S(1)}, bf16[256,512]{1,0:T(8,128)(2,1)S(1)}, u32[]{:S(2)}, u32[]{:S(2)}) %collective-permute-start.40) | collective-permute-done | bytes 262176 | tf_op jit(solution)/shard_map/ppermute | solution.py:12
  324.3 2.4 add_convert_fusion.4
  327.1 1.6 collective-permute-start.20
  328.7 1.3 collective-permute-done.23
  330.0 1.2 add_convert_fusion.9
  331.6 4.5 %collective-permute-done.48 = bf16[256,512]{1,0:T(8,128)(2,1)S(1)} collective-permute-done((bf16[256,512]{1,0:T(8,128)(2,1)}, bf16[256,512]{1,0:T(8,128)(2,1)S(1)}, u32[]{:S(2)}, u32[]{:S(2)}) %collective-permute-start.48) | collective-permute-done | bytes 262176 | tf_op jit(solution)/shard_map/ppermute | solution.py:12
  336.6 1.2 add_convert_fusion.1
  339.1 2.7 collective-permute-done.20
  341.8 1.4 add_convert_fusion.8
  343.2 2.4 collective-permute-done.45
  345.6 1.3 add_convert_fusion
  346.9 1.1 maximum_maximum_fusion
  (141 shorter events, 28.5 us)
Async XLA Ops:
  0.0 12.0 %copy-start = (f32[128,52]{0,1:T(8,128)S(1)}, f32[128,52]{0,1:T(8,128)}, u32[]{:S(2)}) copy-start(f32[128,52]{0,1:T(8,128)} %param.12) | copy-start | bytes 79876
  3.3 9.3 %copy-start.11 = (f32[128,52]{0,1:T(8,128)S(1)}, f32[128,52]{0,1:T(8,128)}, u32[]{:S(2)}) copy-start(f32[128,52]{0,1:T(8,128)} %param.13) | copy-start | bytes 79876
  7.0 80.8 %collective-permute-start = (bf16[256,1024]{1,0:T(8,128)(2,1)}, bf16[256,1024]{1,0:T(8,128)(2,1)S(1)}, u32[]{:S(2)}, u32[]{:S(2)}) collective-permute-start(bf16[256,1024]{1,0:T(8,128)(2,1)} %get-tuple-element.39), channel_id=1, source_target_pairs={{0,1},{1,0},{2,3},{3,2},{4,5},{5,4},{6,7},{7,6},{8,9},{9,8},{10,11... | collective-permute-start | bytes 1572872 | tf_op jit(solution)/shard_map/ppermute | solution.py:12
  7.5 80.6 %collective-permute-start.1 = (bf16[256,1024]{1,0:T(8,128)(2,1)}, bf16[256,1024]{1,0:T(8,128)(2,1)S(1)}, u32[]{:S(2)}, u32[]{:S(2)}) collective-permute-start(bf16[256,1024]{1,0:T(8,128)(2,1)} %get-tuple-element.39), channel_id=1, source_target_pairs={{0,4},{1,5},{2,6},{3,7},{4,0},{5,1},{6,2},{7,3},{8,12},{9,13},{10,... | collective-permute-start | bytes 1572872 | tf_op jit(solution)/shard_map/ppermute | solution.py:12
  10.1 81.3 %collective-permute-start.3 = (bf16[256,1024]{1,0:T(8,128)(2,1)}, bf16[256,1024]{1,0:T(8,128)(2,1)S(1)}, u32[]{:S(2)}, u32[]{:S(2)}) collective-permute-start(bf16[256,1024]{1,0:T(8,128)(2,1)} %get-tuple-element.39), channel_id=1, source_target_pairs={{0,2},{1,3},{2,0},{3,1},{4,6},{5,7},{6,4},{7,5},{8,10},{9,11},{10,... | collective-permute-start | bytes 1572872 | tf_op jit(solution)/shard_map/ppermute | solution.py:12
  11.6 80.8 %collective-permute-start.25 = (bf16[256,1024]{1,0:T(8,128)(2,1)}, bf16[256,1024]{1,0:T(8,128)(2,1)}, u32[]{:S(2)}, u32[]{:S(2)}) collective-permute-start(bf16[256,1024]{1,0:T(8,128)(2,1)} %get-tuple-element.41), channel_id=1, source_target_pairs={{0,1},{1,0},{2,3},{3,2},{4,5},{5,4},{6,7},{7,6},{8,9},{9,8},{10,11... | collective-permute-start | bytes 1572872 | tf_op jit(solution)/shard_map/ppermute | solution.py:12
  11.6 83.8 %collective-permute-start.26 = (bf16[256,1024]{1,0:T(8,128)(2,1)}, bf16[256,1024]{1,0:T(8,128)(2,1)}, u32[]{:S(2)}, u32[]{:S(2)}) collective-permute-start(bf16[256,1024]{1,0:T(8,128)(2,1)} %get-tuple-element.41), channel_id=1, source_target_pairs={{0,4},{1,5},{2,6},{3,7},{4,0},{5,1},{6,2},{7,3},{8,12},{9,13},{10,... | collective-permute-start | bytes 1572872 | tf_op jit(solution)/shard_map/ppermute | solution.py:12
  13.2 21.9 %slice-start = ((s8[13631488]{0:T(1024)(128)(4,1)}), s8[4194304]{0:T(1024)(128)(4,1)S(1)}, s32[]{:S(2)}) async-start(s8[13631488]{0:T(1024)(128)(4,1)} %bitcast.81), calls=%async_computation | async-start | bytes 8388608
  13.2 21.9 %slice-start.1 = ((s8[13631488]{0:T(1024)(128)(4,1)}), s8[4194304]{0:T(1024)(128)(4,1)S(1)}, s32[]{:S(2)}) async-start(s8[13631488]{0:T(1024)(128)(4,1)} %bitcast.81), calls=%async_computation.1 | async-start | bytes 8388608
  24.3 10.8 %slice-start.2 = ((s8[13631488]{0:T(1024)(128)(4,1)}), s8[4194304]{0:T(1024)(128)(4,1)S(1)}, s32[]{:S(2)}) async-start(s8[13631488]{0:T(1024)(128)(4,1)} %bitcast.81), calls=%async_computation.2 | async-start | bytes 8388608
  24.3 10.8 %slice-start.3 = ((s8[13631488]{0:T(1024)(128)(4,1)}), s8[1048576]{0:T(1024)(128)(4,1)S(1)}, s32[]{:S(2)}) async-start(s8[13631488]{0:T(1024)(128)(4,1)} %bitcast.81), calls=%async_computation.3 | async-start | bytes 2097152
  85.3 3.6 %copy-start.12 = (f32[52,128]{1,0:T(8,128)S(1)}, f32[52,128]{1,0:T(8,128)}, u32[]{:S(2)}) copy-start(f32[52,128]{1,0:T(8,128)} %param.15) | copy-start | bytes 79876
  85.8 2.0 copy-start.2
  87.8 0.8 copy-start.5
  87.8 15.1 %collective-permute-start.28 = (bf16[256,1024]{1,0:T(8,128)(2,1)}, bf16[256,1024]{1,0:T(8,128)(2,1)}, u32[]{:S(2)}, u32[]{:S(2)}) collective-permute-start(bf16[256,1024]{1,0:T(8,128)(2,1)} %get-tuple-element.41), channel_id=1, source_target_pairs={{0,2},{1,3},{2,0},{3,1},{4,6},{5,7},{6,4},{7,5},{8,10},{9,11},{10,... | collective-permute-start | bytes 1572872 | tf_op jit(solution)/shard_map/ppermute | solution.py:12
  88.6 21.3 %collective-permute-start.2 = (bf16[256,1024]{1,0:T(8,128)(2,1)S(1)}, bf16[256,1024]{1,0:T(8,128)(2,1)S(1)}, u32[]{:S(2)}, u32[]{:S(2)}) collective-permute-start(bf16[256,1024]{1,0:T(8,128)(2,1)S(1)} %collective-permute-done.1), channel_id=1, source_target_pairs={{0,1},{1,0},{2,3},{3,2},{4,5},{5,4},{6,7},{7,6},{8,9},{9,8},{10,11... | collective-permute-start | bytes 1572872 | tf_op jit(solution)/shard_map/ppermute | solution.py:12
  91.4 17.0 %collective-permute-start.5 = (bf16[256,512]{1,0:T(8,128)(2,1)S(1)}, bf16[256,512]{1,0:T(8,128)(2,1)S(1)}, u32[]{:S(2)}, u32[]{:S(2)}) collective-permute-start(bf16[256,512]{1,0:T(8,128)(2,1)S(1)} %slice.41), channel_id=1, source_target_pairs={{0,2},{1,3},{2,0},{3,1},{4,6},{5,7},{6,4},{7,5},{8,10},{9,11},{10,... | collective-permute-start | bytes 786440 | tf_op jit(solution)/shard_map/ppermute | solution.py:12
  92.4 19.8 %collective-permute-start.4 = (bf16[256,1024]{1,0:T(8,128)(2,1)S(1)}, bf16[256,1024]{1,0:T(8,128)(2,1)S(1)}, u32[]{:S(2)}, u32[]{:S(2)}) collective-permute-start(bf16[256,1024]{1,0:T(8,128)(2,1)S(1)} %collective-permute-done.3), channel_id=1, source_target_pairs={{0,1},{1,0},{2,3},{3,2},{4,5},{5,4},{6,7},{7,6},{8,9},{9,8},{10,11... | collective-permute-start | bytes 1572872 | tf_op jit(solution)/shard_map/ppermute | solution.py:12
  95.4 16.3 %collective-permute-start.7 = (bf16[256,512]{1,0:T(8,128)(2,1)S(1)}, bf16[256,512]{1,0:T(8,128)(2,1)S(1)}, u32[]{:S(2)}, u32[]{:S(2)}) collective-permute-start(bf16[256,512]{1,0:T(8,128)(2,1)S(1)} %slice.42), channel_id=1, source_target_pairs={{0,4},{1,5},{2,6},{3,7},{4,0},{5,1},{6,2},{7,3},{8,12},{9,13},{10,... | collective-permute-start | bytes 786440 | tf_op jit(solution)/shard_map/ppermute | solution.py:12
  102.9 11.0 %collective-permute-start.30 = (bf16[256,512]{1,0:T(8,128)(2,1)S(1)}, bf16[256,512]{1,0:T(8,128)(2,1)}, u32[]{:S(2)}, u32[]{:S(2)}) collective-permute-start(bf16[256,512]{1,0:T(8,128)(2,1)S(1)} %slice.46), channel_id=1, source_target_pairs={{0,2},{1,3},{2,0},{3,1},{4,6},{5,7},{6,4},{7,5},{8,10},{9,11},{10,... | collective-permute-start | bytes 786440 | tf_op jit(solution)/shard_map/ppermute | solution.py:12
  108.4 6.9 %collective-permute-start.32 = (bf16[256,512]{1,0:T(8,128)(2,1)S(1)}, bf16[256,512]{1,0:T(8,128)(2,1)S(1)}, u32[]{:S(2)}, u32[]{:S(2)}) collective-permute-start(bf16[256,512]{1,0:T(8,128)(2,1)S(1)} %slice.47), channel_id=1, source_target_pairs={{0,4},{1,5},{2,6},{3,7},{4,0},{5,1},{6,2},{7,3},{8,12},{9,13},{10,... | collective-permute-start | bytes 786440 | tf_op jit(solution)/shard_map/ppermute | solution.py:12
  110.0 5.3 %collective-permute-start.6 = (bf16[256,512]{1,0:T(8,128)(2,1)S(1)}, bf16[256,512]{1,0:T(8,128)(2,1)S(1)}, u32[]{:S(2)}, u32[]{:S(2)}) collective-permute-start(bf16[256,512]{1,0:T(8,128)(2,1)S(1)} %collective-permute-done.5), channel_id=1, source_target_pairs={{0,1},{1,0},{2,3},{3,2},{4,5},{5,4},{6,7},{7,6},{8,9},{9,8},{10,11... | collective-permute-start | bytes 786440 | tf_op jit(solution)/shard_map/ppermute | solution.py:12
  111.7 27.0 %collective-permute-start.27 = (bf16[256,1024]{1,0:T(8,128)(2,1)}, bf16[256,1024]{1,0:T(8,128)(2,1)}, u32[]{:S(2)}, u32[]{:S(2)}) collective-permute-start(bf16[256,1024]{1,0:T(8,128)(2,1)} %collective-permute-done.26), channel_id=1, source_target_pairs={{0,1},{1,0},{2,3},{3,2},{4,5},{5,4},{6,7},{7,6},{8,9},{9,8},{10,11... | collective-permute-start | bytes 1572872 | tf_op jit(solution)/shard_map/ppermute | solution.py:12
  112.2 5.2 %collective-permute-start.8 = (bf16[256,512]{1,0:T(8,128)(2,1)S(1)}, bf16[256,512]{1,0:T(8,128)(2,1)S(1)}, u32[]{:S(2)}, u32[]{:S(2)}) collective-permute-start(bf16[256,512]{1,0:T(8,128)(2,1)S(1)} %collective-permute-done.7), channel_id=1, source_target_pairs={{0,1},{1,0},{2,3},{3,2},{4,5},{5,4},{6,7},{7,6},{8,9},{9,8},{10,11... | collective-permute-start | bytes 786440 | tf_op jit(solution)/shard_map/ppermute | solution.py:12
  113.9 27.0 %collective-permute-start.29 = (bf16[256,1024]{1,0:T(8,128)(2,1)}, bf16[256,1024]{1,0:T(8,128)(2,1)}, u32[]{:S(2)}, u32[]{:S(2)}) collective-permute-start(bf16[256,1024]{1,0:T(8,128)(2,1)} %collective-permute-done.28), channel_id=1, source_target_pairs={{0,1},{1,0},{2,3},{3,2},{4,5},{5,4},{6,7},{7,6},{8,9},{9,8},{10,11... | collective-permute-start | bytes 1572872 | tf_op jit(solution)/shard_map/ppermute | solution.py:12
  115.3 27.7 %collective-permute-start.31 = (bf16[256,512]{1,0:T(8,128)(2,1)}, bf16[256,512]{1,0:T(8,128)(2,1)}, u32[]{:S(2)}, u32[]{:S(2)}) collective-permute-start(bf16[256,512]{1,0:T(8,128)(2,1)} %collective-permute-done.30), channel_id=1, source_target_pairs={{0,1},{1,0},{2,3},{3,2},{4,5},{5,4},{6,7},{7,6},{8,9},{9,8},{10,11... | collective-permute-start | bytes 786440 | tf_op jit(solution)/shard_map/ppermute | solution.py:12
  115.3 28.7 %collective-permute-start.33 = (bf16[256,512]{1,0:T(8,128)(2,1)S(1)}, bf16[256,512]{1,0:T(8,128)(2,1)}, u32[]{:S(2)}, u32[]{:S(2)}) collective-permute-start(bf16[256,512]{1,0:T(8,128)(2,1)S(1)} %collective-permute-done.32), channel_id=1, source_target_pairs={{0,1},{1,0},{2,3},{3,2},{4,5},{5,4},{6,7},{7,6},{8,9},{9,8},{10,11... | collective-permute-start | bytes 786440 | tf_op jit(solution)/shard_map/ppermute | solution.py:12
  118.2 20.6 %copy-start.3 = (bf16[256,8192]{1,0:T(8,128)(2,1)S(1)}, bf16[256,8192]{1,0:T(8,128)(2,1)}, u32[]{:S(2)}) copy-start(bf16[256,8192]{1,0:T(8,128)(2,1)} %constant_dynamic-update-slice_fusion.7) | copy-start | bytes 12582916
  136.1 28.0 %collective-permute-start.9 = (bf16[2,256,416]{2,1,0:T(8,128)(2,1)}, bf16[2,256,416]{2,1,0:T(8,128)(2,1)}, u32[]{:S(2)}, u32[]{:S(2)}) collective-permute-start(bf16[2,256,416]{2,1,0:T(8,128)(2,1)} %pad_maximum_fusion.3), channel_id=1, source_target_pairs={{0,8},{1,9},{2,10},{3,11},{4,12},{5,13},{6,14},{7,15},{8,0},{9,1},... | collective-permute-start | bytes 1277960 | tf_op jit(solution)/shard_map/ppermute | solution.py:17
  160.0 3.7 %copy-start.4 = (f32[256,1664]{1,0:T(8,128)S(1)}, f32[256,1664]{1,0:T(8,128)}, u32[]{:S(2)}) copy-start(f32[256,1664]{1,0:T(8,128)} %fusion.3) | copy-start | bytes 5111812
  161.7 32.4 %collective-permute-start.34 = (bf16[2,256,416]{2,1,0:T(8,128)(2,1)S(1)}, bf16[2,256,416]{2,1,0:T(8,128)(2,1)S(1)}, u32[]{:S(2)}, u32[]{:S(2)}) collective-permute-start(bf16[2,256,416]{2,1,0:T(8,128)(2,1)S(1)} %pad_maximum_fusion.4), channel_id=1, source_target_pairs={{0,8},{1,9},{2,10},{3,11},{4,12},{5,13},{6,14},{7,15},{8,0},{9,1},... | collective-permute-start | bytes 1277960 | tf_op jit(solution)/shard_map/ppermute | solution.py:17
  165.5 39.8 %collective-permute-start.10 = (bf16[256,416]{1,0:T(8,128)(2,1)S(1)}, bf16[256,416]{1,0:T(8,128)(2,1)S(1)}, u32[]{:S(2)}, u32[]{:S(2)}) collective-permute-start(bf16[256,416]{1,0:T(8,128)(2,1)S(1)} %fusion.9), channel_id=1, source_target_pairs={{0,8},{1,9},{2,10},{3,11},{4,12},{5,13},{6,14},{7,15},{8,0},{9,1},... | collective-permute-start | bytes 638984 | tf_op jit(solution)/shard_map/ppermute | solution.py:17
  194.4 59.2 %collective-permute-start.35 = (bf16[256,416]{1,0:T(8,128)(2,1)S(1)}, bf16[256,416]{1,0:T(8,128)(2,1)S(1)}, u32[]{:S(2)}, u32[]{:S(2)}) collective-permute-start(bf16[256,416]{1,0:T(8,128)(2,1)S(1)} %fusion.7), channel_id=1, source_target_pairs={{0,8},{1,9},{2,10},{3,11},{4,12},{5,13},{6,14},{7,15},{8,0},{9,1},... | collective-permute-start | bytes 638984 | tf_op jit(solution)/shard_map/ppermute | solution.py:17
  253.6 38.3 %collective-permute-start.13 = (bf16[256,512]{1,0:T(8,128)(2,1)}, bf16[256,512]{1,0:T(8,128)(2,1)}, u32[]{:S(2)}, u32[]{:S(2)}) collective-permute-start(bf16[256,512]{1,0:T(8,128)(2,1)} %get-tuple-element.14), channel_id=1, source_target_pairs={{0,1},{1,0},{2,3},{3,2},{4,5},{5,4},{6,7},{7,6},{8,9},{9,8},{10,11... | collective-permute-start | bytes 786440 | tf_op jit(solution)/shard_map/ppermute | solution.py:12
  288.3 3.0 copy-start.8
  290.8 3.0 collective-permute-start.38
  291.4 4.0 %collective-permute-start.12 = (bf16[256,512]{1,0:T(8,128)(2,1)S(1)}, bf16[256,512]{1,0:T(8,128)(2,1)S(1)}, u32[]{:S(2)}, u32[]{:S(2)}) collective-permute-start(bf16[256,512]{1,0:T(8,128)(2,1)S(1)} %copy-done.8), channel_id=1, source_target_pairs={{0,1},{1,0},{2,3},{3,2},{4,5},{5,4},{6,7},{7,6},{8,9},{9,8},{10,11... | collective-permute-start | bytes 786440 | tf_op jit(solution)/shard_map/ppermute | solution.py:12
  291.5 5.4 %collective-permute-start.16 = (bf16[256,512]{1,0:T(8,128)(2,1)S(1)}, bf16[256,512]{1,0:T(8,128)(2,1)S(1)}, u32[]{:S(2)}, u32[]{:S(2)}) collective-permute-start(bf16[256,512]{1,0:T(8,128)(2,1)S(1)} %get-tuple-element.13), channel_id=1, source_target_pairs={{0,1},{1,0},{2,3},{3,2},{4,5},{5,4},{6,7},{7,6},{8,9},{9,8},{10,11... | collective-permute-start | bytes 786440 | tf_op jit(solution)/shard_map/ppermute | solution.py:12
  293.1 9.2 %collective-permute-start.14 = (bf16[256,512]{1,0:T(8,128)(2,1)S(1)}, bf16[256,512]{1,0:T(8,128)(2,1)S(1)}, u32[]{:S(2)}, u32[]{:S(2)}) collective-permute-start(bf16[256,512]{1,0:T(8,128)(2,1)S(1)} %add_convert_fusion.15), channel_id=1, source_target_pairs={{0,2},{1,3},{2,0},{3,1},{4,6},{5,7},{6,4},{7,5},{8,10},{9,11},{10,... | collective-permute-start | bytes 786440 | tf_op jit(solution)/shard_map/ppermute | solution.py:12
  293.8 10.8 %collective-permute-start.37 = (bf16[256,512]{1,0:T(8,128)(2,1)S(1)}, bf16[256,512]{1,0:T(8,128)(2,1)S(1)}, u32[]{:S(2)}, u32[]{:S(2)}) collective-permute-start(bf16[256,512]{1,0:T(8,128)(2,1)S(1)} %get-tuple-element.28), channel_id=1, source_target_pairs={{0,1},{1,0},{2,3},{3,2},{4,5},{5,4},{6,7},{7,6},{8,9},{9,8},{10,11... | collective-permute-start | bytes 786440 | tf_op jit(solution)/shard_map/ppermute | solution.py:12
  293.8 11.4 %collective-permute-start.41 = (bf16[256,512]{1,0:T(8,128)(2,1)S(1)}, bf16[256,512]{1,0:T(8,128)(2,1)S(1)}, u32[]{:S(2)}, u32[]{:S(2)}) collective-permute-start(bf16[256,512]{1,0:T(8,128)(2,1)S(1)} %get-tuple-element.26), channel_id=1, source_target_pairs={{0,1},{1,0},{2,3},{3,2},{4,5},{5,4},{6,7},{7,6},{8,9},{9,8},{10,11... | collective-permute-start | bytes 786440 | tf_op jit(solution)/shard_map/ppermute | solution.py:12
  295.4 11.7 %collective-permute-start.39 = (bf16[256,512]{1,0:T(8,128)(2,1)S(1)}, bf16[256,512]{1,0:T(8,128)(2,1)}, u32[]{:S(2)}, u32[]{:S(2)}) collective-permute-start(bf16[256,512]{1,0:T(8,128)(2,1)S(1)} %add_convert_fusion.7), channel_id=1, source_target_pairs={{0,2},{1,3},{2,0},{3,1},{4,6},{5,7},{6,4},{7,5},{8,10},{9,11},{10,... | collective-permute-start | bytes 786440 | tf_op jit(solution)/shard_map/ppermute | solution.py:12
  296.9 12.5 %collective-permute-start.11 = (bf16[256,512]{1,0:T(8,128)(2,1)S(1)}, bf16[256,512]{1,0:T(8,128)(2,1)S(1)}, u32[]{:S(2)}, u32[]{:S(2)}) collective-permute-start(bf16[256,512]{1,0:T(8,128)(2,1)S(1)} %get-tuple-element.8), channel_id=1, source_target_pairs={{0,1},{1,0},{2,3},{3,2},{4,5},{5,4},{6,7},{7,6},{8,9},{9,8},{10,11... | collective-permute-start | bytes 786440 | tf_op jit(solution)/shard_map/ppermute | solution.py:12
  302.3 7.2 %collective-permute-start.19 = (bf16[256,512]{1,0:T(8,128)(2,1)S(1)}, bf16[256,512]{1,0:T(8,128)(2,1)S(1)}, u32[]{:S(2)}, u32[]{:S(2)}) collective-permute-start(bf16[256,512]{1,0:T(8,128)(2,1)S(1)} %get-tuple-element.11), channel_id=1, source_target_pairs={{0,1},{1,0},{2,3},{3,2},{4,5},{5,4},{6,7},{7,6},{8,9},{9,8},{10,11... | collective-permute-start | bytes 786440 | tf_op jit(solution)/shard_map/ppermute | solution.py:12
  304.6 5.4 %collective-permute-start.22 = (bf16[256,512]{1,0:T(8,128)(2,1)S(1)}, bf16[256,512]{1,0:T(8,128)(2,1)}, u32[]{:S(2)}, u32[]{:S(2)}) collective-permute-start(bf16[256,512]{1,0:T(8,128)(2,1)S(1)} %get-tuple-element.9), channel_id=1, source_target_pairs={{0,1},{1,0},{2,3},{3,2},{4,5},{5,4},{6,7},{7,6},{8,9},{9,8},{10,11... | collective-permute-start | bytes 786440 | tf_op jit(solution)/shard_map/ppermute | solution.py:12
  306.0 9.0 %collective-permute-start.15 = (bf16[256,512]{1,0:T(8,128)(2,1)}, bf16[256,512]{1,0:T(8,128)(2,1)}, u32[]{:S(2)}, u32[]{:S(2)}) collective-permute-start(bf16[256,512]{1,0:T(8,128)(2,1)} %get-tuple-element.16), channel_id=1, source_target_pairs={{0,4},{1,5},{2,6},{3,7},{4,0},{5,1},{6,2},{7,3},{8,12},{9,13},{10,... | collective-permute-start | bytes 786440 | tf_op jit(solution)/shard_map/ppermute | solution.py:12
  307.2 8.2 %collective-permute-start.17 = (bf16[256,512]{1,0:T(8,128)(2,1)}, bf16[256,512]{1,0:T(8,128)(2,1)}, u32[]{:S(2)}, u32[]{:S(2)}) collective-permute-start(bf16[256,512]{1,0:T(8,128)(2,1)} %get-tuple-element.17), channel_id=1, source_target_pairs={{0,2},{1,3},{2,0},{3,1},{4,6},{5,7},{6,4},{7,5},{8,10},{9,11},{10,... | collective-permute-start | bytes 786440 | tf_op jit(solution)/shard_map/ppermute | solution.py:12
  309.4 8.6 %collective-permute-start.36 = (bf16[256,512]{1,0:T(8,128)(2,1)S(1)}, bf16[256,512]{1,0:T(8,128)(2,1)S(1)}, u32[]{:S(2)}, u32[]{:S(2)}) collective-permute-start(bf16[256,512]{1,0:T(8,128)(2,1)S(1)} %get-tuple-element.21), channel_id=1, source_target_pairs={{0,1},{1,0},{2,3},{3,2},{4,5},{5,4},{6,7},{7,6},{8,9},{9,8},{10,11... | collective-permute-start | bytes 786440 | tf_op jit(solution)/shard_map/ppermute | solution.py:12
  309.5 5.8 %copy-start.6 = (bf16[256,512]{1,0:T(8,128)(2,1)}, bf16[256,512]{1,0:T(8,128)(2,1)S(1)}, u32[]{:S(2)}) copy-start(bf16[256,512]{1,0:T(8,128)(2,1)S(1)} %collective-permute-done.19) | copy-start | bytes 786436
  309.5 8.6 %collective-permute-start.44 = (bf16[256,512]{1,0:T(8,128)(2,1)S(1)}, bf16[256,512]{1,0:T(8,128)(2,1)S(1)}, u32[]{:S(2)}, u32[]{:S(2)}) collective-permute-start(bf16[256,512]{1,0:T(8,128)(2,1)S(1)} %get-tuple-element.24), channel_id=1, source_target_pairs={{0,1},{1,0},{2,3},{3,2},{4,5},{5,4},{6,7},{7,6},{8,9},{9,8},{10,11... | collective-permute-start | bytes 786440 | tf_op jit(solution)/shard_map/ppermute | solution.py:12
  310.0 8.6 %collective-permute-start.47 = (bf16[256,512]{1,0:T(8,128)(2,1)S(1)}, bf16[256,512]{1,0:T(8,128)(2,1)S(1)}, u32[]{:S(2)}, u32[]{:S(2)}) collective-permute-start(bf16[256,512]{1,0:T(8,128)(2,1)S(1)} %get-tuple-element.22), channel_id=1, source_target_pairs={{0,1},{1,0},{2,3},{3,2},{4,5},{5,4},{6,7},{7,6},{8,9},{9,8},{10,11... | collective-permute-start | bytes 786440 | tf_op jit(solution)/shard_map/ppermute | solution.py:12
  315.1 9.2 %collective-permute-start.40 = (bf16[256,512]{1,0:T(8,128)(2,1)S(1)}, bf16[256,512]{1,0:T(8,128)(2,1)S(1)}, u32[]{:S(2)}, u32[]{:S(2)}) collective-permute-start(bf16[256,512]{1,0:T(8,128)(2,1)S(1)} %get-tuple-element.29), channel_id=1, source_target_pairs={{0,4},{1,5},{2,6},{3,7},{4,0},{5,1},{6,2},{7,3},{8,12},{9,13},{10,... | collective-permute-start | bytes 786440 | tf_op jit(solution)/shard_map/ppermute | solution.py:12
  315.3 8.9 %collective-permute-start.42 = (bf16[256,512]{1,0:T(8,128)(2,1)S(1)}, bf16[256,512]{1,0:T(8,128)(2,1)S(1)}, u32[]{:S(2)}, u32[]{:S(2)}) collective-permute-start(bf16[256,512]{1,0:T(8,128)(2,1)S(1)} %get-tuple-element.30), channel_id=1, source_target_pairs={{0,2},{1,3},{2,0},{3,1},{4,6},{5,7},{6,4},{7,5},{8,10},{9,11},{10,... | collective-permute-start | bytes 786440 | tf_op jit(solution)/shard_map/ppermute | solution.py:12
  318.1 9.1 %collective-permute-start.21 = (bf16[256,512]{1,0:T(8,128)(2,1)S(1)}, bf16[256,512]{1,0:T(8,128)(2,1)S(1)}, u32[]{:S(2)}, u32[]{:S(2)}) collective-permute-start(bf16[256,512]{1,0:T(8,128)(2,1)S(1)} %get-tuple-element.10), channel_id=1, source_target_pairs={{0,1},{1,0},{2,3},{3,2},{4,5},{5,4},{6,7},{7,6},{8,9},{9,8},{10,11... | collective-permute-start | bytes 786440 | tf_op jit(solution)/shard_map/ppermute | solution.py:12
  318.2 13.4 %collective-permute-start.46 = (bf16[256,512]{1,0:T(8,128)(2,1)S(1)}, bf16[256,512]{1,0:T(8,128)(2,1)S(1)}, u32[]{:S(2)}, u32[]{:S(2)}) collective-permute-start(bf16[256,512]{1,0:T(8,128)(2,1)S(1)} %get-tuple-element.23), channel_id=1, source_target_pairs={{0,1},{1,0},{2,3},{3,2},{4,5},{5,4},{6,7},{7,6},{8,9},{9,8},{10,11... | collective-permute-start | bytes 786440 | tf_op jit(solution)/shard_map/ppermute | solution.py:12
  318.7 11.3 %collective-permute-start.23 = (bf16[256,512]{1,0:T(8,128)(2,1)S(1)}, bf16[256,512]{1,0:T(8,128)(2,1)}, u32[]{:S(2)}, u32[]{:S(2)}) collective-permute-start(bf16[256,512]{1,0:T(8,128)(2,1)S(1)} %get-tuple-element.6), channel_id=1, source_target_pairs={{0,4},{1,5},{2,6},{3,7},{4,0},{5,1},{6,2},{7,3},{8,12},{9,13},{10,... | collective-permute-start | bytes 786440 | tf_op jit(solution)/shard_map/ppermute | solution.py:12
  324.3 23.7 %copy-start.1 = (f32[128,52]{0,1:T(8,128)S(1)}, f32[128,52]{0,1:T(8,128)}, u32[]{:S(2)}) copy-start(f32[128,52]{0,1:T(8,128)} %param.12) | copy-start | bytes 79876
  326.6 9.5 %collective-permute-start.48 = (bf16[256,512]{1,0:T(8,128)(2,1)}, bf16[256,512]{1,0:T(8,128)(2,1)S(1)}, u32[]{:S(2)}, u32[]{:S(2)}) collective-permute-start(bf16[256,512]{1,0:T(8,128)(2,1)} %get-tuple-element.19), channel_id=1, source_target_pairs={{0,4},{1,5},{2,6},{3,7},{4,0},{5,1},{6,2},{7,3},{8,12},{9,13},{10,... | collective-permute-start | bytes 786440 | tf_op jit(solution)/shard_map/ppermute | solution.py:12
  327.1 10.6 %collective-permute-start.18 = (bf16[256,512]{1,0:T(8,128)(2,1)S(1)}, bf16[256,512]{1,0:T(8,128)(2,1)S(1)}, u32[]{:S(2)}, u32[]{:S(2)}) collective-permute-start(bf16[256,512]{1,0:T(8,128)(2,1)S(1)} %get-tuple-element.12), channel_id=1, source_target_pairs={{0,1},{1,0},{2,3},{3,2},{4,5},{5,4},{6,7},{7,6},{8,9},{9,8},{10,11... | collective-permute-start | bytes 786440 | tf_op jit(solution)/shard_map/ppermute | solution.py:12
  327.1 14.7 %collective-permute-start.20 = (bf16[256,512]{1,0:T(8,128)(2,1)S(1)}, bf16[256,512]{1,0:T(8,128)(2,1)}, u32[]{:S(2)}, u32[]{:S(2)}) collective-permute-start(bf16[256,512]{1,0:T(8,128)(2,1)S(1)} %get-tuple-element.7), channel_id=1, source_target_pairs={{0,4},{1,5},{2,6},{3,7},{4,0},{5,1},{6,2},{7,3},{8,12},{9,13},{10,... | collective-permute-start | bytes 786440 | tf_op jit(solution)/shard_map/ppermute | solution.py:12
  331.2 10.6 %collective-permute-start.24 = (bf16[256,512]{1,0:T(8,128)(2,1)S(1)}, bf16[256,512]{1,0:T(8,128)(2,1)S(1)}, u32[]{:S(2)}, u32[]{:S(2)}) collective-permute-start(bf16[256,512]{1,0:T(8,128)(2,1)S(1)} %add_convert_fusion.9), channel_id=1, source_target_pairs={{0,2},{1,3},{2,0},{3,1},{4,6},{5,7},{6,4},{7,5},{8,10},{9,11},{10,... | collective-permute-start | bytes 786440 | tf_op jit(solution)/shard_map/ppermute | solution.py:12
  331.6 11.6 %collective-permute-start.43 = (bf16[256,512]{1,0:T(8,128)(2,1)S(1)}, bf16[256,512]{1,0:T(8,128)(2,1)S(1)}, u32[]{:S(2)}, u32[]{:S(2)}) collective-permute-start(bf16[256,512]{1,0:T(8,128)(2,1)S(1)} %get-tuple-element.25), channel_id=1, source_target_pairs={{0,1},{1,0},{2,3},{3,2},{4,5},{5,4},{6,7},{7,6},{8,9},{9,8},{10,11... | collective-permute-start | bytes 786440 | tf_op jit(solution)/shard_map/ppermute | solution.py:12
  336.1 9.5 %collective-permute-start.45 = (bf16[256,512]{1,0:T(8,128)(2,1)S(1)}, bf16[256,512]{1,0:T(8,128)(2,1)}, u32[]{:S(2)}, u32[]{:S(2)}) collective-permute-start(bf16[256,512]{1,0:T(8,128)(2,1)S(1)} %get-tuple-element.20), channel_id=1, source_target_pairs={{0,4},{1,5},{2,6},{3,7},{4,0},{5,1},{6,2},{7,3},{8,12},{9,13},{10,... | collective-permute-start | bytes 786440 | tf_op jit(solution)/shard_map/ppermute | solution.py:12
  338.5 7.1 %collective-permute-start.49 = (bf16[256,512]{1,0:T(8,128)(2,1)S(1)}, bf16[256,512]{1,0:T(8,128)(2,1)S(1)}, u32[]{:S(2)}, u32[]{:S(2)}) collective-permute-start(bf16[256,512]{1,0:T(8,128)(2,1)S(1)} %add_convert_fusion.1), channel_id=1, source_target_pairs={{0,2},{1,3},{2,0},{3,1},{4,6},{5,7},{6,4},{7,5},{8,10},{9,11},{10,... | collective-permute-start | bytes 786440 | tf_op jit(solution)/shard_map/ppermute | solution.py:12
  (3 other events, 2.1 us)

commit v2 on v1

v2 whole, which is shorter than its diff:
```python
import functools
import math

import jax
import jax.numpy as jnp
from jax import lax
from jax.experimental import pallas as pl
from jax.experimental.pallas import tpu as pltpu
from jax.sharding import PartitionSpec as P

BLK = 128
RO = 8
CHUNKS = 2
VMEM_BYTES = 56 * 2**20
GATHER_MASKS = (0, 1, 4, 5, 2, 3, 6, 7)
SENT_MASKS = (7, 5, 3, 1)
KEPT_MASKS = (6, 4, 2, 0)


def round_up(value, unit):
    return -(-value // unit) * unit


def partner(shard, mask):
    return lax.ppermute(shard, "gx", [(i, i ^ mask) for i in range(lax.axis_size("gx"))])


def from_behind(shard, by):
    devices = lax.axis_size("gx")
    return lax.ppermute(shard, "gx", [(i, (i + by) % devices) for i in range(devices)])


def params():
    return pltpu.CompilerParams(vmem_limit_bytes=VMEM_BYTES)


def cost(flops, moved):
    return pl.CostEstimate(flops=int(flops), bytes_accessed=int(moved), transcendentals=0)


def scale_tokens(tokens, token_scale):
    count, width = tokens.shape
    rows = count // CHUNKS

    def kernel(x_ref, s_ref, *out_refs):
        for chunk, out_ref in enumerate(out_refs):
            span = pl.ds(chunk * rows, rows)
            for block in range(width // BLK):
                columns = pl.ds(block * BLK, BLK)
                value = x_ref[span, columns].astype(jnp.float32)
                factor = s_ref[span, block : block + 1]
                out_ref[:, columns] = (value * factor).astype(jnp.bfloat16)

    return pl.pallas_call(
        kernel,
        out_shape=[jax.ShapeDtypeStruct((rows, width), jnp.bfloat16)] * CHUNKS,
        compiler_params=params(),
        cost_estimate=cost(count * width, 4 * count * width),
    )(tokens, token_scale)


def scale_joined(gate, up, gate_factors, up_factors):
    height, width = gate.shape
    padded = round_up(width, BLK)
    rows = min(1024, height)
    groups = rows // BLK

    def kernel(gate_ref, up_ref, gf_ref, uf_ref, out_ref):
        for index, (w_ref, f_ref) in enumerate(((gate_ref, gf_ref), (up_ref, uf_ref))):
            for group in range(groups):
                span = pl.ds(group * BLK, BLK)
                value = w_ref[span, :].astype(jnp.float32) * f_ref[group : group + 1, :]
                out_ref[span, index * padded : index * padded + width] = value.astype(jnp.bfloat16)
            if padded > width:
                out_ref[:, index * padded + width : (index + 1) * padded] = jnp.zeros(
                    (rows, padded - width), jnp.bfloat16
                )

    return pl.pallas_call(
        kernel,
        grid=(height // rows,),
        in_specs=[pl.BlockSpec((rows, width), lambda i: (i, 0))] * 2
        + [pl.BlockSpec((groups, width), lambda i: (i, 0))] * 2,
        out_specs=pl.BlockSpec((rows, 2 * padded), lambda i: (i, 0)),
        out_shape=jax.ShapeDtypeStruct((height, 2 * padded), jnp.bfloat16),
        compiler_params=params(),
        cost_estimate=cost(2 * height * width, 8 * height * width),
    )(gate, up, gate_factors, up_factors)


def scale_down(down, factors, unit):
    height, width = down.shape
    columns = min(1024, width)

    def kernel(w_ref, f_ref, out_ref):
        for group in range(height // unit):
            span = pl.ds(group * unit, unit)
            value = w_ref[span, :].astype(jnp.float32) * f_ref[group : group + 1, :]
            out_ref[span, :] = value.astype(jnp.bfloat16)

    return pl.pallas_call(
        kernel,
        grid=(width // columns,),
        in_specs=[
            pl.BlockSpec((height, columns), lambda i: (0, i)),
            pl.BlockSpec((factors.shape[0], columns), lambda i: (0, i)),
        ],
        out_specs=pl.BlockSpec((height, columns), lambda i: (0, i)),
        out_shape=jax.ShapeDtypeStruct((height, width), jnp.bfloat16),
        compiler_params=params(),
        cost_estimate=cost(height * width, 4 * height * width),
    )(down, factors)


def joined_product(slot, blocks, joined):
    width = blocks[0].shape[1]
    rows = blocks[0].shape[0]
    columns = joined.shape[1]
    flat = []
    places = []
    for block in blocks:
        parts = block if isinstance(block, tuple) else (block,)
        places.append(tuple(range(len(flat), len(flat) + len(parts))))
        flat.extend(parts)

    def mask_of(step):
        mask = step * 0
        for index, value in enumerate(GATHER_MASKS):
            mask = jnp.where(step == index, value, mask)
        return mask

    def kernel(slot_ref, *refs):
        x_refs, w_ref, out_ref = refs[: len(flat)], refs[len(flat)], refs[len(flat) + 1]
        step = pl.program_id(0)
        for index, place in enumerate(places):

            @pl.when(step == index)
            def _():
                parts = [x_refs[p][...] for p in place]
                x = parts[0] if len(parts) == 1 else jnp.concatenate(parts, 0)
                value = jnp.dot(x, w_ref[...], preferred_element_type=jnp.float32)
                if index == 0:
                    out_ref[...] = value
                else:
                    out_ref[...] += value

    return pl.pallas_call(
        kernel,
        grid_spec=pltpu.PrefetchScalarGridSpec(
            num_scalar_prefetch=1,
            grid=(len(places),),
            in_specs=[pl.BlockSpec(b.shape, lambda i, s: (0, 0)) for b in flat]
            + [pl.BlockSpec((width, columns), lambda i, s: (s[0] ^ mask_of(i), 0))],
            out_specs=pl.BlockSpec((rows, columns), lambda i, s: (0, 0)),
        ),
        out_shape=jax.ShapeDtypeStruct((rows, columns), jnp.float32),
        compiler_params=params(),
        cost_estimate=cost(2 * rows * width * RO * columns, 2 * width * RO * columns),
    )(slot, *flat, joined)


def output_product(slot, hidden, down, masks, kind):
    rows, depth = hidden.shape
    width = down.shape[1] // RO

    def mask_of(step):
        return masks[0] - 2 * step

    def kernel(slot_ref, x_ref, w_ref, out_ref):
        out_ref[0] = jnp.dot(
            x_ref[...], w_ref[...], preferred_element_type=jnp.float32
        ).astype(kind)

    return pl.pallas_call(
        kernel,
        grid_spec=pltpu.PrefetchScalarGridSpec(
            num_scalar_prefetch=1,
            grid=(len(masks),),
            in_specs=[
                pl.BlockSpec((rows, depth), lambda i, s: (0, 0)),
                pl.BlockSpec((depth, width), lambda i, s: (0, s[0] ^ mask_of(i))),
            ],
            out_specs=pl.BlockSpec((1, rows, width), lambda i, s: (i, 0, 0)),
        ),
        out_shape=jax.ShapeDtypeStruct((len(masks), rows, width), kind),
        compiler_params=params(),
        cost_estimate=cost(
            2 * rows * depth * len(masks) * width, 2 * depth * len(masks) * width
        ),
    )(slot, hidden, down)


def gather_features(own):
    half = own.shape[0] // 2
    far = partner(own, 4)
    near = partner(own, 2)
    upper = partner(far[:half], 2)
    lower = partner(near[half:], 4)
    return [
        own,
        partner(own, 1),
        far,
        partner(far, 1),
        near,
        partner(near, 1),
        (upper, lower),
        (partner(upper, 1), partner(lower, 1)),
    ]


def scatter_sum(sent, kept):
    half = sent.shape[1] // 2

    def summed(index, part):
        span = slice(part * half, (part + 1) * half)
        return kept[index, span] + partner(sent[index, span], 1).astype(jnp.float32)

    def send(value, mask):
        return partner(value.astype(jnp.bfloat16), mask).astype(jnp.float32)

    diagonal_a = send(summed(0, 0), 2)
    diagonal_b = send(summed(0, 1), 4)
    far_b = send(summed(1, 1), 4)
    near_a = send(summed(2, 0), 2)
    far_a = send(summed(1, 0) + diagonal_a, 4)
    near_b = send(summed(2, 1) + diagonal_b, 2)
    return [
        (summed(3, 0) + far_a + near_a).astype(jnp.bfloat16),
        (summed(3, 1) + far_b + near_b).astype(jnp.bfloat16),
    ]


def body(tokens, token_scale, gate_tiles, up_tiles, gate_scale, up_scale, down_tiles, down_scale):
    position = lax.axis_index("gx")
    devices = lax.axis_size("gx")
    row_groups = devices // RO
    col_slot = position % RO
    row_slot = position // RO
    slot = col_slot.astype(jnp.int32).reshape(1)
    token_count = tokens.shape[0]
    tile_rows = gate_tiles.shape[1]
    tile_cols = gate_tiles.shape[2]
    piece_cols = tile_cols // row_groups
    padded = round_up(tile_cols, BLK)
    unit = math.gcd(tile_cols, BLK)
    units = tile_cols // unit

    def column_factors(blocks):
        rows = lax.dynamic_slice_in_dim(
            blocks, row_slot * (tile_rows // BLK), tile_rows // BLK, 0
        )
        fine = jnp.repeat(rows, BLK // unit, 1)
        fine = lax.dynamic_slice_in_dim(fine, col_slot * units, units, 1)
        return jnp.repeat(fine, unit, 1)

    def row_factors(blocks):
        columns = lax.dynamic_slice_in_dim(
            blocks, row_slot * (tile_rows // BLK), tile_rows // BLK, 1
        )
        fine = jnp.repeat(columns, BLK // unit, 0)
        fine = lax.dynamic_slice_in_dim(fine, col_slot * units, units, 0)
        return jnp.repeat(fine, BLK, 1)

    tokens_eff = scale_tokens(tokens, token_scale)
    joined = scale_joined(
        gate_tiles[0], up_tiles[0], column_factors(gate_scale), column_factors(up_scale)
    )
    down_eff = scale_down(down_tiles[0], row_factors(down_scale), unit)
    rows = token_count // CHUNKS

    def finish(own):
        partial_value = joined_product(slot, gather_features(own), joined)

        def share(target):
            start = target * piece_cols
            return jnp.stack(
                (
                    lax.dynamic_slice_in_dim(partial_value, start, piece_cols, 1),
                    lax.dynamic_slice_in_dim(partial_value, padded + start, piece_cols, 1),
                ),
                0,
            )

        summed = share((row_slot - 1) % row_groups)
        for step in range(1, row_groups):
            summed = from_behind(summed.astype(jnp.bfloat16), RO).astype(jnp.float32)
            summed = summed + share((row_slot - 1 - step) % row_groups)
        hidden_piece = (jax.nn.silu(summed[0]) * summed[1]).astype(jnp.bfloat16)
        if row_groups == 2:
            other = from_behind(hidden_piece, RO)
            hidden_full = jnp.where(
                row_slot == 0,
                jnp.concatenate((hidden_piece, other), 1),
                jnp.concatenate((other, hidden_piece), 1),
            )
        else:
            hidden_full = jnp.zeros((rows, tile_cols), jnp.bfloat16)
            current = hidden_piece
            for step in range(row_groups):
                if step:
                    current = from_behind(current, RO)
                source = (row_slot - step) % row_groups
                hidden_full = lax.dynamic_update_slice_in_dim(
                    hidden_full, current, source * piece_cols, 1
                )
        sent = output_product(slot, hidden_full, down_eff, SENT_MASKS, jnp.bfloat16)
        kept = output_product(slot, hidden_full, down_eff, KEPT_MASKS, jnp.float32)
        return scatter_sum(sent, kept)

    outs = []
    for own in tokens_eff:
        outs.extend(finish(own))
    return jnp.concatenate(outs, 0)


def solution(mesh):
    return jax.shard_map(
        body,
        mesh=mesh,
        in_specs=(
            P("groups", "gx"),
            P("groups", "gx"),
            P("gx", None, None),
            P("gx", None, None),
            P(),
            P(),
            P("gx", None, None),
            P(),
        ),
        out_specs=P("groups", "gx"),
        check_vma=False,
    )
```

time: 352 us -> 292 us (0.83)
  Pallas kernels: 0 us -> 98.1 us
  matrix products: 96.5 us -> 0 us
  other arithmetic: 71.4 us -> 10.8 us
  waiting for transfers between devices: 67 us -> 95.2 us
  local copies, waits for them, and re-layouts: 82.5 us -> 56 us
    pallas_call x0 -> x9, Pallas kernels: none -> 98.1 us  [the longest x2 33.8 us: joined_product(): pl.pallas_call(kernel, grid_spec=pltpu.PrefetchScalarGridSpec(num_scalar_...]
    dot_general x7 -> x0, matrix products: 96.5 us -> none  [the longest x2 64.4 us: finish(): result = jnp.dot(hidden_full, down_eff, preferred_element_type=jnp.float32)]
    convert_element_type x2 -> x4, other arithmetic: 52 us -> 1.03 us  [the longest x2 0.72 us: scatter_sum(): (summed(3, 0) + far_a + near_a).astype(jnp.bfloat16)]
    unnamed x35 -> x41, local copies, waits for them, and re-layouts: 4.98 us -> 43.1 us
    mul x4 -> x0, local copies, waits for them, and re-layouts: 33.2 us -> none  [the longest x2 21.9 us: scale_by_columns(): stored.astype(jnp.float32).reshape(height // BLK, BLK, width)]
    dynamic_update_slice x23 -> x0, local copies, waits for them, and re-layouts: 27.3 us -> none  [the longest x10 11.2 us: gather_features(): lax.dynamic_update_slice_in_dim(gathered, partner(block, 1), (col_slot ^...]
    ppermute x46, waiting for transfers between devices: 34.6 us -> 55.3 us  [partner(): lax.ppermute(shard, 'gx', [(i, i ^ mask) for i in range(lax.axis_size('gx...]
    ppermute x4, waiting for transfers between devices: 32.4 us -> 39.9 us  [from_behind(): lax.ppermute(shard, 'gx', [(i, (i + by) % devices) for i in range(devices)])]
  transfers between devices with their start and end apart: 50 -> 50, of which waited for: 13 -> 15; matrix products, arithmetic and copies ran while one was open for 68% -> 21% of each run, Pallas kernels for 0% -> 33%
where the time goes in v2:
time: 292 us; the launch traced here: 290 us
  Pallas kernels  98.1 us (34%)
  waiting for transfers between devices  95.2 us (33%)
  local copies, waits for them, and re-layouts  56 us (19%)
  starting transfers between devices  29.7 us (10%)
  other arithmetic  10.8 us (4%)
    ppermute x46, waiting for transfers between devices, partner(): lax.ppermute(shard, 'gx', [(i, i ^ mask) for i in range(lax.axis_size('gx...  55.3 us
    unnamed x41, local copies, waits for them, and re-layouts  43.1 us
    ppermute x4, waiting for transfers between devices, from_behind(): lax.ppermute(shard, 'gx', [(i, (i + by) % devices) for i in range(devices)])  39.9 us
    pallas_call x2, Pallas kernels, joined_product(): pl.pallas_call(kernel, grid_spec=pltpu.PrefetchScalarGridSpec(num_scalar_...  33.8 us
    pallas_call x4, Pallas kernels, output_product(): pl.pallas_call(kernel, grid_spec=pltpu.PrefetchScalarGridSpec(num_scalar_...  26.5 us
    ppermute x46, starting transfers between devices, partner(): lax.ppermute(shard, 'gx', [(i, i ^ mask) for i in range(lax.axis_size('gx...  25.6 us
    pallas_call x1, Pallas kernels, scale_joined(): pl.pallas_call(kernel, grid=(height // rows,), in_specs=[pl.BlockSpec((ro...  22.4 us
    pallas_call x1, Pallas kernels, scale_down(): pl.pallas_call(kernel, grid=(width // columns,), in_specs=[pl.BlockSpec((...  12.6 us
  transfers between devices with their start and end apart: 50, of which 15 were waited for; matrix products, arithmetic and copies ran while one was open for 21% of the time, Pallas kernels for 33%

profile of v2, /device:TPU:0, one launch (start us, length us, event | category | flops | bytes accessed | tf_op | source)
XLA Modules:
  0.0 290.3 jit_solution(5967785577972184790)
XLA Ops:
  0.0 1.6 copy.14.s_ref
  1.6 2.8 shard_map.82
  4.4 3.0 %collective-permute-start.1 = (bf16[256,1024]{1,0:T(8,128)(2,1)}, bf16[256,1024]{1,0:T(8,128)(2,1)S(1)}, u32[]{:S(2)}, u32[]{:S(2)}) collective-permute-start(bf16[256,1024]{1,0:T(8,128)(2,1)} %get-tuple-element.7.refs_0_), channel_id=1, source_target_pairs={{0,4},{1,5},{2,6},{3,7},{4,0},{5,1},{6,2},{7,3},{8,12},{9,13},{10,... | collective-permute-start | bytes 1572872 | tf_op jit(solution)/shard_map/ppermute | solution.py:25
  7.4 1.5 collective-permute-start.3
  9.4 10.9 %collective-permute-done.1.refs_2_ = bf16[256,1024]{1,0:T(8,128)(2,1)S(1)} collective-permute-done((bf16[256,1024]{1,0:T(8,128)(2,1)}, bf16[256,1024]{1,0:T(8,128)(2,1)S(1)}, u32[]{:S(2)}, u32[]{:S(2)}) %collective-permute-start.1) | collective-permute-done | bytes 524320 | tf_op jit(solution)/shard_map/ppermute | solution.py:25
  20.4 2.1 collective-permute-start.5
  22.5 1.6 collective-permute-start.6
  24.1 7.5 %collective-permute-done.26.refs_2_ = bf16[256,1024]{1,0:T(8,128)(2,1)S(1)} collective-permute-done((bf16[256,1024]{1,0:T(8,128)(2,1)}, bf16[256,1024]{1,0:T(8,128)(2,1)S(1)}, u32[]{:S(2)}, u32[]{:S(2)}) %collective-permute-start.26) | collective-permute-done | bytes 524320 | tf_op jit(solution)/shard_map/ppermute | solution.py:25
  31.6 0.8 slice.180
  32.4 2.0 collective-permute-start.30
  34.4 0.5 collective-permute-start.4
  34.9 0.8 constant_dynamic-slice_fusion.3
  35.8 0.7 slice.181
  36.5 2.9 %collective-permute-done.5.refs_6_ = bf16[128,1024]{1,0:T(8,128)(2,1)} collective-permute-done((bf16[128,1024]{1,0:T(8,128)(2,1)S(1)}, bf16[128,1024]{1,0:T(8,128)(2,1)}, u32[]{:S(2)}, u32[]{:S(2)}) %collective-permute-start.5) | collective-permute-done | bytes 262176 | tf_op jit(solution)/shard_map/ppermute | solution.py:25
  39.4 4.0 %collective-permute-done.30.refs_6_ = bf16[128,1024]{1,0:T(8,128)(2,1)S(1)} collective-permute-done((bf16[128,1024]{1,0:T(8,128)(2,1)}, bf16[128,1024]{1,0:T(8,128)(2,1)S(1)}, u32[]{:S(2)}, u32[]{:S(2)}) %collective-permute-start.30) | collective-permute-done | bytes 262176 | tf_op jit(solution)/shard_map/ppermute | solution.py:25
  43.9 0.8 reshape.23.gf_ref
  45.0 0.8 reshape.25.uf_ref
  45.8 19.3 %copy.15 = bf16[1,8192,832]{2,1,0:T(8,128)(2,1)} copy(bf16[1,8192,832]{1,2,0:T(8,128)(2,1)} %param.10) | data formatting | bytes 27262976 | tf_op args[2]
  65.1 19.2 %copy.16 = bf16[1,8192,832]{2,1,0:T(8,128)(2,1)} copy(bf16[1,8192,832]{1,2,0:T(8,128)(2,1)} %param.11) | data formatting | bytes 27262976 | tf_op args[3]
  84.7 1.1 copy.19
  85.9 12.6 %shard_map.85.w_ref = bf16[832,8192]{1,0:T(8,128)(2,1)} custom-call(bf16[832,8192]{1,0:T(8,128)(2,1)} %bitcast.200, f32[13,8192]{1,0:T(8,128)} %bitcast.201), custom_call_target="tpu_custom_call" | custom-call | flops 6815744 | bytes 27262976 | tf_op jit(solution)/shard_map/pallas_call | solution.py:101
  98.5 22.4 %shard_map.83.refs_10_ = bf16[8192,1792]{1,0:T(8,128)(2,1)} custom-call(bf16[8192,832]{1,0:T(8,128)(2,1)} %bitcast.198, bf16[8192,832]{1,0:T(8,128)(2,1)} %bitcast.199, f32[64,832]{1,0:T(8,128)} %reshape.23.gf_ref, f32[64,832]{1,0:T(8,128)} %reshape.25.uf_ref), custom_call_target="tpu_custom_call" | custom-call | flops 13631488 | bytes 54525952 | tf_op jit(solution)/shard_map/pallas_call | solution.py:79
  120.9 0.6 collective-permute-start.25
  122.5 16.9 %shard_map.84 = f32[256,1792]{1,0:T(8,128)} custom-call(s32[1]{0:T(128)} %bitcast.slot_ref, bf16[256,1024]{1,0:T(8,128)(2,1)} %get-tuple-element.7.refs_0_, bf16[256,1024]{1,0:T(8,128)(2,1)} %copy-done.11, bf16[256,1024]{1,0:T(8,128)(2,1)} %copy-done.8, bf16[256,1024]{1,0:T(8,128)(2,1)} %collective-permute-done.2.refs_3_, bf16[256,1024]{1,0:T(8,128)(2,1)} %copy-done.9, ...), custom_call_target="tpu_custom_call" | custom-call | flops 7516192768 | bytes 29360128 | tf_op jit(solution)/shard_map/pallas_call | solution.py:147
  139.4 1.5 fusion.48
  141.0 2.7 collective-permute-start.9
  143.8 0.7 copy-done.16
  144.7 0.8 copy-done.14
  145.5 16.9 %shard_map.88 = f32[256,1792]{1,0:T(8,128)} custom-call(s32[1]{0:T(128)} %bitcast.slot_ref, bf16[256,1024]{1,0:T(8,128)(2,1)} %get-tuple-element.8.refs_0_, bf16[256,1024]{1,0:T(8,128)(2,1)} %copy-done.12, bf16[256,1024]{1,0:T(8,128)(2,1)} %copy-done.6, bf16[256,1024]{1,0:T(8,128)(2,1)} %copy-done.13, bf16[256,1024]{1,0:T(8,128)(2,1)} %copy-done.7, ...), custom_call_target="tpu_custom_call" | custom-call | flops 7516192768 | bytes 29360128 | tf_op jit(solution)/shard_map/pallas_call | solution.py:147
  162.5 1.6 fusion.50
  165.3 1.7 collective-permute-done.9
  167.4 0.9 collective-permute-start.10
  168.3 27.4 %collective-permute-done.34 = bf16[2,256,416]{2,1,0:T(8,128)(2,1)S(1)} collective-permute-done((bf16[2,256,416]{2,1,0:T(8,128)(2,1)S(1)}, bf16[2,256,416]{2,1,0:T(8,128)(2,1)S(1)}, u32[]{:S(2)}, u32[]{:S(2)}) %collective-permute-start.34) | collective-permute-done | bytes 426016 | tf_op jit(solution)/shard_map/ppermute | solution.py:30
  196.0 10.8 %collective-permute-done.10 = bf16[256,416]{1,0:T(8,128)(2,1)S(1)} collective-permute-done((bf16[256,416]{1,0:T(8,128)(2,1)S(1)}, bf16[256,416]{1,0:T(8,128)(2,1)S(1)}, u32[]{:S(2)}, u32[]{:S(2)}) %collective-permute-start.10) | collective-permute-done | bytes 213024 | tf_op jit(solution)/shard_map/ppermute | solution.py:30
  206.9 1.1 maximum_select_fusion.x_ref
  208.0 6.3 %shard_map.87 = bf16[4,256,1024]{2,1,0:T(8,128)(2,1)} custom-call(s32[1]{0:T(128)} %bitcast.slot_ref, bf16[256,832]{1,0:T(8,128)(2,1)} %maximum_select_fusion.x_ref, bf16[832,8192]{1,0:T(8,128)(2,1)} %shard_map.85.w_ref), custom_call_target="tpu_custom_call" | custom-call | flops 1744830464 | bytes 6815744 | tf_op jit(solution)/shard_map/pallas_call | solution.py:174
  214.3 1.7 slice_bitcast_fusion.35
  216.0 0.5 collective-permute-start.12
  216.6 1.1 maximum_select_fusion.1.x_ref
  217.7 6.3 %shard_map.90 = bf16[4,256,1024]{2,1,0:T(8,128)(2,1)} custom-call(s32[1]{0:T(128)} %bitcast.slot_ref, bf16[256,832]{1,0:T(8,128)(2,1)} %maximum_select_fusion.1.x_ref, bf16[832,8192]{1,0:T(8,128)(2,1)} %shard_map.85.w_ref), custom_call_target="tpu_custom_call" | custom-call | flops 1744830464 | bytes 6815744 | tf_op jit(solution)/shard_map/pallas_call | solution.py:174
  224.0 2.5 slice_bitcast_fusion.27
  226.9 6.9 %shard_map.86 = f32[4,256,1024]{2,1,0:T(8,128)} custom-call(s32[1]{0:T(128)} %bitcast.slot_ref, bf16[256,832]{1,0:T(8,128)(2,1)} %maximum_select_fusion.x_ref, bf16[832,8192]{1,0:T(8,128)(2,1)} %shard_map.85.w_ref), custom_call_target="tpu_custom_call" | custom-call | flops 1744830464 | bytes 6815744 | tf_op jit(solution)/shard_map/pallas_call | solution.py:174
  233.8 1.8 fusion.38
  235.6 1.5 collective-permute-start.14
  237.1 7.0 %shard_map.89 = f32[4,256,1024]{2,1,0:T(8,128)} custom-call(s32[1]{0:T(128)} %bitcast.slot_ref, bf16[256,832]{1,0:T(8,128)(2,1)} %maximum_select_fusion.1.x_ref, bf16[832,8192]{1,0:T(8,128)(2,1)} %shard_map.85.w_ref), custom_call_target="tpu_custom_call" | custom-call | flops 1744830464 | bytes 6815744 | tf_op jit(solution)/shard_map/pallas_call | solution.py:174
  244.1 0.5 collective-permute-start.19
  244.6 1.2 fusion.14
  246.3 0.8 collective-permute-start.39
  247.2 1.2 fusion.41
  248.7 5.9 %collective-permute-done.39 = bf16[128,1024]{1,0:T(8,128)(2,1)S(1)} collective-permute-done((bf16[128,1024]{1,0:T(8,128)(2,1)S(1)}, bf16[128,1024]{1,0:T(8,128)(2,1)S(1)}, u32[]{:S(2)}, u32[]{:S(2)}) %collective-permute-start.39) | collective-permute-done | bytes 262176 | tf_op jit(solution)/shard_map/ppermute | solution.py:25
  254.6 0.8 collective-permute-start.17
  255.5 1.4 fusion.17
  257.6 4.5 %collective-permute-done.17 = bf16[128,1024]{1,0:T(8,128)(2,1)S(1)} collective-permute-done((bf16[128,1024]{1,0:T(8,128)(2,1)S(1)}, bf16[128,1024]{1,0:T(8,128)(2,1)S(1)}, u32[]{:S(2)}, u32[]{:S(2)}) %collective-permute-start.17) | collective-permute-done | bytes 262176 | tf_op jit(solution)/shard_map/ppermute | solution.py:25
  262.1 0.8 collective-permute-start.42
  264.0 2.2 collective-permute-done.40
  266.2 2.4 collective-permute-done.42
  269.3 1.8 collective-permute-start.20
  271.1 2.0 collective-permute-done.23
  273.2 1.2 collective-permute-start.24
  274.5 4.3 %collective-permute-done.48 = bf16[128,1024]{1,0:T(8,128)(2,1)S(1)} collective-permute-done((bf16[128,1024]{1,0:T(8,128)(2,1)S(1)}, bf16[128,1024]{1,0:T(8,128)(2,1)S(1)}, u32[]{:S(2)}, u32[]{:S(2)}) %collective-permute-start.48) | collective-permute-done | bytes 262176 | tf_op jit(solution)/shard_map/ppermute | solution.py:25
  278.9 1.5 collective-permute-start.49
  280.3 4.0 %collective-permute-done.20 = bf16[128,1024]{1,0:T(8,128)(2,1)S(1)} collective-permute-done((bf16[128,1024]{1,0:T(8,128)(2,1)S(1)}, bf16[128,1024]{1,0:T(8,128)(2,1)S(1)}, u32[]{:S(2)}, u32[]{:S(2)}) %collective-permute-start.20) | collective-permute-done | bytes 262176 | tf_op jit(solution)/shard_map/ppermute | solution.py:25
  284.5 4.6 %collective-permute-done.45 = bf16[128,1024]{1,0:T(8,128)(2,1)S(1)} collective-permute-done((bf16[128,1024]{1,0:T(8,128)(2,1)S(1)}, bf16[128,1024]{1,0:T(8,128)(2,1)S(1)}, u32[]{:S(2)}, u32[]{:S(2)}) %collective-permute-start.45) | collective-permute-done | bytes 262176 | tf_op jit(solution)/shard_map/ppermute | solution.py:25
  289.2 1.0 pad_maximum_fusion
  (130 shorter events, 9.4 us)
Async XLA Ops:
  0.0 84.4 %copy-start = (f32[52,128]{1,0:T(8,128)S(1)}, f32[52,128]{1,0:T(8,128)}, u32[]{:S(2)}) copy-start(f32[52,128]{1,0:T(8,128)} %param.15) | copy-start | bytes 79876
  4.4 16.0 %collective-permute-start.1 = (bf16[256,1024]{1,0:T(8,128)(2,1)}, bf16[256,1024]{1,0:T(8,128)(2,1)S(1)}, u32[]{:S(2)}, u32[]{:S(2)}) collective-permute-start(bf16[256,1024]{1,0:T(8,128)(2,1)} %get-tuple-element.7.refs_0_), channel_id=1, source_target_pairs={{0,4},{1,5},{2,6},{3,7},{4,0},{5,1},{6,2},{7,3},{8,12},{9,13},{10,... | collective-permute-start | bytes 1572872 | tf_op jit(solution)/shard_map/ppermute | solution.py:25
  7.4 15.1 %collective-permute-start.3 = (bf16[256,1024]{1,0:T(8,128)(2,1)}, bf16[256,1024]{1,0:T(8,128)(2,1)S(1)}, u32[]{:S(2)}, u32[]{:S(2)}) collective-permute-start(bf16[256,1024]{1,0:T(8,128)(2,1)} %get-tuple-element.7.refs_0_), channel_id=1, source_target_pairs={{0,2},{1,3},{2,0},{3,1},{4,6},{5,7},{6,4},{7,5},{8,10},{9,11},{10,... | collective-permute-start | bytes 1572872 | tf_op jit(solution)/shard_map/ppermute | solution.py:25
  8.9 22.7 %collective-permute-start.26 = (bf16[256,1024]{1,0:T(8,128)(2,1)}, bf16[256,1024]{1,0:T(8,128)(2,1)S(1)}, u32[]{:S(2)}, u32[]{:S(2)}) collective-permute-start(bf16[256,1024]{1,0:T(8,128)(2,1)} %get-tuple-element.8.refs_0_), channel_id=1, source_target_pairs={{0,4},{1,5},{2,6},{3,7},{4,0},{5,1},{6,2},{7,3},{8,12},{9,13},{10,... | collective-permute-start | bytes 1572872 | tf_op jit(solution)/shard_map/ppermute | solution.py:25
  9.4 25.0 %collective-permute-start = (bf16[256,1024]{1,0:T(8,128)(2,1)}, bf16[256,1024]{1,0:T(8,128)(2,1)S(1)}, u32[]{:S(2)}, u32[]{:S(2)}) collective-permute-start(bf16[256,1024]{1,0:T(8,128)(2,1)} %get-tuple-element.7.refs_0_), channel_id=1, source_target_pairs={{0,1},{1,0},{2,3},{3,2},{4,5},{5,4},{6,7},{7,6},{8,9},{9,8},{10,11... | collective-permute-start | bytes 1572872 | tf_op jit(solution)/shard_map/ppermute | solution.py:25
  9.4 25.0 %collective-permute-start.28 = (bf16[256,1024]{1,0:T(8,128)(2,1)}, bf16[256,1024]{1,0:T(8,128)(2,1)S(1)}, u32[]{:S(2)}, u32[]{:S(2)}) collective-permute-start(bf16[256,1024]{1,0:T(8,128)(2,1)} %get-tuple-element.8.refs_0_), channel_id=1, source_target_pairs={{0,2},{1,3},{2,0},{3,1},{4,6},{5,7},{6,4},{7,5},{8,10},{9,11},{10,... | collective-permute-start | bytes 1572872 | tf_op jit(solution)/shard_map/ppermute | solution.py:25
  20.4 44.8 %copy-start.8 = (bf16[256,1024]{1,0:T(8,128)(2,1)}, bf16[256,1024]{1,0:T(8,128)(2,1)S(1)}, u32[]{:S(2)}) copy-start(bf16[256,1024]{1,0:T(8,128)(2,1)S(1)} %collective-permute-done.1.refs_2_) | copy-start | bytes 1572868
  20.4 19.0 %collective-permute-start.5 = (bf16[128,1024]{1,0:T(8,128)(2,1)S(1)}, bf16[128,1024]{1,0:T(8,128)(2,1)}, u32[]{:S(2)}, u32[]{:S(2)}) collective-permute-start(bf16[128,1024]{1,0:T(8,128)(2,1)S(1)} %slice.160), channel_id=1, source_target_pairs={{0,2},{1,3},{2,0},{3,1},{4,6},{5,7},{6,4},{7,5},{8,10},{9,11},{10,... | collective-permute-start | bytes 786440 | tf_op jit(solution)/shard_map/ppermute | solution.py:25
  22.5 42.7 %copy-start.9 = (bf16[256,1024]{1,0:T(8,128)(2,1)}, bf16[256,1024]{1,0:T(8,128)(2,1)S(1)}, u32[]{:S(2)}) copy-start(bf16[256,1024]{1,0:T(8,128)(2,1)S(1)} %collective-permute-done.3.refs_4_) | copy-start | bytes 1572868
  22.5 16.9 %collective-permute-start.6 = (bf16[128,1024]{1,0:T(8,128)(2,1)S(1)}, bf16[128,1024]{1,0:T(8,128)(2,1)}, u32[]{:S(2)}, u32[]{:S(2)}) collective-permute-start(bf16[128,1024]{1,0:T(8,128)(2,1)S(1)} %slice.161), channel_id=1, source_target_pairs={{0,4},{1,5},{2,6},{3,7},{4,0},{5,1},{6,2},{7,3},{8,12},{9,13},{10,... | collective-permute-start | bytes 786440 | tf_op jit(solution)/shard_map/ppermute | solution.py:25
  31.6 89.9 %copy-start.6 = (bf16[256,1024]{1,0:T(8,128)(2,1)}, bf16[256,1024]{1,0:T(8,128)(2,1)S(1)}, u32[]{:S(2)}) copy-start(bf16[256,1024]{1,0:T(8,128)(2,1)S(1)} %collective-permute-done.26.refs_2_) | copy-start | bytes 1572868
  32.4 11.1 %collective-permute-start.30 = (bf16[128,1024]{1,0:T(8,128)(2,1)}, bf16[128,1024]{1,0:T(8,128)(2,1)S(1)}, u32[]{:S(2)}, u32[]{:S(2)}) collective-permute-start(bf16[128,1024]{1,0:T(8,128)(2,1)} %slice.180), channel_id=1, source_target_pairs={{0,2},{1,3},{2,0},{3,1},{4,6},{5,7},{6,4},{7,5},{8,10},{9,11},{10,... | collective-permute-start | bytes 786440 | tf_op jit(solution)/shard_map/ppermute | solution.py:25
  34.4 30.8 %copy-start.11 = (bf16[256,1024]{1,0:T(8,128)(2,1)}, bf16[256,1024]{1,0:T(8,128)(2,1)S(1)}, u32[]{:S(2)}) copy-start(bf16[256,1024]{1,0:T(8,128)(2,1)S(1)} %collective-permute-done.refs_1_) | copy-start | bytes 1572868
  34.4 87.6 %collective-permute-start.2 = (bf16[256,1024]{1,0:T(8,128)(2,1)S(1)}, bf16[256,1024]{1,0:T(8,128)(2,1)}, u32[]{:S(2)}, u32[]{:S(2)}) collective-permute-start(bf16[256,1024]{1,0:T(8,128)(2,1)S(1)} %collective-permute-done.1.refs_2_), channel_id=1, source_target_pairs={{0,1},{1,0},{2,3},{3,2},{4,5},{5,4},{6,7},{7,6},{8,9},{9,8},{10,11... | collective-permute-start | bytes 1572872 | tf_op jit(solution)/shard_map/ppermute | solution.py:25
  34.4 87.2 %copy-start.7 = (bf16[256,1024]{1,0:T(8,128)(2,1)}, bf16[256,1024]{1,0:T(8,128)(2,1)S(1)}, u32[]{:S(2)}) copy-start(bf16[256,1024]{1,0:T(8,128)(2,1)S(1)} %collective-permute-done.28.refs_4_) | copy-start | bytes 1572868
  34.4 87.7 %collective-permute-start.4 = (bf16[256,1024]{1,0:T(8,128)(2,1)S(1)}, bf16[256,1024]{1,0:T(8,128)(2,1)}, u32[]{:S(2)}, u32[]{:S(2)}) collective-permute-start(bf16[256,1024]{1,0:T(8,128)(2,1)S(1)} %collective-permute-done.3.refs_4_), channel_id=1, source_target_pairs={{0,1},{1,0},{2,3},{3,2},{4,5},{5,4},{6,7},{7,6},{8,9},{9,8},{10,11... | collective-permute-start | bytes 1572872 | tf_op jit(solution)/shard_map/ppermute | solution.py:25
  39.4 81.5 %collective-permute-start.31 = (bf16[128,1024]{1,0:T(8,128)(2,1)}, bf16[128,1024]{1,0:T(8,128)(2,1)}, u32[]{:S(2)}, u32[]{:S(2)}) collective-permute-start(bf16[128,1024]{1,0:T(8,128)(2,1)} %slice.181), channel_id=1, source_target_pairs={{0,4},{1,5},{2,6},{3,7},{4,0},{5,1},{6,2},{7,3},{8,12},{9,13},{10,... | collective-permute-start | bytes 786440 | tf_op jit(solution)/shard_map/ppermute | solution.py:25
  39.4 82.0 %collective-permute-start.7 = (bf16[128,1024]{1,0:T(8,128)(2,1)}, bf16[128,1024]{1,0:T(8,128)(2,1)}, u32[]{:S(2)}, u32[]{:S(2)}) collective-permute-start(bf16[128,1024]{1,0:T(8,128)(2,1)} %collective-permute-done.5.refs_6_), channel_id=1, source_target_pairs={{0,1},{1,0},{2,3},{3,2},{4,5},{5,4},{6,7},{7,6},{8,9},{9,8},{10,11... | collective-permute-start | bytes 786440 | tf_op jit(solution)/shard_map/ppermute | solution.py:25
  43.5 78.5 %copy-start.15 = (bf16[128,1024]{1,0:T(8,128)(2,1)}, bf16[128,1024]{1,0:T(8,128)(2,1)S(1)}, u32[]{:S(2)}) copy-start(bf16[128,1024]{1,0:T(8,128)(2,1)S(1)} %collective-permute-done.30.refs_6_) | copy-start | bytes 786436
  43.5 78.1 %collective-permute-start.8 = (bf16[128,1024]{1,0:T(8,128)(2,1)}, bf16[128,1024]{1,0:T(8,128)(2,1)}, u32[]{:S(2)}, u32[]{:S(2)}) collective-permute-start(bf16[128,1024]{1,0:T(8,128)(2,1)} %collective-permute-done.6.refs_7_), channel_id=1, source_target_pairs={{0,1},{1,0},{2,3},{3,2},{4,5},{5,4},{6,7},{7,6},{8,9},{9,8},{10,11... | collective-permute-start | bytes 786440 | tf_op jit(solution)/shard_map/ppermute | solution.py:25
  98.5 22.4 %copy-start.10 = (bf16[256,1024]{1,0:T(8,128)(2,1)S(1)}, bf16[256,1024]{1,0:T(8,128)(2,1)}, u32[]{:S(2)}) copy-start(bf16[256,1024]{1,0:T(8,128)(2,1)} %get-tuple-element.8.refs_0_) | copy-start | bytes 1572868
  120.9 20.1 %collective-permute-start.25 = (bf16[256,1024]{1,0:T(8,128)(2,1)S(1)}, bf16[256,1024]{1,0:T(8,128)(2,1)S(1)}, u32[]{:S(2)}, u32[]{:S(2)}) collective-permute-start(bf16[256,1024]{1,0:T(8,128)(2,1)S(1)} %copy-done.10), channel_id=1, source_target_pairs={{0,1},{1,0},{2,3},{3,2},{4,5},{5,4},{6,7},{7,6},{8,9},{9,8},{10,11... | collective-permute-start | bytes 1572872 | tf_op jit(solution)/shard_map/ppermute | solution.py:25
  121.5 22.2 %collective-permute-start.27 = (bf16[256,1024]{1,0:T(8,128)(2,1)S(1)}, bf16[256,1024]{1,0:T(8,128)(2,1)S(1)}, u32[]{:S(2)}, u32[]{:S(2)}) collective-permute-start(bf16[256,1024]{1,0:T(8,128)(2,1)S(1)} %collective-permute-done.26.refs_2_), channel_id=1, source_target_pairs={{0,1},{1,0},{2,3},{3,2},{4,5},{5,4},{6,7},{7,6},{8,9},{9,8},{10,11... | collective-permute-start | bytes 1572872 | tf_op jit(solution)/shard_map/ppermute | solution.py:25
  121.6 22.2 %collective-permute-start.29 = (bf16[256,1024]{1,0:T(8,128)(2,1)S(1)}, bf16[256,1024]{1,0:T(8,128)(2,1)S(1)}, u32[]{:S(2)}, u32[]{:S(2)}) collective-permute-start(bf16[256,1024]{1,0:T(8,128)(2,1)S(1)} %collective-permute-done.28.refs_4_), channel_id=1, source_target_pairs={{0,1},{1,0},{2,3},{3,2},{4,5},{5,4},{6,7},{7,6},{8,9},{9,8},{10,11... | collective-permute-start | bytes 1572872 | tf_op jit(solution)/shard_map/ppermute | solution.py:25
  122.0 21.7 %collective-permute-start.32 = (bf16[128,1024]{1,0:T(8,128)(2,1)S(1)}, bf16[128,1024]{1,0:T(8,128)(2,1)S(1)}, u32[]{:S(2)}, u32[]{:S(2)}) collective-permute-start(bf16[128,1024]{1,0:T(8,128)(2,1)S(1)} %collective-permute-done.30.refs_6_), channel_id=1, source_target_pairs={{0,1},{1,0},{2,3},{3,2},{4,5},{5,4},{6,7},{7,6},{8,9},{9,8},{10,11... | collective-permute-start | bytes 786440 | tf_op jit(solution)/shard_map/ppermute | solution.py:25
  122.1 21.6 %collective-permute-start.33 = (bf16[128,1024]{1,0:T(8,128)(2,1)}, bf16[128,1024]{1,0:T(8,128)(2,1)S(1)}, u32[]{:S(2)}, u32[]{:S(2)}) collective-permute-start(bf16[128,1024]{1,0:T(8,128)(2,1)} %collective-permute-done.31.refs_7_), channel_id=1, source_target_pairs={{0,1},{1,0},{2,3},{3,2},{4,5},{5,4},{6,7},{7,6},{8,9},{9,8},{10,11... | collective-permute-start | bytes 786440 | tf_op jit(solution)/shard_map/ppermute | solution.py:25
  141.0 23.6 %copy-start.4 = (f32[256,1792]{1,0:T(8,128)S(1)}, f32[256,1792]{1,0:T(8,128)}, u32[]{:S(2)}) copy-start(f32[256,1792]{1,0:T(8,128)} %shard_map.84) | copy-start | bytes 5505028
  141.0 2.8 copy-start.12
  141.0 26.0 %collective-permute-start.9 = (bf16[2,256,416]{2,1,0:T(8,128)(2,1)S(1)}, bf16[2,256,416]{2,1,0:T(8,128)(2,1)S(1)}, u32[]{:S(2)}, u32[]{:S(2)}) collective-permute-start(bf16[2,256,416]{2,1,0:T(8,128)(2,1)S(1)} %pad_maximum_fusion.1), channel_id=1, source_target_pairs={{0,8},{1,9},{2,10},{3,11},{4,12},{5,13},{6,14},{7,15},{8,0},{9,1},... | collective-permute-start | bytes 1277960 | tf_op jit(solution)/shard_map/ppermute | solution.py:30
  162.5 2.4 copy-start.5
  164.1 31.5 %collective-permute-start.34 = (bf16[2,256,416]{2,1,0:T(8,128)(2,1)S(1)}, bf16[2,256,416]{2,1,0:T(8,128)(2,1)S(1)}, u32[]{:S(2)}, u32[]{:S(2)}) collective-permute-start(bf16[2,256,416]{2,1,0:T(8,128)(2,1)S(1)} %pad_maximum_fusion.2), channel_id=1, source_target_pairs={{0,8},{1,9},{2,10},{3,11},{4,12},{5,13},{6,14},{7,15},{8,0},{9,1},... | collective-permute-start | bytes 1277960 | tf_op jit(solution)/shard_map/ppermute | solution.py:30
  167.4 39.5 %collective-permute-start.10 = (bf16[256,416]{1,0:T(8,128)(2,1)S(1)}, bf16[256,416]{1,0:T(8,128)(2,1)S(1)}, u32[]{:S(2)}, u32[]{:S(2)}) collective-permute-start(bf16[256,416]{1,0:T(8,128)(2,1)S(1)} %fusion.47), channel_id=1, source_target_pairs={{0,8},{1,9},{2,10},{3,11},{4,12},{5,13},{6,14},{7,15},{8,0},{9,1},... | collective-permute-start | bytes 638984 | tf_op jit(solution)/shard_map/ppermute | solution.py:30
  196.0 20.6 %collective-permute-start.35 = (bf16[256,416]{1,0:T(8,128)(2,1)S(1)}, bf16[256,416]{1,0:T(8,128)(2,1)S(1)}, u32[]{:S(2)}, u32[]{:S(2)}) collective-permute-start(bf16[256,416]{1,0:T(8,128)(2,1)S(1)} %fusion.23), channel_id=1, source_target_pairs={{0,8},{1,9},{2,10},{3,11},{4,12},{5,13},{6,14},{7,15},{8,0},{9,1},... | collective-permute-start | bytes 638984 | tf_op jit(solution)/shard_map/ppermute | solution.py:30
  216.0 17.8 %collective-permute-start.13 = (bf16[128,1024]{1,0:T(8,128)(2,1)S(1)}, bf16[128,1024]{1,0:T(8,128)(2,1)S(1)}, u32[]{:S(2)}, u32[]{:S(2)}) collective-permute-start(bf16[128,1024]{1,0:T(8,128)(2,1)S(1)} %get-tuple-element.25), channel_id=1, source_target_pairs={{0,1},{1,0},{2,3},{3,2},{4,5},{5,4},{6,7},{7,6},{8,9},{9,8},{10,11... | collective-permute-start | bytes 786440 | tf_op jit(solution)/shard_map/ppermute | solution.py:25
  216.0 29.7 %collective-permute-start.12 = (bf16[128,1024]{1,0:T(8,128)(2,1)S(1)}, bf16[128,1024]{1,0:T(8,128)(2,1)S(1)}, u32[]{:S(2)}, u32[]{:S(2)}) collective-permute-start(bf16[128,1024]{1,0:T(8,128)(2,1)S(1)} %get-tuple-element.26), channel_id=1, source_target_pairs={{0,1},{1,0},{2,3},{3,2},{4,5},{5,4},{6,7},{7,6},{8,9},{9,8},{10,11... | collective-permute-start | bytes 786440 | tf_op jit(solution)/shard_map/ppermute | solution.py:25
  216.5 29.4 %collective-permute-start.16 = (bf16[128,1024]{1,0:T(8,128)(2,1)S(1)}, bf16[128,1024]{1,0:T(8,128)(2,1)S(1)}, u32[]{:S(2)}, u32[]{:S(2)}) collective-permute-start(bf16[128,1024]{1,0:T(8,128)(2,1)S(1)} %get-tuple-element.24), channel_id=1, source_target_pairs={{0,1},{1,0},{2,3},{3,2},{4,5},{5,4},{6,7},{7,6},{8,9},{9,8},{10,11... | collective-permute-start | bytes 786440 | tf_op jit(solution)/shard_map/ppermute | solution.py:25
  226.4 17.6 %collective-permute-start.38 = (bf16[128,1024]{1,0:T(8,128)(2,1)}, bf16[128,1024]{1,0:T(8,128)(2,1)}, u32[]{:S(2)}, u32[]{:S(2)}) collective-permute-start(bf16[128,1024]{1,0:T(8,128)(2,1)} %get-tuple-element.33), channel_id=1, source_target_pairs={{0,1},{1,0},{2,3},{3,2},{4,5},{5,4},{6,7},{7,6},{8,9},{9,8},{10,11... | collective-permute-start | bytes 786440 | tf_op jit(solution)/shard_map/ppermute | solution.py:25
  235.6 11.6 %copy-start.3 = (f32[4,256,1024]{2,1,0:T(8,128)S(1)}, f32[4,256,1024]{2,1,0:T(8,128)}, u32[]{:S(2)}) copy-start(f32[4,256,1024]{2,1,0:T(8,128)} %shard_map.86) | copy-start | bytes 12582916
  235.6 10.7 %collective-permute-start.14 = (bf16[128,1024]{1,0:T(8,128)(2,1)}, bf16[128,1024]{1,0:T(8,128)(2,1)}, u32[]{:S(2)}, u32[]{:S(2)}) collective-permute-start(bf16[128,1024]{1,0:T(8,128)(2,1)} %fusion.38), channel_id=1, source_target_pairs={{0,2},{1,3},{2,0},{3,1},{4,6},{5,7},{6,4},{7,5},{8,10},{9,11},{10,... | collective-permute-start | bytes 786440 | tf_op jit(solution)/shard_map/ppermute | solution.py:25
  244.0 12.8 %collective-permute-start.11 = (bf16[128,1024]{1,0:T(8,128)(2,1)S(1)}, bf16[128,1024]{1,0:T(8,128)(2,1)S(1)}, u32[]{:S(2)}, u32[]{:S(2)}) collective-permute-start(bf16[128,1024]{1,0:T(8,128)(2,1)S(1)} %get-tuple-element.19), channel_id=1, source_target_pairs={{0,1},{1,0},{2,3},{3,2},{4,5},{5,4},{6,7},{7,6},{8,9},{9,8},{10,11... | collective-permute-start | bytes 786440 | tf_op jit(solution)/shard_map/ppermute | solution.py:25
  244.1 12.9 %collective-permute-start.19 = (bf16[128,1024]{1,0:T(8,128)(2,1)S(1)}, bf16[128,1024]{1,0:T(8,128)(2,1)S(1)}, u32[]{:S(2)}, u32[]{:S(2)}) collective-permute-start(bf16[128,1024]{1,0:T(8,128)(2,1)S(1)} %get-tuple-element.22), channel_id=1, source_target_pairs={{0,1},{1,0},{2,3},{3,2},{4,5},{5,4},{6,7},{7,6},{8,9},{9,8},{10,11... | collective-permute-start | bytes 786440 | tf_op jit(solution)/shard_map/ppermute | solution.py:25
  245.7 2.6 collective-permute-start.37
  245.9 22.8 %copy-start.2 = (f32[4,256,1024]{2,1,0:T(8,128)S(1)}, f32[4,256,1024]{2,1,0:T(8,128)}, u32[]{:S(2)}) copy-start(f32[4,256,1024]{2,1,0:T(8,128)} %shard_map.89) | copy-start | bytes 12582916
  245.9 2.7 collective-permute-start.41
  246.3 8.3 %collective-permute-start.39 = (bf16[128,1024]{1,0:T(8,128)(2,1)S(1)}, bf16[128,1024]{1,0:T(8,128)(2,1)S(1)}, u32[]{:S(2)}, u32[]{:S(2)}) collective-permute-start(bf16[128,1024]{1,0:T(8,128)(2,1)S(1)} %fusion.14), channel_id=1, source_target_pairs={{0,2},{1,3},{2,0},{3,1},{4,6},{5,7},{6,4},{7,5},{8,10},{9,11},{10,... | collective-permute-start | bytes 786440 | tf_op jit(solution)/shard_map/ppermute | solution.py:25
  248.3 9.1 %collective-permute-start.22 = (bf16[128,1024]{1,0:T(8,128)(2,1)S(1)}, bf16[128,1024]{1,0:T(8,128)(2,1)S(1)}, u32[]{:S(2)}, u32[]{:S(2)}) collective-permute-start(bf16[128,1024]{1,0:T(8,128)(2,1)S(1)} %get-tuple-element.20), channel_id=1, source_target_pairs={{0,1},{1,0},{2,3},{3,2},{4,5},{5,4},{6,7},{7,6},{8,9},{9,8},{10,11... | collective-permute-start | bytes 786440 | tf_op jit(solution)/shard_map/ppermute | solution.py:25
  248.6 9.0 %collective-permute-start.15 = (bf16[128,1024]{1,0:T(8,128)(2,1)S(1)}, bf16[128,1024]{1,0:T(8,128)(2,1)S(1)}, u32[]{:S(2)}, u32[]{:S(2)}) collective-permute-start(bf16[128,1024]{1,0:T(8,128)(2,1)S(1)} %get-tuple-element.12), channel_id=1, source_target_pairs={{0,4},{1,5},{2,6},{3,7},{4,0},{5,1},{6,2},{7,3},{8,12},{9,13},{10,... | collective-permute-start | bytes 786440 | tf_op jit(solution)/shard_map/ppermute | solution.py:25
  254.6 7.5 %collective-permute-start.17 = (bf16[128,1024]{1,0:T(8,128)(2,1)S(1)}, bf16[128,1024]{1,0:T(8,128)(2,1)S(1)}, u32[]{:S(2)}, u32[]{:S(2)}) collective-permute-start(bf16[128,1024]{1,0:T(8,128)(2,1)S(1)} %get-tuple-element.13), channel_id=1, source_target_pairs={{0,2},{1,3},{2,0},{3,1},{4,6},{5,7},{6,4},{7,5},{8,10},{9,11},{10,... | collective-permute-start | bytes 786440 | tf_op jit(solution)/shard_map/ppermute | solution.py:25
  256.9 6.4 %collective-permute-start.36 = (bf16[128,1024]{1,0:T(8,128)(2,1)S(1)}, bf16[128,1024]{1,0:T(8,128)(2,1)S(1)}, u32[]{:S(2)}, u32[]{:S(2)}) collective-permute-start(bf16[128,1024]{1,0:T(8,128)(2,1)S(1)} %get-tuple-element.27), channel_id=1, source_target_pairs={{0,1},{1,0},{2,3},{3,2},{4,5},{5,4},{6,7},{7,6},{8,9},{9,8},{10,11... | collective-permute-start | bytes 786440 | tf_op jit(solution)/shard_map/ppermute | solution.py:25
  257.0 6.4 %collective-permute-start.44 = (bf16[128,1024]{1,0:T(8,128)(2,1)S(1)}, bf16[128,1024]{1,0:T(8,128)(2,1)S(1)}, u32[]{:S(2)}, u32[]{:S(2)}) collective-permute-start(bf16[128,1024]{1,0:T(8,128)(2,1)S(1)} %get-tuple-element.30), channel_id=1, source_target_pairs={{0,1},{1,0},{2,3},{3,2},{4,5},{5,4},{6,7},{7,6},{8,9},{9,8},{10,11... | collective-permute-start | bytes 786440 | tf_op jit(solution)/shard_map/ppermute | solution.py:25
  257.5 6.4 %collective-permute-start.47 = (bf16[128,1024]{1,0:T(8,128)(2,1)S(1)}, bf16[128,1024]{1,0:T(8,128)(2,1)S(1)}, u32[]{:S(2)}, u32[]{:S(2)}) collective-permute-start(bf16[128,1024]{1,0:T(8,128)(2,1)S(1)} %get-tuple-element.28), channel_id=1, source_target_pairs={{0,1},{1,0},{2,3},{3,2},{4,5},{5,4},{6,7},{7,6},{8,9},{9,8},{10,11... | collective-permute-start | bytes 786440 | tf_op jit(solution)/shard_map/ppermute | solution.py:25
  257.6 8.7 %collective-permute-start.40 = (bf16[128,1024]{1,0:T(8,128)(2,1)S(1)}, bf16[128,1024]{1,0:T(8,128)(2,1)S(1)}, u32[]{:S(2)}, u32[]{:S(2)}) collective-permute-start(bf16[128,1024]{1,0:T(8,128)(2,1)S(1)} %get-tuple-element.17), channel_id=1, source_target_pairs={{0,4},{1,5},{2,6},{3,7},{4,0},{5,1},{6,2},{7,3},{8,12},{9,13},{10,... | collective-permute-start | bytes 786440 | tf_op jit(solution)/shard_map/ppermute | solution.py:25
  262.1 6.5 %collective-permute-start.42 = (bf16[128,1024]{1,0:T(8,128)(2,1)S(1)}, bf16[128,1024]{1,0:T(8,128)(2,1)S(1)}, u32[]{:S(2)}, u32[]{:S(2)}) collective-permute-start(bf16[128,1024]{1,0:T(8,128)(2,1)S(1)} %get-tuple-element.18), channel_id=1, source_target_pairs={{0,2},{1,3},{2,0},{3,1},{4,6},{5,7},{6,4},{7,5},{8,10},{9,11},{10,... | collective-permute-start | bytes 786440 | tf_op jit(solution)/shard_map/ppermute | solution.py:25
  263.3 6.0 %collective-permute-start.21 = (bf16[128,1024]{1,0:T(8,128)(2,1)S(1)}, bf16[128,1024]{1,0:T(8,128)(2,1)S(1)}, u32[]{:S(2)}, u32[]{:S(2)}) collective-permute-start(bf16[128,1024]{1,0:T(8,128)(2,1)S(1)} %get-tuple-element.21), channel_id=1, source_target_pairs={{0,1},{1,0},{2,3},{3,2},{4,5},{5,4},{6,7},{7,6},{8,9},{9,8},{10,11... | collective-permute-start | bytes 786440 | tf_op jit(solution)/shard_map/ppermute | solution.py:25
  263.4 11.0 %collective-permute-start.46 = (bf16[128,1024]{1,0:T(8,128)(2,1)S(1)}, bf16[128,1024]{1,0:T(8,128)(2,1)S(1)}, u32[]{:S(2)}, u32[]{:S(2)}) collective-permute-start(bf16[128,1024]{1,0:T(8,128)(2,1)S(1)} %get-tuple-element.29), channel_id=1, source_target_pairs={{0,1},{1,0},{2,3},{3,2},{4,5},{5,4},{6,7},{7,6},{8,9},{9,8},{10,11... | collective-permute-start | bytes 786440 | tf_op jit(solution)/shard_map/ppermute | solution.py:25
  263.9 9.2 %collective-permute-start.23 = (bf16[128,1024]{1,0:T(8,128)(2,1)S(1)}, bf16[128,1024]{1,0:T(8,128)(2,1)S(1)}, u32[]{:S(2)}, u32[]{:S(2)}) collective-permute-start(bf16[128,1024]{1,0:T(8,128)(2,1)S(1)} %get-tuple-element.10), channel_id=1, source_target_pairs={{0,4},{1,5},{2,6},{3,7},{4,0},{5,1},{6,2},{7,3},{8,12},{9,13},{10,... | collective-permute-start | bytes 786440 | tf_op jit(solution)/shard_map/ppermute | solution.py:25
  268.7 21.6 %copy-start.1 = (f32[52,128]{1,0:T(8,128)S(1)}, f32[52,128]{1,0:T(8,128)}, u32[]{:S(2)}) copy-start(f32[52,128]{1,0:T(8,128)} %param.15) | copy-start | bytes 79876
  269.0 9.7 %collective-permute-start.48 = (bf16[128,1024]{1,0:T(8,128)(2,1)S(1)}, bf16[128,1024]{1,0:T(8,128)(2,1)S(1)}, u32[]{:S(2)}, u32[]{:S(2)}) collective-permute-start(bf16[128,1024]{1,0:T(8,128)(2,1)S(1)} %get-tuple-element.15), channel_id=1, source_target_pairs={{0,4},{1,5},{2,6},{3,7},{4,0},{5,1},{6,2},{7,3},{8,12},{9,13},{10,... | collective-permute-start | bytes 786440 | tf_op jit(solution)/shard_map/ppermute | solution.py:25
  269.3 9.5 %collective-permute-start.18 = (bf16[128,1024]{1,0:T(8,128)(2,1)S(1)}, bf16[128,1024]{1,0:T(8,128)(2,1)S(1)}, u32[]{:S(2)}, u32[]{:S(2)}) collective-permute-start(bf16[128,1024]{1,0:T(8,128)(2,1)S(1)} %get-tuple-element.23), channel_id=1, source_target_pairs={{0,1},{1,0},{2,3},{3,2},{4,5},{5,4},{6,7},{7,6},{8,9},{9,8},{10,11... | collective-permute-start | bytes 786440 | tf_op jit(solution)/shard_map/ppermute | solution.py:25
  269.3 15.0 %collective-permute-start.20 = (bf16[128,1024]{1,0:T(8,128)(2,1)S(1)}, bf16[128,1024]{1,0:T(8,128)(2,1)S(1)}, u32[]{:S(2)}, u32[]{:S(2)}) collective-permute-start(bf16[128,1024]{1,0:T(8,128)(2,1)S(1)} %get-tuple-element.11), channel_id=1, source_target_pairs={{0,4},{1,5},{2,6},{3,7},{4,0},{5,1},{6,2},{7,3},{8,12},{9,13},{10,... | collective-permute-start | bytes 786440 | tf_op jit(solution)/shard_map/ppermute | solution.py:25
  273.2 11.1 %collective-permute-start.24 = (bf16[128,1024]{1,0:T(8,128)(2,1)S(1)}, bf16[128,1024]{1,0:T(8,128)(2,1)S(1)}, u32[]{:S(2)}, u32[]{:S(2)}) collective-permute-start(bf16[128,1024]{1,0:T(8,128)(2,1)S(1)} %fusion.28), channel_id=1, source_target_pairs={{0,2},{1,3},{2,0},{3,1},{4,6},{5,7},{6,4},{7,5},{8,10},{9,11},{10,... | collective-permute-start | bytes 786440 | tf_op jit(solution)/shard_map/ppermute | solution.py:25
  274.5 10.0 %collective-permute-start.43 = (bf16[128,1024]{1,0:T(8,128)(2,1)S(1)}, bf16[128,1024]{1,0:T(8,128)(2,1)S(1)}, u32[]{:S(2)}, u32[]{:S(2)}) collective-permute-start(bf16[128,1024]{1,0:T(8,128)(2,1)S(1)} %get-tuple-element.31), channel_id=1, source_target_pairs={{0,1},{1,0},{2,3},{3,2},{4,5},{5,4},{6,7},{7,6},{8,9},{9,8},{10,11... | collective-permute-start | bytes 786440 | tf_op jit(solution)/shard_map/ppermute | solution.py:25
  278.7 10.4 %collective-permute-start.45 = (bf16[128,1024]{1,0:T(8,128)(2,1)S(1)}, bf16[128,1024]{1,0:T(8,128)(2,1)S(1)}, u32[]{:S(2)}, u32[]{:S(2)}) collective-permute-start(bf16[128,1024]{1,0:T(8,128)(2,1)S(1)} %get-tuple-element.16), channel_id=1, source_target_pairs={{0,4},{1,5},{2,6},{3,7},{4,0},{5,1},{6,2},{7,3},{8,12},{9,13},{10,... | collective-permute-start | bytes 786440 | tf_op jit(solution)/shard_map/ppermute | solution.py:25
  278.9 10.2 %collective-permute-start.49 = (bf16[128,1024]{1,0:T(8,128)(2,1)S(1)}, bf16[128,1024]{1,0:T(8,128)(2,1)S(1)}, u32[]{:S(2)}, u32[]{:S(2)}) collective-permute-start(bf16[128,1024]{1,0:T(8,128)(2,1)S(1)} %fusion.4), channel_id=1, source_target_pairs={{0,2},{1,3},{2,0},{3,1},{4,6},{5,7},{6,4},{7,5},{8,10},{9,11},{10,... | collective-permute-start | bytes 786440 | tf_op jit(solution)/shard_map/ppermute | solution.py:25
  (4 other events, 3.3 us)

commit v3 on v2

v3 whole, which is shorter than its diff:
```python
import math

import jax
import jax.numpy as jnp
from jax import lax
from jax.experimental import pallas as pl
from jax.experimental.pallas import tpu as pltpu
from jax.sharding import PartitionSpec as P

BLK = 128
RO = 8
CHUNKS = 2
VMEM_BYTES = 56 * 2**20
GATHER_MASKS = (0, 1, 4, 5, 2, 3, 6, 7)
SENT_MASKS = (7, 5, 3, 1)
KEPT_MASKS = (6, 4, 2, 0)


def partner(shard, mask):
    return lax.ppermute(shard, "gx", [(i, i ^ mask) for i in range(lax.axis_size("gx"))])


def from_behind(shard, by):
    devices = lax.axis_size("gx")
    return lax.ppermute(shard, "gx", [(i, (i + by) % devices) for i in range(devices)])


def params():
    return pltpu.CompilerParams(vmem_limit_bytes=VMEM_BYTES)


def cost(flops, moved):
    return pl.CostEstimate(flops=int(flops), bytes_accessed=int(moved), transcendentals=0)


def scale_tokens(tokens, token_scale):
    count, width = tokens.shape
    rows = count // CHUNKS

    def kernel(x_ref, s_ref, *out_refs):
        factors = s_ref[...].T
        for chunk, out_ref in enumerate(out_refs):
            span = slice(chunk * rows, (chunk + 1) * rows)
            for block in range(width // BLK):
                columns = pl.ds(block * BLK, BLK)
                value = x_ref[span, columns].astype(jnp.float32)
                out_ref[:, columns] = (value * factors[span, block : block + 1]).astype(
                    jnp.bfloat16
                )

    return pl.pallas_call(
        kernel,
        out_shape=[jax.ShapeDtypeStruct((rows, width), jnp.bfloat16)] * CHUNKS,
        compiler_params=params(),
        cost_estimate=cost(count * width, 4 * count * width),
    )(tokens, token_scale.T)


def scale_rows(weights, factors, unit):
    height, width = weights[0].shape
    columns = width // RO
    many = len(weights)

    def kernel(*refs):
        out_ref = refs[-1]
        for index in range(many):
            w_ref, f_ref = refs[index], refs[many + index]
            for group in range(height // unit):
                span = pl.ds(group * unit, unit)
                value = w_ref[span, :].astype(jnp.float32) * f_ref[group : group + 1, :]
                out_ref[0, pl.ds(index * height + group * unit, unit), :] = value.astype(
                    jnp.bfloat16
                )

    return pl.pallas_call(
        kernel,
        grid=(RO,),
        in_specs=[pl.BlockSpec((height, columns), lambda i: (0, i))] * many
        + [pl.BlockSpec((height // unit, columns), lambda i: (0, i))] * many,
        out_specs=pl.BlockSpec((1, many * height, columns), lambda i: (i, 0, 0)),
        out_shape=jax.ShapeDtypeStruct((RO, many * height, columns), jnp.bfloat16),
        compiler_params=params(),
        cost_estimate=cost(many * height * width, 4 * many * height * width),
    )(*weights, *factors)


def joined_product(slot, blocks, joined):
    width = blocks[0].shape[1]
    rows = blocks[0].shape[0]
    height = joined.shape[1]
    flat = []
    places = []
    for block in blocks:
        parts = block if isinstance(block, tuple) else (block,)
        places.append(tuple(range(len(flat), len(flat) + len(parts))))
        flat.extend(parts)

    def mask_of(step):
        mask = step * 0
        for index, value in enumerate(GATHER_MASKS):
            mask = jnp.where(step == index, value, mask)
        return mask

    def kernel(slot_ref, *refs):
        x_refs, w_ref, out_ref = refs[: len(flat)], refs[len(flat)], refs[len(flat) + 1]
        step = pl.program_id(0)
        for index, place in enumerate(places):

            @pl.when(step == index)
            def _():
                parts = [x_refs[p][...] for p in place]
                x = parts[0] if len(parts) == 1 else jnp.concatenate(parts, 0)
                value = lax.dot_general(
                    w_ref[0], x, (((1,), (1,)), ((), ())), preferred_element_type=jnp.float32
                )
                if index == 0:
                    out_ref[...] = value
                else:
                    out_ref[...] += value

    return pl.pallas_call(
        kernel,
        grid_spec=pltpu.PrefetchScalarGridSpec(
            num_scalar_prefetch=1,
            grid=(len(places),),
            in_specs=[pl.BlockSpec(b.shape, lambda i, s: (0, 0)) for b in flat]
            + [pl.BlockSpec((1, height, width), lambda i, s: (s[0] ^ mask_of(i), 0, 0))],
            out_specs=pl.BlockSpec((height, rows), lambda i, s: (0, 0)),
        ),
        out_shape=jax.ShapeDtypeStruct((height, rows), jnp.float32),
        compiler_params=params(),
        cost_estimate=cost(2 * rows * width * RO * height, 2 * width * RO * height),
    )(slot, *flat, joined)


def output_product(slot, hidden, down, masks, kind):
    depth, rows = hidden.shape
    width = down.shape[2]

    def mask_of(step):
        return masks[0] - 2 * step

    def kernel(slot_ref, x_ref, w_ref, out_ref, turned):
        @pl.when(pl.program_id(0) == 0)
        def _():
            turned[...] = x_ref[...].T

        out_ref[0] = jnp.dot(
            turned[...], w_ref[0], preferred_element_type=jnp.float32
        ).astype(kind)

    return pl.pallas_call(
        kernel,
        grid_spec=pltpu.PrefetchScalarGridSpec(
            num_scalar_prefetch=1,
            grid=(len(masks),),
            in_specs=[
                pl.BlockSpec((depth, rows), lambda i, s: (0, 0)),
                pl.BlockSpec((1, depth, width), lambda i, s: (s[0] ^ mask_of(i), 0, 0)),
            ],
            out_specs=pl.BlockSpec((1, rows, width), lambda i, s: (i, 0, 0)),
            scratch_shapes=[pltpu.VMEM((rows, depth), jnp.bfloat16)],
        ),
        out_shape=jax.ShapeDtypeStruct((len(masks), rows, width), kind),
        compiler_params=params(),
        cost_estimate=cost(
            2 * rows * depth * len(masks) * width, 2 * depth * len(masks) * width
        ),
    )(slot, hidden, down)


def tie(*values):
    return lax.optimization_barrier(values)


def scatter_sum(sent, kept):
    half = sent.shape[1] // 2

    def summed(index, part):
        span = slice(part * half, (part + 1) * half)
        return kept[index, span] + partner(sent[index, span], 1).astype(jnp.float32)

    def send(value, mask):
        return partner(value.astype(jnp.bfloat16), mask).astype(jnp.float32)

    diagonal_a = send(summed(0, 0), 2)
    diagonal_b = send(summed(0, 1), 4)
    far_b = send(summed(1, 1), 4)
    near_a = send(summed(2, 0), 2)
    far_a = send(summed(1, 0) + diagonal_a, 4)
    near_b = send(summed(2, 1) + diagonal_b, 2)
    return [
        (summed(3, 0) + far_a + near_a).astype(jnp.bfloat16),
        (summed(3, 1) + far_b + near_b).astype(jnp.bfloat16),
    ]


def body(tokens, token_scale, gate_tiles, up_tiles, gate_scale, up_scale, down_tiles, down_scale):
    position = lax.axis_index("gx")
    devices = lax.axis_size("gx")
    row_groups = devices // RO
    col_slot = position % RO
    row_slot = position // RO
    slot = col_slot.astype(jnp.int32).reshape(1)
    token_count = tokens.shape[0]
    tile_rows = gate_tiles.shape[1]
    tile_cols = gate_tiles.shape[2]
    piece_cols = tile_cols // row_groups
    unit = math.gcd(tile_cols, BLK)
    units = tile_cols // unit

    first_block = row_slot * (tile_rows // BLK)

    def spread(blocks):
        columns = lax.dynamic_slice_in_dim(blocks, first_block, tile_rows // BLK, 1)
        fine = jnp.repeat(columns, BLK // unit, 0)
        fine = lax.dynamic_slice_in_dim(fine, col_slot * units, units, 0)
        return jnp.repeat(fine, BLK, 1)

    own_a, own_b = scale_tokens(tokens, token_scale)
    rows = token_count // CHUNKS
    half = rows // 2
    far_a, near_a = partner(own_a, 4), partner(own_a, 2)
    pair_a = partner(own_a, 1)
    far_b, near_b = partner(own_b, 4), partner(own_b, 2)
    pair_b = partner(own_b, 1)
    joined = scale_rows(
        (gate_tiles[0].T, up_tiles[0].T), (spread(gate_scale.T), spread(up_scale.T)), unit
    )
    far_a, near_a, pair_a, joined = tie(far_a, near_a, pair_a, joined)
    diagonal_a = partner(far_a[:half], 2), partner(near_a[half:], 4)
    far_pair_a, near_pair_a = partner(far_a, 1), partner(near_a, 1)
    down_eff = scale_rows((down_tiles[0],), (spread(down_scale),), unit)
    *diagonal_a, far_b, near_b, pair_b, down_eff = tie(
        *diagonal_a, far_b, near_b, pair_b, down_eff
    )

    def product(own, pair, far, far_pair, near, near_pair, diagonal):
        last = tuple(partner(part, 1) for part in diagonal)
        blocks = [own, pair, far, far_pair, near, near_pair, tuple(diagonal), last]
        return joined_product(slot, blocks, joined)

    def share(partial_value, target):
        start = target * piece_cols
        return jnp.stack(
            (
                lax.dynamic_slice_in_dim(partial_value, start, piece_cols, 0),
                lax.dynamic_slice_in_dim(partial_value, tile_cols + start, piece_cols, 0),
            ),
            0,
        )

    def first_share(partial_value):
        return share(partial_value, (row_slot - 1) % row_groups).astype(jnp.bfloat16)

    def hidden_of(sent, partial_value):
        summed = sent
        for step in range(1, row_groups):
            summed = from_behind(summed.astype(jnp.bfloat16), RO).astype(jnp.float32)
            summed = summed + share(partial_value, (row_slot - 1 - step) % row_groups)
        return (jax.nn.silu(summed[0]) * summed[1]).astype(jnp.bfloat16)

    def spread_hidden(piece):
        if row_groups == 2:
            other = from_behind(piece, RO)
            return jnp.where(
                row_slot == 0,
                jnp.concatenate((piece, other), 0),
                jnp.concatenate((other, piece), 0),
            )
        full = jnp.zeros((tile_cols, rows), jnp.bfloat16)
        current = piece
        for step in range(row_groups):
            if step:
                current = from_behind(current, RO)
            source = (row_slot - step) % row_groups
            full = lax.dynamic_update_slice_in_dim(full, current, source * piece_cols, 0)
        return full

    def output(hidden):
        sent = output_product(slot, hidden, down_eff, SENT_MASKS, jnp.bfloat16)
        kept = output_product(slot, hidden, down_eff, KEPT_MASKS, jnp.float32)
        return scatter_sum(sent, kept)

    partial_a = product(own_a, pair_a, far_a, far_pair_a, near_a, near_pair_a, diagonal_a)
    sent_a = first_share(partial_a)
    diagonal_b = partner(far_b[:half], 2), partner(near_b[half:], 4)
    far_pair_b, near_pair_b = partner(far_b, 1), partner(near_b, 1)
    *diagonal_b, partial_a = tie(*diagonal_b, partial_a)
    partial_b = product(own_b, pair_b, far_b, far_pair_b, near_b, near_pair_b, diagonal_b)
    piece_a = hidden_of(sent_a, partial_a)
    sent_b = first_share(partial_b)
    piece_a, sent_b = tie(piece_a, sent_b)
    piece_b = hidden_of(sent_b, partial_b)
    out_a = output(spread_hidden(piece_a))
    out_b = output(spread_hidden(piece_b))
    return jnp.concatenate(out_a + out_b, 0)


def solution(mesh):
    return jax.shard_map(
        body,
        mesh=mesh,
        in_specs=(
            P("groups", "gx"),
            P("groups", "gx"),
            P("gx", None, None),
            P("gx", None, None),
            P(),
            P(),
            P("gx", None, None),
            P(),
        ),
        out_specs=P("groups", "gx"),
        check_vma=False,
    )
```

time: 292 us -> 217 us (0.74)
  local copies, waits for them, and re-layouts: 56 us -> 15.2 us
  waiting for transfers between devices: 95.2 us -> 65.3 us
    unnamed x41 -> x44, local copies, waits for them, and re-layouts: 43.1 us -> 6.13 us
    ppermute x4, waiting for transfers between devices: 39.9 us -> 21.7 us  [from_behind(): lax.ppermute(shard, 'gx', [(i, (i + by) % devices) for i in range(devices)])]
    ppermute x46, waiting for transfers between devices: 55.3 us -> 43.6 us  [partner(): lax.ppermute(shard, 'gx', [(i, i ^ mask) for i in range(lax.axis_size('gx...]
    ppermute x46, starting transfers between devices: 25.6 us -> 22.4 us  [partner(): lax.ppermute(shard, 'gx', [(i, i ^ mask) for i in range(lax.axis_size('gx...]
  transfers between devices with their start and end apart: 50 -> 50, of which waited for: 15 -> 14; matrix products, arithmetic and copies ran while one was open for 21% -> 10% of each run, Pallas kernels for 33% -> 43%
where the time goes in v3:
time: 217 us; the launch traced here: 216 us
  Pallas kernels  96.2 us (44%)
  waiting for transfers between devices  65.3 us (30%)
  starting transfers between devices  28.5 us (13%)
  local copies, waits for them, and re-layouts  15.2 us (7%)
  other arithmetic  10.4 us (5%)
    ppermute x46, waiting for transfers between devices, partner(): lax.ppermute(shard, 'gx', [(i, i ^ mask) for i in range(lax.axis_size('gx...  43.6 us
    pallas_call x2, Pallas kernels, scale_rows(): pl.pallas_call(kernel, grid=(RO,), in_specs=[pl.BlockSpec((height, column...  33.5 us
    pallas_call x2, Pallas kernels, joined_product(): pl.pallas_call(kernel, grid_spec=pltpu.PrefetchScalarGridSpec(num_scalar_...  32.8 us
    pallas_call x4, Pallas kernels, output_product(): pl.pallas_call(kernel, grid_spec=pltpu.PrefetchScalarGridSpec(num_scalar_...  27 us
    ppermute x46, starting transfers between devices, partner(): lax.ppermute(shard, 'gx', [(i, i ^ mask) for i in range(lax.axis_size('gx...  22.4 us
    ppermute x4, waiting for transfers between devices, from_behind(): lax.ppermute(shard, 'gx', [(i, (i + by) % devices) for i in range(devices)])  21.7 us
    unnamed x44, local copies, waits for them, and re-layouts  6.13 us
    ppermute x4, starting transfers between devices, from_behind(): lax.ppermute(shard, 'gx', [(i, (i + by) % devices) for i in range(devices)])  6.12 us
  transfers between devices with their start and end apart: 50, of which 14 were waited for; matrix products, arithmetic and copies ran while one was open for 10% of the time, Pallas kernels for 43%

profile of v3, /device:TPU:0, one launch (start us, length us, event | category | flops | bytes accessed | tf_op | source)
XLA Modules:
  0.0 216.1 jit_solution(10470231672369983907)
XLA Ops:
  0.0 2.9 %shard_map.82 = (bf16[256,1024]{1,0:T(8,128)(2,1)}, bf16[256,1024]{1,0:T(8,128)(2,1)}) custom-call(bf16[512,1024]{1,0:T(8,128)(2,1)} %x_ref.1, f32[8,512]{1,0:T(8,128)} %bitcast.225), custom_call_target="tpu_custom_call" | custom-call | flops 524288 | bytes 2097152 | tf_op jit(solution)/shard_map/pallas_call | solution.py:51
  2.9 3.0 %collective-permute-start = (bf16[256,1024]{1,0:T(8,128)(2,1)}, bf16[256,1024]{1,0:T(8,128)(2,1)S(1)}, u32[]{:S(2)}, u32[]{:S(2)}) collective-permute-start(bf16[256,1024]{1,0:T(8,128)(2,1)} %get-tuple-element.22.refs_0_), channel_id=1, source_target_pairs={{0,4},{1,5},{2,6},{3,7},{4,0},{5,1},{6,2},{7,3},{8,12},{9,13},{10,... | collective-permute-start | bytes 1572872 | tf_op jit(solution)/shard_map/ppermute | solution.py:20
  5.9 1.5 collective-permute-start.1
  7.4 0.4 collective-permute-start.7
  8.0 10.9 %collective-permute-done.refs_2_ = bf16[256,1024]{1,0:T(8,128)(2,1)S(1)} collective-permute-done((bf16[256,1024]{1,0:T(8,128)(2,1)}, bf16[256,1024]{1,0:T(8,128)(2,1)S(1)}, u32[]{:S(2)}, u32[]{:S(2)}) %collective-permute-start) | collective-permute-done | bytes 524320 | tf_op jit(solution)/shard_map/ppermute | solution.py:20
  18.9 0.9 dynamic-slice_bitcast_fusion.4
  20.1 1.1 copy.9
  21.4 1.1 copy.10
  22.5 20.9 %shard_map.83.refs_10_ = bf16[8,1664,1024]{2,1,0:T(8,128)(2,1)} custom-call(bf16[832,8192]{1,0:T(8,128)(2,1)} %bitcast.214, bf16[832,8192]{1,0:T(8,128)(2,1)} %bitcast.215, f32[13,8192]{1,0:T(8,128)} %bitcast.216, f32[13,8192]{1,0:T(8,128)} %bitcast.217), custom_call_target="tpu_custom_call" | custom-call | flops 13631488 | bytes 54525952 | tf_op jit(solution)/shard_map/pallas_call | solution.py:75
  43.5 2.1 collective-permute-start.5
  45.6 1.6 collective-permute-start.6
  47.3 0.5 collective-permute-start.4
  48.1 1.1 copy.11
  49.3 12.6 %shard_map.84.w_ref = bf16[8,832,1024]{2,1,0:T(8,128)(2,1)} custom-call(bf16[832,8192]{1,0:T(8,128)(2,1)} %bitcast.213, f32[13,8192]{1,0:T(8,128)} %bitcast.218), custom_call_target="tpu_custom_call" | custom-call | flops 6815744 | bytes 27262976 | tf_op jit(solution)/shard_map/pallas_call | solution.py:75
  62.7 0.9 collective-permute-done.10.refs_8_
  63.8 0.4 collective-permute-done.11.refs_9_
  64.2 0.5 collective-permute-start.13
  64.8 16.4 %shard_map.85 = f32[1664,256]{1,0:T(8,128)} custom-call(s32[1]{0:T(128)} %bitcast.slot_ref, bf16[256,1024]{1,0:T(8,128)(2,1)} %get-tuple-element.22.refs_0_, bf16[256,1024]{1,0:T(8,128)(2,1)} %copy-done.10, bf16[256,1024]{1,0:T(8,128)(2,1)} %copy-done.8, bf16[256,1024]{1,0:T(8,128)(2,1)} %collective-permute-done.3.refs_3_, bf16[256,1024]{1,0:T(8,128)(2,1)} %copy-done.9, ...), custom_call_target="tpu_custom_call" | custom-call | flops 6979321856 | bytes 27262976 | tf_op jit(solution)/shard_map/pallas_call | solution.py:121
  81.3 0.5 collective-permute-start.18
  81.8 1.2 fusion.48
  83.1 3.1 %collective-permute-start.12 = (bf16[2,416,256]{2,1,0:T(8,128)(2,1)S(1)}, bf16[2,416,256]{2,1,0:T(8,128)(2,1)S(1)}, u32[]{:S(2)}, u32[]{:S(2)}) collective-permute-start(bf16[2,416,256]{2,1,0:T(8,128)(2,1)S(1)} %pad_maximum_fusion.1), channel_id=1, source_target_pairs={{0,8},{1,9},{2,10},{3,11},{4,12},{5,13},{6,14},{7,15},{8,0},{9,1},... | collective-permute-start | bytes 1277960 | tf_op jit(solution)/shard_map/ppermute | solution.py:25
  86.1 1.2 dynamic-slice_bitcast_fusion.3
  87.4 0.6 copy-done.17
  88.3 0.8 copy-done.13
  89.1 16.4 %shard_map.86 = f32[1664,256]{1,0:T(8,128)} custom-call(s32[1]{0:T(128)} %bitcast.slot_ref, bf16[256,1024]{1,0:T(8,128)(2,1)} %get-tuple-element.26.refs_0_, bf16[256,1024]{1,0:T(8,128)(2,1)} %copy-done.11, bf16[256,1024]{1,0:T(8,128)(2,1)} %copy-done.6, bf16[256,1024]{1,0:T(8,128)(2,1)} %copy-done.12, bf16[256,1024]{1,0:T(8,128)(2,1)} %copy-done.7, ...), custom_call_target="tpu_custom_call" | custom-call | flops 6979321856 | bytes 27262976 | tf_op jit(solution)/shard_map/pallas_call | solution.py:121
  105.5 1.3 fusion.50
  107.2 2.9 %collective-permute-start.34 = (bf16[2,416,256]{2,1,0:T(8,128)(2,1)S(1)}, bf16[2,416,256]{2,1,0:T(8,128)(2,1)S(1)}, u32[]{:S(2)}, u32[]{:S(2)}) collective-permute-start(bf16[2,416,256]{2,1,0:T(8,128)(2,1)S(1)} %pad_maximum_fusion.2), channel_id=1, source_target_pairs={{0,8},{1,9},{2,10},{3,11},{4,12},{5,13},{6,14},{7,15},{8,0},{9,1},... | collective-permute-start | bytes 1277960 | tf_op jit(solution)/shard_map/ppermute | solution.py:25
  110.1 19.7 %collective-permute-done.19 = bf16[416,256]{1,0:T(8,128)(2,1)S(1)} collective-permute-done((bf16[416,256]{1,0:T(8,128)(2,1)S(1)}, bf16[416,256]{1,0:T(8,128)(2,1)S(1)}, u32[]{:S(2)}, u32[]{:S(2)}) %collective-permute-start.19) | collective-permute-done | bytes 213024 | tf_op jit(solution)/shard_map/ppermute | solution.py:25
  129.8 0.9 maximum_select_fusion.x_ref
  130.8 6.4 %shard_map.88 = bf16[4,256,1024]{2,1,0:T(8,128)(2,1)} custom-call(s32[1]{0:T(128)} %bitcast.slot_ref, bf16[832,256]{1,0:T(8,128)(2,1)} %maximum_select_fusion.x_ref, bf16[8,832,1024]{2,1,0:T(8,128)(2,1)} %shard_map.84.w_ref), custom_call_target="tpu_custom_call" | custom-call | flops 1744830464 | bytes 6815744 | tf_op jit(solution)/shard_map/pallas_call | solution.py:152
  137.2 0.6 collective-permute-done.34
  138.1 0.7 copy-done.4
  138.8 1.0 slice_bitcast_fusion.35
  139.8 0.5 collective-permute-start.21
  140.4 0.5 collective-permute-start.20
  140.9 7.1 %shard_map.87 = f32[4,256,1024]{2,1,0:T(8,128)} custom-call(s32[1]{0:T(128)} %bitcast.slot_ref, bf16[832,256]{1,0:T(8,128)(2,1)} %maximum_select_fusion.x_ref, bf16[8,832,1024]{2,1,0:T(8,128)(2,1)} %shard_map.84.w_ref), custom_call_target="tpu_custom_call" | custom-call | flops 1744830464 | bytes 6815744 | tf_op jit(solution)/shard_map/pallas_call | solution.py:152
  147.9 1.4 collective-permute-done.35
  149.3 0.9 maximum_select_fusion.1.x_ref
  150.3 6.4 %shard_map.90 = bf16[4,256,1024]{2,1,0:T(8,128)(2,1)} custom-call(s32[1]{0:T(128)} %bitcast.slot_ref, bf16[832,256]{1,0:T(8,128)(2,1)} %maximum_select_fusion.1.x_ref, bf16[8,832,1024]{2,1,0:T(8,128)(2,1)} %shard_map.84.w_ref), custom_call_target="tpu_custom_call" | custom-call | flops 1744830464 | bytes 6815744 | tf_op jit(solution)/shard_map/pallas_call | solution.py:152
  156.7 2.6 %slice_bitcast_fusion.27 = (bf16[128,1024]{1,0:T(8,128)(2,1)S(1)}, bf16[128,1024]{1,0:T(8,128)(2,1)S(1)}, bf16[128,1024]{1,0:T(8,128)(2,1)S(1)}, bf16[128,1024]{...) fusion(bf16[4,256,1024]{2,1,0:T(8,128)(2,1)} %shard_map.90), kind=kLoop, calls=%fused_computation.90 | loop fusion | bytes 4194304 | tf_op jit(solution)/shard_map/squeeze | solution.py:181
  159.6 1.7 fusion.36
  161.4 1.6 collective-permute-start.23
  163.0 7.1 %shard_map.89 = f32[4,256,1024]{2,1,0:T(8,128)} custom-call(s32[1]{0:T(128)} %bitcast.slot_ref, bf16[832,256]{1,0:T(8,128)(2,1)} %maximum_select_fusion.1.x_ref, bf16[8,832,1024]{2,1,0:T(8,128)(2,1)} %shard_map.84.w_ref), custom_call_target="tpu_custom_call" | custom-call | flops 1744830464 | bytes 6815744 | tf_op jit(solution)/shard_map/pallas_call | solution.py:152
  170.0 1.2 fusion.14
  171.2 0.6 collective-permute-start.37
  171.9 0.4 collective-permute-start.39
  172.3 1.4 fusion.39
  174.0 6.5 %collective-permute-done.39 = bf16[128,1024]{1,0:T(8,128)(2,1)S(1)} collective-permute-done((bf16[128,1024]{1,0:T(8,128)(2,1)S(1)}, bf16[128,1024]{1,0:T(8,128)(2,1)S(1)}, u32[]{:S(2)}, u32[]{:S(2)}) %collective-permute-start.39) | collective-permute-done | bytes 262176 | tf_op jit(solution)/shard_map/ppermute | solution.py:20
  180.5 0.4 collective-permute-start.26
  180.9 1.4 fusion.17
  182.5 0.5 collective-permute-start.44
  183.0 5.3 %collective-permute-done.26 = bf16[128,1024]{1,0:T(8,128)(2,1)S(1)} collective-permute-done((bf16[128,1024]{1,0:T(8,128)(2,1)S(1)}, bf16[128,1024]{1,0:T(8,128)(2,1)S(1)}, u32[]{:S(2)}, u32[]{:S(2)}) %collective-permute-start.26) | collective-permute-done | bytes 262176 | tf_op jit(solution)/shard_map/ppermute | solution.py:20
  188.4 0.4 collective-permute-start.42
  189.3 0.5 collective-permute-start.46
  189.8 1.9 collective-permute-done.40
  191.7 3.6 %collective-permute-done.42 = bf16[128,1024]{1,0:T(8,128)(2,1)S(1)} collective-permute-done((bf16[128,1024]{1,0:T(8,128)(2,1)S(1)}, bf16[128,1024]{1,0:T(8,128)(2,1)S(1)}, u32[]{:S(2)}, u32[]{:S(2)}) %collective-permute-start.42) | collective-permute-done | bytes 262176 | tf_op jit(solution)/shard_map/ppermute | solution.py:20
  195.8 1.9 collective-permute-start.29
  197.8 1.2 collective-permute-done.32
  199.0 1.7 collective-permute-start.33
  200.7 4.3 %collective-permute-done.48 = bf16[128,1024]{1,0:T(8,128)(2,1)S(1)} collective-permute-done((bf16[128,1024]{1,0:T(8,128)(2,1)S(1)}, bf16[128,1024]{1,0:T(8,128)(2,1)S(1)}, u32[]{:S(2)}, u32[]{:S(2)}) %collective-permute-start.48) | collective-permute-done | bytes 262176 | tf_op jit(solution)/shard_map/ppermute | solution.py:20
  205.1 1.2 collective-permute-start.49
  206.3 4.3 %collective-permute-done.29 = bf16[128,1024]{1,0:T(8,128)(2,1)S(1)} collective-permute-done((bf16[128,1024]{1,0:T(8,128)(2,1)S(1)}, bf16[128,1024]{1,0:T(8,128)(2,1)S(1)}, u32[]{:S(2)}, u32[]{:S(2)}) %collective-permute-start.29) | collective-permute-done | bytes 262176 | tf_op jit(solution)/shard_map/ppermute | solution.py:20
  210.8 4.1 %collective-permute-done.45 = bf16[128,1024]{1,0:T(8,128)(2,1)S(1)} collective-permute-done((bf16[128,1024]{1,0:T(8,128)(2,1)S(1)}, bf16[128,1024]{1,0:T(8,128)(2,1)S(1)}, u32[]{:S(2)}, u32[]{:S(2)}) %collective-permute-start.45) | collective-permute-done | bytes 262176 | tf_op jit(solution)/shard_map/ppermute | solution.py:20
  215.1 1.0 pad_maximum_fusion
  (129 shorter events, 5.4 us)
Async XLA Ops:
  0.0 47.8 %copy-start = (f32[52,128]{1,0:T(8,128)S(1)}, f32[52,128]{1,0:T(8,128)}, u32[]{:S(2)}) copy-start(f32[52,128]{1,0:T(8,128)} %param.15) | copy-start | bytes 79876
  2.9 16.0 %collective-permute-start = (bf16[256,1024]{1,0:T(8,128)(2,1)}, bf16[256,1024]{1,0:T(8,128)(2,1)S(1)}, u32[]{:S(2)}, u32[]{:S(2)}) collective-permute-start(bf16[256,1024]{1,0:T(8,128)(2,1)} %get-tuple-element.22.refs_0_), channel_id=1, source_target_pairs={{0,4},{1,5},{2,6},{3,7},{4,0},{5,1},{6,2},{7,3},{8,12},{9,13},{10,... | collective-permute-start | bytes 1572872 | tf_op jit(solution)/shard_map/ppermute | solution.py:20
  5.9 37.5 %collective-permute-start.1 = (bf16[256,1024]{1,0:T(8,128)(2,1)}, bf16[256,1024]{1,0:T(8,128)(2,1)S(1)}, u32[]{:S(2)}, u32[]{:S(2)}) collective-permute-start(bf16[256,1024]{1,0:T(8,128)(2,1)} %get-tuple-element.22.refs_0_), channel_id=1, source_target_pairs={{0,2},{1,3},{2,0},{3,1},{4,6},{5,7},{6,4},{7,5},{8,10},{9,11},{10,... | collective-permute-start | bytes 1572872 | tf_op jit(solution)/shard_map/ppermute | solution.py:20
  7.4 36.0 %collective-permute-start.2 = (bf16[256,1024]{1,0:T(8,128)(2,1)}, bf16[256,1024]{1,0:T(8,128)(2,1)S(1)}, u32[]{:S(2)}, u32[]{:S(2)}) collective-permute-start(bf16[256,1024]{1,0:T(8,128)(2,1)} %get-tuple-element.22.refs_0_), channel_id=1, source_target_pairs={{0,1},{1,0},{2,3},{3,2},{4,5},{5,4},{6,7},{7,6},{8,9},{9,8},{10,11... | collective-permute-start | bytes 1572872 | tf_op jit(solution)/shard_map/ppermute | solution.py:20
  7.4 39.8 %collective-permute-start.7 = (bf16[256,1024]{1,0:T(8,128)(2,1)}, bf16[256,1024]{1,0:T(8,128)(2,1)S(1)}, u32[]{:S(2)}, u32[]{:S(2)}) collective-permute-start(bf16[256,1024]{1,0:T(8,128)(2,1)} %get-tuple-element.26.refs_0_), channel_id=1, source_target_pairs={{0,4},{1,5},{2,6},{3,7},{4,0},{5,1},{6,2},{7,3},{8,12},{9,13},{10,... | collective-permute-start | bytes 1572872 | tf_op jit(solution)/shard_map/ppermute | solution.py:20
  7.9 39.4 %collective-permute-start.8 = (bf16[256,1024]{1,0:T(8,128)(2,1)}, bf16[256,1024]{1,0:T(8,128)(2,1)S(1)}, u32[]{:S(2)}, u32[]{:S(2)}) collective-permute-start(bf16[256,1024]{1,0:T(8,128)(2,1)} %get-tuple-element.26.refs_0_), channel_id=1, source_target_pairs={{0,2},{1,3},{2,0},{3,1},{4,6},{5,7},{6,4},{7,5},{8,10},{9,11},{10,... | collective-permute-start | bytes 1572872 | tf_op jit(solution)/shard_map/ppermute | solution.py:20
  18.9 28.3 %copy-start.8 = (bf16[256,1024]{1,0:T(8,128)(2,1)}, bf16[256,1024]{1,0:T(8,128)(2,1)S(1)}, u32[]{:S(2)}) copy-start(bf16[256,1024]{1,0:T(8,128)(2,1)S(1)} %collective-permute-done.refs_2_) | copy-start | bytes 1572868
  18.9 43.0 %collective-permute-start.9 = (bf16[256,1024]{1,0:T(8,128)(2,1)}, bf16[256,1024]{1,0:T(8,128)(2,1)S(1)}, u32[]{:S(2)}, u32[]{:S(2)}) collective-permute-start(bf16[256,1024]{1,0:T(8,128)(2,1)} %get-tuple-element.26.refs_0_), channel_id=1, source_target_pairs={{0,1},{1,0},{2,3},{3,2},{4,5},{5,4},{6,7},{7,6},{8,9},{9,8},{10,11... | collective-permute-start | bytes 1572872 | tf_op jit(solution)/shard_map/ppermute | solution.py:20
  43.4 18.5 %copy-start.9 = (bf16[256,1024]{1,0:T(8,128)(2,1)}, bf16[256,1024]{1,0:T(8,128)(2,1)S(1)}, u32[]{:S(2)}) copy-start(bf16[256,1024]{1,0:T(8,128)(2,1)S(1)} %collective-permute-done.1.refs_4_) | copy-start | bytes 1572868
  43.4 18.4 %copy-start.10 = (bf16[256,1024]{1,0:T(8,128)(2,1)}, bf16[256,1024]{1,0:T(8,128)(2,1)S(1)}, u32[]{:S(2)}) copy-start(bf16[256,1024]{1,0:T(8,128)(2,1)S(1)} %collective-permute-done.2.refs_1_) | copy-start | bytes 1572868
  43.5 18.4 %collective-permute-start.5 = (bf16[128,1024]{1,0:T(8,128)(2,1)S(1)}, bf16[128,1024]{1,0:T(8,128)(2,1)S(1)}, u32[]{:S(2)}, u32[]{:S(2)}) collective-permute-start(bf16[128,1024]{1,0:T(8,128)(2,1)S(1)} %slice.120), channel_id=1, source_target_pairs={{0,2},{1,3},{2,0},{3,1},{4,6},{5,7},{6,4},{7,5},{8,10},{9,11},{10,... | collective-permute-start | bytes 786440 | tf_op jit(solution)/shard_map/ppermute | solution.py:20
  45.6 16.4 %collective-permute-start.6 = (bf16[128,1024]{1,0:T(8,128)(2,1)S(1)}, bf16[128,1024]{1,0:T(8,128)(2,1)}, u32[]{:S(2)}, u32[]{:S(2)}) collective-permute-start(bf16[128,1024]{1,0:T(8,128)(2,1)S(1)} %slice.121), channel_id=1, source_target_pairs={{0,4},{1,5},{2,6},{3,7},{4,0},{5,1},{6,2},{7,3},{8,12},{9,13},{10,... | collective-permute-start | bytes 786440 | tf_op jit(solution)/shard_map/ppermute | solution.py:20
  47.2 15.3 %copy-start.6 = (bf16[256,1024]{1,0:T(8,128)(2,1)}, bf16[256,1024]{1,0:T(8,128)(2,1)S(1)}, u32[]{:S(2)}) copy-start(bf16[256,1024]{1,0:T(8,128)(2,1)S(1)} %collective-permute-done.7.refs_2_) | copy-start | bytes 1572868
  47.2 17.5 %collective-permute-start.3 = (bf16[256,1024]{1,0:T(8,128)(2,1)S(1)}, bf16[256,1024]{1,0:T(8,128)(2,1)}, u32[]{:S(2)}, u32[]{:S(2)}) collective-permute-start(bf16[256,1024]{1,0:T(8,128)(2,1)S(1)} %collective-permute-done.refs_2_), channel_id=1, source_target_pairs={{0,1},{1,0},{2,3},{3,2},{4,5},{5,4},{6,7},{7,6},{8,9},{9,8},{10,11... | collective-permute-start | bytes 1572872 | tf_op jit(solution)/shard_map/ppermute | solution.py:20
  47.3 16.4 %copy-start.7 = (bf16[256,1024]{1,0:T(8,128)(2,1)}, bf16[256,1024]{1,0:T(8,128)(2,1)S(1)}, u32[]{:S(2)}) copy-start(bf16[256,1024]{1,0:T(8,128)(2,1)S(1)} %collective-permute-done.8.refs_4_) | copy-start | bytes 1572868
  47.3 17.5 %collective-permute-start.4 = (bf16[256,1024]{1,0:T(8,128)(2,1)S(1)}, bf16[256,1024]{1,0:T(8,128)(2,1)}, u32[]{:S(2)}, u32[]{:S(2)}) collective-permute-start(bf16[256,1024]{1,0:T(8,128)(2,1)S(1)} %collective-permute-done.1.refs_4_), channel_id=1, source_target_pairs={{0,1},{1,0},{2,3},{3,2},{4,5},{5,4},{6,7},{7,6},{8,9},{9,8},{10,11... | collective-permute-start | bytes 1572872 | tf_op jit(solution)/shard_map/ppermute | solution.py:20
  61.9 19.3 %copy-start.11 = (bf16[256,1024]{1,0:T(8,128)(2,1)}, bf16[256,1024]{1,0:T(8,128)(2,1)S(1)}, u32[]{:S(2)}) copy-start(bf16[256,1024]{1,0:T(8,128)(2,1)S(1)} %collective-permute-done.9.refs_1_) | copy-start | bytes 1572868
  61.9 2.9 %copy-start.14 = (bf16[128,1024]{1,0:T(8,128)(2,1)}, bf16[128,1024]{1,0:T(8,128)(2,1)S(1)}, u32[]{:S(2)}) copy-start(bf16[128,1024]{1,0:T(8,128)(2,1)S(1)} %collective-permute-done.5.refs_6_) | copy-start | bytes 786436
  61.9 1.7 collective-permute-start.10
  62.1 2.2 collective-permute-start.11
  62.5 24.8 %collective-permute-start.15 = (bf16[256,1024]{1,0:T(8,128)(2,1)S(1)}, bf16[256,1024]{1,0:T(8,128)(2,1)S(1)}, u32[]{:S(2)}, u32[]{:S(2)}) collective-permute-start(bf16[256,1024]{1,0:T(8,128)(2,1)S(1)} %collective-permute-done.7.refs_2_), channel_id=1, source_target_pairs={{0,1},{1,0},{2,3},{3,2},{4,5},{5,4},{6,7},{7,6},{8,9},{9,8},{10,11... | collective-permute-start | bytes 1572872 | tf_op jit(solution)/shard_map/ppermute | solution.py:20
  63.7 23.7 %collective-permute-start.16 = (bf16[256,1024]{1,0:T(8,128)(2,1)S(1)}, bf16[256,1024]{1,0:T(8,128)(2,1)S(1)}, u32[]{:S(2)}, u32[]{:S(2)}) collective-permute-start(bf16[256,1024]{1,0:T(8,128)(2,1)S(1)} %collective-permute-done.8.refs_4_), channel_id=1, source_target_pairs={{0,1},{1,0},{2,3},{3,2},{4,5},{5,4},{6,7},{7,6},{8,9},{9,8},{10,11... | collective-permute-start | bytes 1572872 | tf_op jit(solution)/shard_map/ppermute | solution.py:20
  64.2 17.0 %collective-permute-start.13 = (bf16[128,1024]{1,0:T(8,128)(2,1)S(1)}, bf16[128,1024]{1,0:T(8,128)(2,1)S(1)}, u32[]{:S(2)}, u32[]{:S(2)}) collective-permute-start(bf16[128,1024]{1,0:T(8,128)(2,1)S(1)} %slice.122), channel_id=1, source_target_pairs={{0,2},{1,3},{2,0},{3,1},{4,6},{5,7},{6,4},{7,5},{8,10},{9,11},{10,... | collective-permute-start | bytes 786440 | tf_op jit(solution)/shard_map/ppermute | solution.py:20
  64.8 16.5 %collective-permute-start.14 = (bf16[128,1024]{1,0:T(8,128)(2,1)S(1)}, bf16[128,1024]{1,0:T(8,128)(2,1)S(1)}, u32[]{:S(2)}, u32[]{:S(2)}) collective-permute-start(bf16[128,1024]{1,0:T(8,128)(2,1)S(1)} %slice.123), channel_id=1, source_target_pairs={{0,4},{1,5},{2,6},{3,7},{4,0},{5,1},{6,2},{7,3},{8,12},{9,13},{10,... | collective-permute-start | bytes 786440 | tf_op jit(solution)/shard_map/ppermute | solution.py:20
  81.2 6.2 %copy-start.15 = (bf16[128,1024]{1,0:T(8,128)(2,1)}, bf16[128,1024]{1,0:T(8,128)(2,1)S(1)}, u32[]{:S(2)}) copy-start(bf16[128,1024]{1,0:T(8,128)(2,1)S(1)} %collective-permute-done.13.refs_6_) | copy-start | bytes 786436
  81.2 6.2 %copy-start.16 = (bf16[128,1024]{1,0:T(8,128)(2,1)}, bf16[128,1024]{1,0:T(8,128)(2,1)S(1)}, u32[]{:S(2)}) copy-start(bf16[128,1024]{1,0:T(8,128)(2,1)S(1)} %collective-permute-done.14.refs_7_) | copy-start | bytes 786436
  81.3 6.1 %collective-permute-start.17 = (bf16[128,1024]{1,0:T(8,128)(2,1)S(1)}, bf16[128,1024]{1,0:T(8,128)(2,1)S(1)}, u32[]{:S(2)}, u32[]{:S(2)}) collective-permute-start(bf16[128,1024]{1,0:T(8,128)(2,1)S(1)} %collective-permute-done.13.refs_6_), channel_id=1, source_target_pairs={{0,1},{1,0},{2,3},{3,2},{4,5},{5,4},{6,7},{7,6},{8,9},{9,8},{10,11... | collective-permute-start | bytes 786440 | tf_op jit(solution)/shard_map/ppermute | solution.py:20
  81.3 6.0 %collective-permute-start.18 = (bf16[128,1024]{1,0:T(8,128)(2,1)S(1)}, bf16[128,1024]{1,0:T(8,128)(2,1)S(1)}, u32[]{:S(2)}, u32[]{:S(2)}) collective-permute-start(bf16[128,1024]{1,0:T(8,128)(2,1)S(1)} %collective-permute-done.14.refs_7_), channel_id=1, source_target_pairs={{0,1},{1,0},{2,3},{3,2},{4,5},{5,4},{6,7},{7,6},{8,9},{9,8},{10,11... | collective-permute-start | bytes 786440 | tf_op jit(solution)/shard_map/ppermute | solution.py:20
  83.1 23.8 %collective-permute-start.12 = (bf16[2,416,256]{2,1,0:T(8,128)(2,1)S(1)}, bf16[2,416,256]{2,1,0:T(8,128)(2,1)S(1)}, u32[]{:S(2)}, u32[]{:S(2)}) collective-permute-start(bf16[2,416,256]{2,1,0:T(8,128)(2,1)S(1)} %pad_maximum_fusion.1), channel_id=1, source_target_pairs={{0,8},{1,9},{2,10},{3,11},{4,12},{5,13},{6,14},{7,15},{8,0},{9,1},... | collective-permute-start | bytes 1277960 | tf_op jit(solution)/shard_map/ppermute | solution.py:25
  105.5 4.6 %copy-start.5 = (f32[1664,256]{1,0:T(8,128)S(1)}, f32[1664,256]{1,0:T(8,128)}, u32[]{:S(2)}) copy-start(f32[1664,256]{1,0:T(8,128)} %shard_map.86) | copy-start | bytes 5111812
  107.1 22.7 %collective-permute-start.19 = (bf16[416,256]{1,0:T(8,128)(2,1)S(1)}, bf16[416,256]{1,0:T(8,128)(2,1)S(1)}, u32[]{:S(2)}, u32[]{:S(2)}) collective-permute-start(bf16[416,256]{1,0:T(8,128)(2,1)S(1)} %fusion.47), channel_id=1, source_target_pairs={{0,8},{1,9},{2,10},{3,11},{4,12},{5,13},{6,14},{7,15},{8,0},{9,1},... | collective-permute-start | bytes 638984 | tf_op jit(solution)/shard_map/ppermute | solution.py:25
  107.2 30.7 %collective-permute-start.34 = (bf16[2,416,256]{2,1,0:T(8,128)(2,1)S(1)}, bf16[2,416,256]{2,1,0:T(8,128)(2,1)S(1)}, u32[]{:S(2)}, u32[]{:S(2)}) collective-permute-start(bf16[2,416,256]{2,1,0:T(8,128)(2,1)S(1)} %pad_maximum_fusion.2), channel_id=1, source_target_pairs={{0,8},{1,9},{2,10},{3,11},{4,12},{5,13},{6,14},{7,15},{8,0},{9,1},... | collective-permute-start | bytes 1277960 | tf_op jit(solution)/shard_map/ppermute | solution.py:25
  138.1 11.3 %collective-permute-start.35 = (bf16[416,256]{1,0:T(8,128)(2,1)S(1)}, bf16[416,256]{1,0:T(8,128)(2,1)S(1)}, u32[]{:S(2)}, u32[]{:S(2)}) collective-permute-start(bf16[416,256]{1,0:T(8,128)(2,1)S(1)} %fusion.45), channel_id=1, source_target_pairs={{0,8},{1,9},{2,10},{3,11},{4,12},{5,13},{6,14},{7,15},{8,0},{9,1},... | collective-permute-start | bytes 638984 | tf_op jit(solution)/shard_map/ppermute | solution.py:25
  139.8 19.5 %collective-permute-start.22 = (bf16[128,1024]{1,0:T(8,128)(2,1)}, bf16[128,1024]{1,0:T(8,128)(2,1)}, u32[]{:S(2)}, u32[]{:S(2)}) collective-permute-start(bf16[128,1024]{1,0:T(8,128)(2,1)} %get-tuple-element.55), channel_id=1, source_target_pairs={{0,1},{1,0},{2,3},{3,2},{4,5},{5,4},{6,7},{7,6},{8,9},{9,8},{10,11... | collective-permute-start | bytes 786440 | tf_op jit(solution)/shard_map/ppermute | solution.py:20
  139.8 31.4 %collective-permute-start.21 = (bf16[128,1024]{1,0:T(8,128)(2,1)}, bf16[128,1024]{1,0:T(8,128)(2,1)S(1)}, u32[]{:S(2)}, u32[]{:S(2)}) collective-permute-start(bf16[128,1024]{1,0:T(8,128)(2,1)} %get-tuple-element.56), channel_id=1, source_target_pairs={{0,1},{1,0},{2,3},{3,2},{4,5},{5,4},{6,7},{7,6},{8,9},{9,8},{10,11... | collective-permute-start | bytes 786440 | tf_op jit(solution)/shard_map/ppermute | solution.py:20
  140.4 31.4 %collective-permute-start.25 = (bf16[128,1024]{1,0:T(8,128)(2,1)S(1)}, bf16[128,1024]{1,0:T(8,128)(2,1)S(1)}, u32[]{:S(2)}, u32[]{:S(2)}) collective-permute-start(bf16[128,1024]{1,0:T(8,128)(2,1)S(1)} %get-tuple-element.54), channel_id=1, source_target_pairs={{0,1},{1,0},{2,3},{3,2},{4,5},{5,4},{6,7},{7,6},{8,9},{9,8},{10,11... | collective-permute-start | bytes 786440 | tf_op jit(solution)/shard_map/ppermute | solution.py:20
  140.4 42.0 %collective-permute-start.20 = (bf16[128,1024]{1,0:T(8,128)(2,1)S(1)}, bf16[128,1024]{1,0:T(8,128)(2,1)S(1)}, u32[]{:S(2)}, u32[]{:S(2)}) collective-permute-start(bf16[128,1024]{1,0:T(8,128)(2,1)S(1)} %get-tuple-element.49), channel_id=1, source_target_pairs={{0,1},{1,0},{2,3},{3,2},{4,5},{5,4},{6,7},{7,6},{8,9},{9,8},{10,11... | collective-permute-start | bytes 786440 | tf_op jit(solution)/shard_map/ppermute | solution.py:20
  156.7 2.9 %copy-start.2 = (f32[4,256,1024]{2,1,0:T(8,128)S(1)}, f32[4,256,1024]{2,1,0:T(8,128)}, u32[]{:S(2)}) copy-start(f32[4,256,1024]{2,1,0:T(8,128)} %shard_map.87) | copy-start | bytes 12582916
  159.3 10.7 %collective-permute-start.38 = (bf16[128,1024]{1,0:T(8,128)(2,1)}, bf16[128,1024]{1,0:T(8,128)(2,1)}, u32[]{:S(2)}, u32[]{:S(2)}) collective-permute-start(bf16[128,1024]{1,0:T(8,128)(2,1)} %get-tuple-element.63), channel_id=1, source_target_pairs={{0,1},{1,0},{2,3},{3,2},{4,5},{5,4},{6,7},{7,6},{8,9},{9,8},{10,11... | collective-permute-start | bytes 786440 | tf_op jit(solution)/shard_map/ppermute | solution.py:20
  161.4 10.5 %collective-permute-start.23 = (bf16[128,1024]{1,0:T(8,128)(2,1)}, bf16[128,1024]{1,0:T(8,128)(2,1)}, u32[]{:S(2)}, u32[]{:S(2)}) collective-permute-start(bf16[128,1024]{1,0:T(8,128)(2,1)} %fusion.36), channel_id=1, source_target_pairs={{0,2},{1,3},{2,0},{3,1},{4,6},{5,7},{6,4},{7,5},{8,10},{9,11},{10,... | collective-permute-start | bytes 786440 | tf_op jit(solution)/shard_map/ppermute | solution.py:20
  170.0 12.4 %collective-permute-start.28 = (bf16[128,1024]{1,0:T(8,128)(2,1)S(1)}, bf16[128,1024]{1,0:T(8,128)(2,1)S(1)}, u32[]{:S(2)}, u32[]{:S(2)}) collective-permute-start(bf16[128,1024]{1,0:T(8,128)(2,1)S(1)} %get-tuple-element.52), channel_id=1, source_target_pairs={{0,1},{1,0},{2,3},{3,2},{4,5},{5,4},{6,7},{7,6},{8,9},{9,8},{10,11... | collective-permute-start | bytes 786440 | tf_op jit(solution)/shard_map/ppermute | solution.py:20
  171.2 2.5 %collective-permute-start.37 = (bf16[128,1024]{1,0:T(8,128)(2,1)}, bf16[128,1024]{1,0:T(8,128)(2,1)S(1)}, u32[]{:S(2)}, u32[]{:S(2)}) collective-permute-start(bf16[128,1024]{1,0:T(8,128)(2,1)} %get-tuple-element.64), channel_id=1, source_target_pairs={{0,1},{1,0},{2,3},{3,2},{4,5},{5,4},{6,7},{7,6},{8,9},{9,8},{10,11... | collective-permute-start | bytes 786440 | tf_op jit(solution)/shard_map/ppermute | solution.py:20
  171.8 23.5 %copy-start.3 = (f32[4,256,1024]{2,1,0:T(8,128)S(1)}, f32[4,256,1024]{2,1,0:T(8,128)}, u32[]{:S(2)}) copy-start(f32[4,256,1024]{2,1,0:T(8,128)} %shard_map.89) | copy-start | bytes 12582916
  171.8 2.2 %collective-permute-start.41 = (bf16[128,1024]{1,0:T(8,128)(2,1)S(1)}, bf16[128,1024]{1,0:T(8,128)(2,1)S(1)}, u32[]{:S(2)}, u32[]{:S(2)}) collective-permute-start(bf16[128,1024]{1,0:T(8,128)(2,1)S(1)} %get-tuple-element.62), channel_id=1, source_target_pairs={{0,1},{1,0},{2,3},{3,2},{4,5},{5,4},{6,7},{7,6},{8,9},{9,8},{10,11... | collective-permute-start | bytes 786440 | tf_op jit(solution)/shard_map/ppermute | solution.py:20
  171.9 8.6 %collective-permute-start.39 = (bf16[128,1024]{1,0:T(8,128)(2,1)S(1)}, bf16[128,1024]{1,0:T(8,128)(2,1)S(1)}, u32[]{:S(2)}, u32[]{:S(2)}) collective-permute-start(bf16[128,1024]{1,0:T(8,128)(2,1)S(1)} %fusion.14), channel_id=1, source_target_pairs={{0,2},{1,3},{2,0},{3,1},{4,6},{5,7},{6,4},{7,5},{8,10},{9,11},{10,... | collective-permute-start | bytes 786440 | tf_op jit(solution)/shard_map/ppermute | solution.py:20
  173.7 9.2 %collective-permute-start.31 = (bf16[128,1024]{1,0:T(8,128)(2,1)S(1)}, bf16[128,1024]{1,0:T(8,128)(2,1)S(1)}, u32[]{:S(2)}, u32[]{:S(2)}) collective-permute-start(bf16[128,1024]{1,0:T(8,128)(2,1)S(1)} %get-tuple-element.50), channel_id=1, source_target_pairs={{0,1},{1,0},{2,3},{3,2},{4,5},{5,4},{6,7},{7,6},{8,9},{9,8},{10,11... | collective-permute-start | bytes 786440 | tf_op jit(solution)/shard_map/ppermute | solution.py:20
  174.0 9.0 %collective-permute-start.24 = (bf16[128,1024]{1,0:T(8,128)(2,1)S(1)}, bf16[128,1024]{1,0:T(8,128)(2,1)S(1)}, u32[]{:S(2)}, u32[]{:S(2)}) collective-permute-start(bf16[128,1024]{1,0:T(8,128)(2,1)S(1)} %get-tuple-element.42), channel_id=1, source_target_pairs={{0,4},{1,5},{2,6},{3,7},{4,0},{5,1},{6,2},{7,3},{8,12},{9,13},{10,... | collective-permute-start | bytes 786440 | tf_op jit(solution)/shard_map/ppermute | solution.py:20
  180.5 7.8 %collective-permute-start.26 = (bf16[128,1024]{1,0:T(8,128)(2,1)S(1)}, bf16[128,1024]{1,0:T(8,128)(2,1)S(1)}, u32[]{:S(2)}, u32[]{:S(2)}) collective-permute-start(bf16[128,1024]{1,0:T(8,128)(2,1)S(1)} %get-tuple-element.43), channel_id=1, source_target_pairs={{0,2},{1,3},{2,0},{3,1},{4,6},{5,7},{6,4},{7,5},{8,10},{9,11},{10,... | collective-permute-start | bytes 786440 | tf_op jit(solution)/shard_map/ppermute | solution.py:20
  182.4 6.8 %collective-permute-start.36 = (bf16[128,1024]{1,0:T(8,128)(2,1)S(1)}, bf16[128,1024]{1,0:T(8,128)(2,1)S(1)}, u32[]{:S(2)}, u32[]{:S(2)}) collective-permute-start(bf16[128,1024]{1,0:T(8,128)(2,1)S(1)} %get-tuple-element.57), channel_id=1, source_target_pairs={{0,1},{1,0},{2,3},{3,2},{4,5},{5,4},{6,7},{7,6},{8,9},{9,8},{10,11... | collective-permute-start | bytes 786440 | tf_op jit(solution)/shard_map/ppermute | solution.py:20
  182.5 6.8 %collective-permute-start.44 = (bf16[128,1024]{1,0:T(8,128)(2,1)S(1)}, bf16[128,1024]{1,0:T(8,128)(2,1)S(1)}, u32[]{:S(2)}, u32[]{:S(2)}) collective-permute-start(bf16[128,1024]{1,0:T(8,128)(2,1)S(1)} %get-tuple-element.60), channel_id=1, source_target_pairs={{0,1},{1,0},{2,3},{3,2},{4,5},{5,4},{6,7},{7,6},{8,9},{9,8},{10,11... | collective-permute-start | bytes 786440 | tf_op jit(solution)/shard_map/ppermute | solution.py:20
  182.9 6.8 %collective-permute-start.47 = (bf16[128,1024]{1,0:T(8,128)(2,1)S(1)}, bf16[128,1024]{1,0:T(8,128)(2,1)S(1)}, u32[]{:S(2)}, u32[]{:S(2)}) collective-permute-start(bf16[128,1024]{1,0:T(8,128)(2,1)S(1)} %get-tuple-element.58), channel_id=1, source_target_pairs={{0,1},{1,0},{2,3},{3,2},{4,5},{5,4},{6,7},{7,6},{8,9},{9,8},{10,11... | collective-permute-start | bytes 786440 | tf_op jit(solution)/shard_map/ppermute | solution.py:20
  183.0 8.7 %collective-permute-start.40 = (bf16[128,1024]{1,0:T(8,128)(2,1)S(1)}, bf16[128,1024]{1,0:T(8,128)(2,1)S(1)}, u32[]{:S(2)}, u32[]{:S(2)}) collective-permute-start(bf16[128,1024]{1,0:T(8,128)(2,1)S(1)} %get-tuple-element.47), channel_id=1, source_target_pairs={{0,4},{1,5},{2,6},{3,7},{4,0},{5,1},{6,2},{7,3},{8,12},{9,13},{10,... | collective-permute-start | bytes 786440 | tf_op jit(solution)/shard_map/ppermute | solution.py:20
  188.4 6.9 %collective-permute-start.42 = (bf16[128,1024]{1,0:T(8,128)(2,1)S(1)}, bf16[128,1024]{1,0:T(8,128)(2,1)S(1)}, u32[]{:S(2)}, u32[]{:S(2)}) collective-permute-start(bf16[128,1024]{1,0:T(8,128)(2,1)S(1)} %get-tuple-element.48), channel_id=1, source_target_pairs={{0,2},{1,3},{2,0},{3,1},{4,6},{5,7},{6,4},{7,5},{8,10},{9,11},{10,... | collective-permute-start | bytes 786440 | tf_op jit(solution)/shard_map/ppermute | solution.py:20
  189.2 6.7 %collective-permute-start.30 = (bf16[128,1024]{1,0:T(8,128)(2,1)S(1)}, bf16[128,1024]{1,0:T(8,128)(2,1)S(1)}, u32[]{:S(2)}, u32[]{:S(2)}) collective-permute-start(bf16[128,1024]{1,0:T(8,128)(2,1)S(1)} %get-tuple-element.51), channel_id=1, source_target_pairs={{0,1},{1,0},{2,3},{3,2},{4,5},{5,4},{6,7},{7,6},{8,9},{9,8},{10,11... | collective-permute-start | bytes 786440 | tf_op jit(solution)/shard_map/ppermute | solution.py:20
  189.3 11.4 %collective-permute-start.46 = (bf16[128,1024]{1,0:T(8,128)(2,1)S(1)}, bf16[128,1024]{1,0:T(8,128)(2,1)S(1)}, u32[]{:S(2)}, u32[]{:S(2)}) collective-permute-start(bf16[128,1024]{1,0:T(8,128)(2,1)S(1)} %get-tuple-element.59), channel_id=1, source_target_pairs={{0,1},{1,0},{2,3},{3,2},{4,5},{5,4},{6,7},{7,6},{8,9},{9,8},{10,11... | collective-permute-start | bytes 786440 | tf_op jit(solution)/shard_map/ppermute | solution.py:20
  189.8 9.2 %collective-permute-start.32 = (bf16[128,1024]{1,0:T(8,128)(2,1)S(1)}, bf16[128,1024]{1,0:T(8,128)(2,1)S(1)}, u32[]{:S(2)}, u32[]{:S(2)}) collective-permute-start(bf16[128,1024]{1,0:T(8,128)(2,1)S(1)} %get-tuple-element.40), channel_id=1, source_target_pairs={{0,4},{1,5},{2,6},{3,7},{4,0},{5,1},{6,2},{7,3},{8,12},{9,13},{10,... | collective-permute-start | bytes 786440 | tf_op jit(solution)/shard_map/ppermute | solution.py:20
  195.3 20.8 %copy-start.1 = (f32[52,128]{1,0:T(8,128)S(1)}, f32[52,128]{1,0:T(8,128)}, u32[]{:S(2)}) copy-start(f32[52,128]{1,0:T(8,128)} %param.15) | copy-start | bytes 79876
  195.7 9.3 %collective-permute-start.48 = (bf16[128,1024]{1,0:T(8,128)(2,1)S(1)}, bf16[128,1024]{1,0:T(8,128)(2,1)S(1)}, u32[]{:S(2)}, u32[]{:S(2)}) collective-permute-start(bf16[128,1024]{1,0:T(8,128)(2,1)S(1)} %get-tuple-element.45), channel_id=1, source_target_pairs={{0,4},{1,5},{2,6},{3,7},{4,0},{5,1},{6,2},{7,3},{8,12},{9,13},{10,... | collective-permute-start | bytes 786440 | tf_op jit(solution)/shard_map/ppermute | solution.py:20
  195.8 9.3 %collective-permute-start.27 = (bf16[128,1024]{1,0:T(8,128)(2,1)S(1)}, bf16[128,1024]{1,0:T(8,128)(2,1)S(1)}, u32[]{:S(2)}, u32[]{:S(2)}) collective-permute-start(bf16[128,1024]{1,0:T(8,128)(2,1)S(1)} %get-tuple-element.53), channel_id=1, source_target_pairs={{0,1},{1,0},{2,3},{3,2},{4,5},{5,4},{6,7},{7,6},{8,9},{9,8},{10,11... | collective-permute-start | bytes 786440 | tf_op jit(solution)/shard_map/ppermute | solution.py:20
  195.8 14.8 %collective-permute-start.29 = (bf16[128,1024]{1,0:T(8,128)(2,1)S(1)}, bf16[128,1024]{1,0:T(8,128)(2,1)S(1)}, u32[]{:S(2)}, u32[]{:S(2)}) collective-permute-start(bf16[128,1024]{1,0:T(8,128)(2,1)S(1)} %get-tuple-element.41), channel_id=1, source_target_pairs={{0,4},{1,5},{2,6},{3,7},{4,0},{5,1},{6,2},{7,3},{8,12},{9,13},{10,... | collective-permute-start | bytes 786440 | tf_op jit(solution)/shard_map/ppermute | solution.py:20
  199.0 11.6 %collective-permute-start.33 = (bf16[128,1024]{1,0:T(8,128)(2,1)S(1)}, bf16[128,1024]{1,0:T(8,128)(2,1)S(1)}, u32[]{:S(2)}, u32[]{:S(2)}) collective-permute-start(bf16[128,1024]{1,0:T(8,128)(2,1)S(1)} %fusion.26), channel_id=1, source_target_pairs={{0,2},{1,3},{2,0},{3,1},{4,6},{5,7},{6,4},{7,5},{8,10},{9,11},{10,... | collective-permute-start | bytes 786440 | tf_op jit(solution)/shard_map/ppermute | solution.py:20
  200.7 10.1 %collective-permute-start.43 = (bf16[128,1024]{1,0:T(8,128)(2,1)S(1)}, bf16[128,1024]{1,0:T(8,128)(2,1)S(1)}, u32[]{:S(2)}, u32[]{:S(2)}) collective-permute-start(bf16[128,1024]{1,0:T(8,128)(2,1)S(1)} %get-tuple-element.61), channel_id=1, source_target_pairs={{0,1},{1,0},{2,3},{3,2},{4,5},{5,4},{6,7},{7,6},{8,9},{9,8},{10,11... | collective-permute-start | bytes 786440 | tf_op jit(solution)/shard_map/ppermute | solution.py:20
  205.0 9.9 %collective-permute-start.45 = (bf16[128,1024]{1,0:T(8,128)(2,1)S(1)}, bf16[128,1024]{1,0:T(8,128)(2,1)S(1)}, u32[]{:S(2)}, u32[]{:S(2)}) collective-permute-start(bf16[128,1024]{1,0:T(8,128)(2,1)S(1)} %get-tuple-element.46), channel_id=1, source_target_pairs={{0,4},{1,5},{2,6},{3,7},{4,0},{5,1},{6,2},{7,3},{8,12},{9,13},{10,... | collective-permute-start | bytes 786440 | tf_op jit(solution)/shard_map/ppermute | solution.py:20
  205.1 9.8 %collective-permute-start.49 = (bf16[128,1024]{1,0:T(8,128)(2,1)S(1)}, bf16[128,1024]{1,0:T(8,128)(2,1)S(1)}, u32[]{:S(2)}, u32[]{:S(2)}) collective-permute-start(bf16[128,1024]{1,0:T(8,128)(2,1)S(1)} %fusion.4), channel_id=1, source_target_pairs={{0,2},{1,3},{2,0},{3,1},{4,6},{5,7},{6,4},{7,5},{8,10},{9,11},{10,... | collective-permute-start | bytes 786440 | tf_op jit(solution)/shard_map/ppermute | solution.py:20
  (5 other events, 4.8 us)

commit v4 on v3

--- a/solution.py
+++ b/solution.py
@@ -11,7 +11,8 @@
 RO = 8
 CHUNKS = 2
 VMEM_BYTES = 56 * 2**20
-GATHER_MASKS = (0, 1, 4, 5, 2, 3, 6, 7)
+FIRST_MASKS = (0, 1, 4, 5, 2, 3)
+LAST_MASKS = (6, 7)
 SENT_MASKS = (7, 5, 3, 1)
 KEPT_MASKS = (6, 4, 2, 0)
 
@@ -84,9 +85,9 @@
     )(*weights, *factors)
 
 
-def joined_product(slot, blocks, joined):
-    width = blocks[0].shape[1]
-    rows = blocks[0].shape[0]
+def joined_product(slot, blocks, masks, joined, before=None):
+    width = joined.shape[2]
+    rows = sum(part.shape[0] for part in blocks[0]) if isinstance(blocks[0], tuple) else blocks[0].shape[0]
     height = joined.shape[1]
     flat = []
     places = []
@@ -95,14 +96,16 @@
         places.append(tuple(range(len(flat), len(flat) + len(parts))))
         flat.extend(parts)
 
+    extra = () if before is None else (before,)
+
     def mask_of(step):
         mask = step * 0
-        for index, value in enumerate(GATHER_MASKS):
+        for index, value in enumerate(masks):
             mask = jnp.where(step == index, value, mask)
         return mask
 
     def kernel(slot_ref, *refs):
-        x_refs, w_ref, out_ref = refs[: len(flat)], refs[len(flat)], refs[len(flat) + 1]
+        x_refs, w_ref, out_ref = refs[: len(flat)], refs[len(flat)], refs[-1]
         step = pl.program_id(0)
         for index, place in enumerate(places):
 
@@ -113,8 +116,10 @@
                 value = lax.dot_general(
                     w_ref[0], x, (((1,), (1,)), ((), ())), preferred_element_type=jnp.float32
                 )
-                if index == 0:
+                if index == 0 and before is None:
                     out_ref[...] = value
+                elif index == 0:
+                    out_ref[...] = refs[-2][...] + value
                 else:
                     out_ref[...] += value
 
@@ -124,13 +129,16 @@
             num_scalar_prefetch=1,
             grid=(len(places),),
             in_specs=[pl.BlockSpec(b.shape, lambda i, s: (0, 0)) for b in flat]
-            + [pl.BlockSpec((1, height, width), lambda i, s: (s[0] ^ mask_of(i), 0, 0))],
+            + [pl.BlockSpec((1, height, width), lambda i, s: (s[0] ^ mask_of(i), 0, 0))]
+            + [pl.BlockSpec((height, rows), lambda i, s: (0, 0))] * len(extra),
             out_specs=pl.BlockSpec((height, rows), lambda i, s: (0, 0)),
         ),
         out_shape=jax.ShapeDtypeStruct((height, rows), jnp.float32),
         compiler_params=params(),
-        cost_estimate=cost(2 * rows * width * RO * height, 2 * width * RO * height),
-    )(slot, *flat, joined)
+        cost_estimate=cost(
+            2 * rows * width * len(masks) * height, 2 * width * len(masks) * height
+        ),
+    )(slot, *flat, joined, *extra)
 
 
 def output_product(slot, hidden, down, masks, kind):
@@ -173,26 +181,27 @@
     return lax.optimization_barrier(values)
 
 
-def scatter_sum(sent, kept):
-    half = sent.shape[1] // 2
-
-    def summed(index, part):
-        span = slice(part * half, (part + 1) * half)
-        return kept[index, span] + partner(sent[index, span], 1).astype(jnp.float32)
-
-    def send(value, mask):
-        return partner(value.astype(jnp.bfloat16), mask).astype(jnp.float32)
-
-    diagonal_a = send(summed(0, 0), 2)
-    diagonal_b = send(summed(0, 1), 4)
-    far_b = send(summed(1, 1), 4)
-    near_a = send(summed(2, 0), 2)
-    far_a = send(summed(1, 0) + diagonal_a, 4)
-    near_b = send(summed(2, 1) + diagonal_b, 2)
-    return [
-        (summed(3, 0) + far_a + near_a).astype(jnp.bfloat16),
-        (summed(3, 1) + far_b + near_b).astype(jnp.bfloat16),
-    ]
+def exchange_pair(sent, kept):
+    first = kept[0] + partner(sent[0], 1).astype(jnp.float32)
+    rest = partner(sent[1:], 1)
+    return first.astype(jnp.bfloat16), rest
+
+
+def forward(diagonal, rest, kept, by_y):
+    arrived = partner(diagonal, 2 if by_y else 4).astype(jnp.float32)
+    far = kept[1] + rest[0].astype(jnp.float32)
+    near = kept[2] + rest[1].astype(jnp.float32)
+    if by_y:
+        far = far + arrived
+    else:
+        near = near + arrived
+    return far.astype(jnp.bfloat16), near.astype(jnp.bfloat16)
+
+
+def collect(far, near, rest, kept):
+    total = kept[3] + rest[2].astype(jnp.float32)
+    total = total + partner(far, 4).astype(jnp.float32) + partner(near, 2).astype(jnp.float32)
+    return total.astype(jnp.bfloat16)
 
 
 def body(tokens, token_scale, gate_tiles, up_tiles, gate_scale, up_scale, down_tiles, down_scale):
@@ -223,22 +232,16 @@
     far_a, near_a = partner(own_a, 4), partner(own_a, 2)
     pair_a = partner(own_a, 1)
     far_b, near_b = partner(own_b, 4), partner(own_b, 2)
-    pair_b = partner(own_b, 1)
     joined = scale_rows(
         (gate_tiles[0].T, up_tiles[0].T), (spread(gate_scale.T), spread(up_scale.T)), unit
     )
-    far_a, near_a, pair_a, joined = tie(far_a, near_a, pair_a, joined)
+    far_a, near_a, pair_a, own_b, joined = tie(far_a, near_a, pair_a, own_b, joined)
     diagonal_a = partner(far_a[:half], 2), partner(near_a[half:], 4)
     far_pair_a, near_pair_a = partner(far_a, 1), partner(near_a, 1)
-    down_eff = scale_rows((down_tiles[0],), (spread(down_scale),), unit)
-    *diagonal_a, far_b, near_b, pair_b, down_eff = tie(
-        *diagonal_a, far_b, near_b, pair_b, down_eff
-    )
-
-    def product(own, pair, far, far_pair, near, near_pair, diagonal):
-        last = tuple(partner(part, 1) for part in diagonal)
-        blocks = [own, pair, far, far_pair, near, near_pair, tuple(diagonal), last]
-        return joined_product(slot, blocks, joined)
+    pair_b = partner(own_b, 1)
+
+    def pairs(diagonal):
+        return [tuple(diagonal), tuple(partner(part, 1) for part in diagonal)]
 
     def share(partial_value, target):
         start = target * piece_cols
@@ -277,24 +280,48 @@
             full = lax.dynamic_update_slice_in_dim(full, current, source * piece_cols, 0)
         return full
 
-    def output(hidden):
-        sent = output_product(slot, hidden, down_eff, SENT_MASKS, jnp.bfloat16)
-        kept = output_product(slot, hidden, down_eff, KEPT_MASKS, jnp.float32)
-        return scatter_sum(sent, kept)
-
-    partial_a = product(own_a, pair_a, far_a, far_pair_a, near_a, near_pair_a, diagonal_a)
-    sent_a = first_share(partial_a)
+    blocks_a = [own_a, pair_a, far_a, far_pair_a, near_a, near_pair_a]
+    partial_a = joined_product(slot, blocks_a, FIRST_MASKS, joined)
+    *diagonal_a, far_b, near_b, pair_b, partial_a = tie(
+        *diagonal_a, far_b, near_b, pair_b, partial_a
+    )
+    last_a = pairs(diagonal_a)
     diagonal_b = partner(far_b[:half], 2), partner(near_b[half:], 4)
     far_pair_b, near_pair_b = partner(far_b, 1), partner(near_b, 1)
-    *diagonal_b, partial_a = tie(*diagonal_b, partial_a)
-    partial_b = product(own_b, pair_b, far_b, far_pair_b, near_b, near_pair_b, diagonal_b)
+    partial_a = joined_product(slot, last_a, LAST_MASKS, joined, partial_a)
+    sent_a = first_share(partial_a)
+    *diagonal_b, far_pair_b, near_pair_b, sent_a = tie(
+        *diagonal_b, far_pair_b, near_pair_b, sent_a
+    )
+    blocks_b = [own_b, pair_b, far_b, far_pair_b, near_b, near_pair_b] + pairs(diagonal_b)
+    partial_b = joined_product(slot, blocks_b, FIRST_MASKS + LAST_MASKS, joined)
     piece_a = hidden_of(sent_a, partial_a)
     sent_b = first_share(partial_b)
-    piece_a, sent_b = tie(piece_a, sent_b)
+    piece_a, sent_b, factors = tie(piece_a, sent_b, spread(down_scale))
+    down_eff = scale_rows((down_tiles[0],), (factors,), unit)
+    hidden_a = spread_hidden(piece_a)
+    hidden_a, down_eff = tie(hidden_a, down_eff)
     piece_b = hidden_of(sent_b, partial_b)
-    out_a = output(spread_hidden(piece_a))
-    out_b = output(spread_hidden(piece_b))
-    return jnp.concatenate(out_a + out_b, 0)
+
+    def sent_product(hidden):
+        return output_product(slot, hidden, down_eff, SENT_MASKS, jnp.bfloat16)
+
+    def kept_product(hidden):
+        return output_product(slot, hidden, down_eff, KEPT_MASKS, jnp.float32)
+
+    to_pair_a, kept_a = sent_product(hidden_a), kept_product(hidden_a)
+    diagonal, rest_a = exchange_pair(to_pair_a, kept_a)
+    hidden_b = spread_hidden(piece_b)
+    diagonal, hidden_b = tie(diagonal, hidden_b)
+    to_pair_b = sent_product(hidden_b)
+    forward_a = forward(diagonal, rest_a, kept_a, True)
+    *forward_a, hidden_b = tie(*forward_a, hidden_b)
+    kept_b = kept_product(hidden_b)
+    diagonal, rest_b = exchange_pair(to_pair_b, kept_b)
+    forward_b = forward(diagonal, rest_b, kept_b, False)
+    out_a = collect(*forward_a, rest_a, kept_a)
+    out_b = collect(*forward_b, rest_b, kept_b)
+    return jnp.concatenate((out_a, out_b), 0)
 
 
 def solution(mesh):

time: 217 us -> 200 us (0.922)
  waiting for transfers between devices: 65.3 us -> 40.8 us
  other arithmetic: 10.4 us -> 16 us
  Pallas kernels: 96.2 us -> 99.3 us
  starting transfers between devices: 28.5 us -> 25.6 us
    ppermute x46 -> x28, waiting for transfers between devices: 43.6 us -> 30.7 us  [partner(): lax.ppermute(shard, 'gx', [(i, i ^ mask) for i in range(lax.axis_size('gx...]
    ppermute x4, waiting for transfers between devices: 21.7 us -> 10.1 us  [from_behind(): lax.ppermute(shard, 'gx', [(i, (i + by) % devices) for i in range(devices)])]
    convert_element_type x10 -> x8, other arithmetic: 6.92 us -> 11.8 us  [the longest x4 5.27 us: forward(): return (far.astype(jnp.bfloat16), near.astype(jnp.bfloat16))]
    slice x0 -> x2, local copies, waits for them, and re-layouts: none -> 3.05 us  [exchange_pair(): rest = partner(sent[1:], 1)]
    pallas_call x2 -> x3, Pallas kernels: 32.8 us -> 35.5 us  [joined_product(): pl.pallas_call(kernel, grid_spec=pltpu.PrefetchScalarGridSpec(num_scalar_...]
    ppermute x46 -> x28, starting transfers between devices: 22.4 us -> 20.5 us  [partner(): lax.ppermute(shard, 'gx', [(i, i ^ mask) for i in range(lax.axis_size('gx...]
    unnamed x44 -> x48, local copies, waits for them, and re-layouts: 6.13 us -> 6.4 us
  transfers between devices with their start and end apart: 50 -> 32, of which waited for: 14 -> 10; matrix products, arithmetic and copies ran while one was open for 10% -> 14% of each run, Pallas kernels for 43% -> 49%
where the time goes in v4:
time: 200 us; the launch traced here: 199 us
  Pallas kernels  99.3 us (50%)
  waiting for transfers between devices  40.8 us (20%)
  starting transfers between devices  25.6 us (13%)
  local copies, waits for them, and re-layouts  16.6 us (8%)
  other arithmetic  16 us (8%)
    pallas_call x3, Pallas kernels, joined_product(): pl.pallas_call(kernel, grid_spec=pltpu.PrefetchScalarGridSpec(num_scalar_...  35.5 us
    pallas_call x2, Pallas kernels, scale_rows(): pl.pallas_call(kernel, grid=(RO,), in_specs=[pl.BlockSpec((height, column...  33.6 us
    ppermute x28, waiting for transfers between devices, partner(): lax.ppermute(shard, 'gx', [(i, i ^ mask) for i in range(lax.axis_size('gx...  30.7 us
    pallas_call x4, Pallas kernels, output_product(): pl.pallas_call(kernel, grid_spec=pltpu.PrefetchScalarGridSpec(num_scalar_...  27.3 us
    ppermute x28, starting transfers between devices, partner(): lax.ppermute(shard, 'gx', [(i, i ^ mask) for i in range(lax.axis_size('gx...  20.5 us
    ppermute x4, waiting for transfers between devices, from_behind(): lax.ppermute(shard, 'gx', [(i, (i + by) % devices) for i in range(devices)])  10.1 us
    unnamed x48, local copies, waits for them, and re-layouts  6.4 us
    convert_element_type x4, other arithmetic, forward(): return (far.astype(jnp.bfloat16), near.astype(jnp.bfloat16))  5.27 us
  transfers between devices with their start and end apart: 32, of which 10 were waited for; matrix products, arithmetic and copies ran while one was open for 14% of the time, Pallas kernels for 49%

profile of v4, /device:TPU:0, one launch (start us, length us, event | category | flops | bytes accessed | tf_op | source)
XLA Modules:
  0.0 198.7 jit_solution(15937798163797437424)
XLA Ops:
  0.0 2.9 %shard_map.82 = (bf16[256,1024]{1,0:T(8,128)(2,1)}, bf16[256,1024]{1,0:T(8,128)(2,1)}) custom-call(bf16[512,1024]{1,0:T(8,128)(2,1)} %x_ref.1, f32[8,512]{1,0:T(8,128)} %bitcast.121), custom_call_target="tpu_custom_call" | custom-call | flops 524288 | bytes 2097152 | tf_op jit(solution)/shard_map/pallas_call | solution.py:52
  2.9 3.0 %collective-permute-start = (bf16[256,1024]{1,0:T(8,128)(2,1)}, bf16[256,1024]{1,0:T(8,128)(2,1)S(1)}, u32[]{:S(2)}, u32[]{:S(2)}) collective-permute-start(bf16[256,1024]{1,0:T(8,128)(2,1)} %get-tuple-element.33.refs_0_), channel_id=1, source_target_pairs={{0,4},{1,5},{2,6},{3,7},{4,0},{5,1},{6,2},{7,3},{8,12},{9,13},{10,... | collective-permute-start | bytes 1572872 | tf_op jit(solution)/shard_map/ppermute | solution.py:21
  5.9 1.5 collective-permute-start.1
  7.4 0.8 dynamic-slice_bitcast_fusion.4
  8.6 1.1 copy.9
  9.9 1.1 copy.10
  11.0 21.0 %shard_map.83.refs_6_.refs_4_.refs_10_ = bf16[8,1664,1024]{2,1,0:T(8,128)(2,1)} custom-call(bf16[832,8192]{1,0:T(8,128)(2,1)} %bitcast.110, bf16[832,8192]{1,0:T(8,128)(2,1)} %bitcast.111, f32[13,8192]{1,0:T(8,128)} %bitcast.112, f32[13,8192]{1,0:T(8,128)} %bitcast.113), custom_call_target="tpu_custom_call" | custom-call | flops 13631488 | bytes 54525952 | tf_op jit(solution)/shard_map/pallas_call | solution.py:76
  32.0 0.6 collective-permute-start.8
  32.7 0.4 collective-permute-start.5
  33.1 0.3 collective-permute-start.6
  33.7 0.5 collective-permute-done.8.refs_3_
  34.2 1.2 collective-permute-start.3
  35.3 1.6 collective-permute-start.4
  36.9 12.9 %shard_map.84.refs_5_ = f32[1664,256]{1,0:T(8,128)} custom-call(s32[1]{0:T(128)} %bitcast.slot_ref, bf16[256,1024]{1,0:T(8,128)(2,1)} %get-tuple-element.33.refs_0_, bf16[256,1024]{1,0:T(8,128)(2,1)} %copy-done.13, bf16[256,1024]{1,0:T(8,128)(2,1)} %copy-done.8, bf16[256,1024]{1,0:T(8,128)(2,1)} %copy-done.14, bf16[256,1024]{1,0:T(8,128)(2,1)} %copy-done.9, ...), custom_call_target="tpu_custom_call" | custom-call | flops 5234491392 | bytes 20447232 | tf_op jit(solution)/shard_map/pallas_call | solution.py:126
  49.8 3.2 %collective-permute-done.3.refs_0_ = bf16[128,1024]{1,0:T(8,128)(2,1)} collective-permute-done((bf16[128,1024]{1,0:T(8,128)(2,1)S(1)}, bf16[128,1024]{1,0:T(8,128)(2,1)}, u32[]{:S(2)}, u32[]{:S(2)}) %collective-permute-start.3) | collective-permute-done | bytes 262176 | tf_op jit(solution)/shard_map/ppermute | solution.py:21
  53.1 0.5 collective-permute-start.15
  53.6 0.4 collective-permute-start.13
  54.1 0.6 collective-permute-start.10
  54.8 1.5 collective-permute-start.11
  56.3 0.7 copy-done.20
  57.0 6.2 %shard_map.85 = f32[1664,256]{1,0:T(8,128)} custom-call(s32[1]{0:T(128)} %bitcast.slot_ref, bf16[128,1024]{1,0:T(8,128)(2,1)} %collective-permute-done.3.refs_0_, bf16[128,1024]{1,0:T(8,128)(2,1)} %collective-permute-done.4.refs_1_, bf16[128,1024]{1,0:T(8,128)(2,1)} %copy-done.19, bf16[128,1024]{1,0:T(8,128)(2,1)} %copy-done.20, ...), custom_call_target="tpu_custom_call" | custom-call | flops 1744830464 | bytes 6815744 | tf_op jit(solution)/shard_map/pallas_call | solution.py:126
  63.2 1.3 fusion.26
  64.5 0.8 pad_maximum_fusion.1
  65.4 0.5 collective-permute-start.18
  66.3 1.1 copy.11
  67.5 2.7 %collective-permute-start.16 = (bf16[2,416,256]{2,1,0:T(8,128)(2,1)S(1)}, bf16[2,416,256]{2,1,0:T(8,128)(2,1)S(1)}, u32[]{:S(2)}, u32[]{:S(2)}) collective-permute-start(bf16[2,416,256]{2,1,0:T(8,128)(2,1)S(1)} %copy-done.16), channel_id=1, source_target_pairs={{0,8},{1,9},{2,10},{3,11},{4,12},{5,13},{6,14},{7,15},{8,0},{9,1},... | collective-permute-start | bytes 1277960 | tf_op jit(solution)/shard_map/ppermute | solution.py:26
  70.2 0.7 copy-done.17
  70.9 0.7 copy-done.18
  71.6 16.4 %shard_map.86 = f32[1664,256]{1,0:T(8,128)} custom-call(s32[1]{0:T(128)} %bitcast.slot_ref, bf16[256,1024]{1,0:T(8,128)(2,1)} %get-tuple-element.37.refs_0_, bf16[256,1024]{1,0:T(8,128)(2,1)} %copy-done.11, bf16[256,1024]{1,0:T(8,128)(2,1)} %copy-done.6, bf16[256,1024]{1,0:T(8,128)(2,1)} %copy-done.12, bf16[256,1024]{1,0:T(8,128)(2,1)} %copy-done.7, ...), custom_call_target="tpu_custom_call" | custom-call | flops 6979321856 | bytes 27262976 | tf_op jit(solution)/shard_map/pallas_call | solution.py:126
  88.0 1.2 fusion.28
  89.9 0.8 copy-done.5
  90.7 2.0 %collective-permute-start.22 = (bf16[2,416,256]{2,1,0:T(8,128)(2,1)S(1)}, bf16[2,416,256]{2,1,0:T(8,128)(2,1)S(1)}, u32[]{:S(2)}, u32[]{:S(2)}) collective-permute-start(bf16[2,416,256]{2,1,0:T(8,128)(2,1)S(1)} %pad_maximum_fusion.2), channel_id=1, source_target_pairs={{0,8},{1,9},{2,10},{3,11},{4,12},{5,13},{6,14},{7,15},{8,0},{9,1},... | collective-permute-start | bytes 1277960 | tf_op jit(solution)/shard_map/ppermute | solution.py:26
  92.7 12.7 %shard_map.87.w_ref = bf16[8,832,1024]{2,1,0:T(8,128)(2,1)} custom-call(bf16[832,8192]{1,0:T(8,128)(2,1)} %bitcast.109, f32[13,8192]{1,0:T(8,128)} %bitcast.114), custom_call_target="tpu_custom_call" | custom-call | flops 6815744 | bytes 27262976 | tf_op jit(solution)/shard_map/pallas_call | solution.py:76
  105.4 6.0 %collective-permute-done.19 = bf16[416,256]{1,0:T(8,128)(2,1)S(1)} collective-permute-done((bf16[416,256]{1,0:T(8,128)(2,1)S(1)}, bf16[416,256]{1,0:T(8,128)(2,1)S(1)}, u32[]{:S(2)}, u32[]{:S(2)}) %collective-permute-start.19) | collective-permute-done | bytes 213024 | tf_op jit(solution)/shard_map/ppermute | solution.py:26
  111.4 0.9 maximum_select_fusion.x_ref
  112.4 6.5 %shard_map.89 = bf16[4,256,1024]{2,1,0:T(8,128)(2,1)} custom-call(s32[1]{0:T(128)} %bitcast.slot_ref, bf16[832,256]{1,0:T(8,128)(2,1)} %maximum_select_fusion.x_ref, bf16[8,832,1024]{2,1,0:T(8,128)(2,1)} %shard_map.87.w_ref), custom_call_target="tpu_custom_call" | custom-call | flops 1744830464 | bytes 6815744 | tf_op jit(solution)/shard_map/pallas_call | solution.py:160
  118.8 1.5 slice.107
  120.4 1.1 slice_bitcast_fusion.3
  121.5 0.6 collective-permute-start.21
  122.4 7.1 %shard_map.88 = f32[4,256,1024]{2,1,0:T(8,128)} custom-call(s32[1]{0:T(128)} %bitcast.slot_ref, bf16[832,256]{1,0:T(8,128)(2,1)} %maximum_select_fusion.x_ref, bf16[8,832,1024]{2,1,0:T(8,128)(2,1)} %shard_map.87.w_ref), custom_call_target="tpu_custom_call" | custom-call | flops 1744830464 | bytes 6815744 | tf_op jit(solution)/shard_map/pallas_call | solution.py:160
  129.5 3.9 %collective-permute-done.23 = bf16[416,256]{1,0:T(8,128)(2,1)S(1)} collective-permute-done((bf16[416,256]{1,0:T(8,128)(2,1)S(1)}, bf16[416,256]{1,0:T(8,128)(2,1)S(1)}, u32[]{:S(2)}, u32[]{:S(2)}) %collective-permute-start.23) | collective-permute-done | bytes 213024 | tf_op jit(solution)/shard_map/ppermute | solution.py:26
  133.4 0.9 maximum_select_fusion.1.x_ref
  134.4 2.2 %fusion.12 = bf16[256,1024]{1,0:T(8,128)(2,1)} fusion(f32[4,256,1024]{2,1,0:T(8,128)} %shard_map.88, bf16[256,1024]{1,0:T(8,128)(2,1)S(1)} %collective-permute-done.21), kind=kLoop, calls=%fused_computation.18 | loop fusion | flops 786432 | bytes 2097152 | tf_op jit(solution)/shard_map/convert_element_type | solution.py:187
  136.6 1.5 collective-permute-start.24
  138.1 6.6 %shard_map.91 = bf16[4,256,1024]{2,1,0:T(8,128)(2,1)} custom-call(s32[1]{0:T(128)} %bitcast.slot_ref, bf16[832,256]{1,0:T(8,128)(2,1)} %maximum_select_fusion.1.x_ref, bf16[8,832,1024]{2,1,0:T(8,128)(2,1)} %shard_map.87.w_ref), custom_call_target="tpu_custom_call" | custom-call | flops 1744830464 | bytes 6815744 | tf_op jit(solution)/shard_map/pallas_call | solution.py:160
  144.7 1.5 slice.118
  146.3 1.9 slice_bitcast_fusion.2
  148.2 0.5 collective-permute-start.29
  148.7 1.2 fusion.20
  149.9 0.8 collective-permute-done.24
  150.6 1.3 fusion.15
  151.9 7.1 %shard_map.90 = f32[4,256,1024]{2,1,0:T(8,128)} custom-call(s32[1]{0:T(128)} %bitcast.slot_ref, bf16[832,256]{1,0:T(8,128)(2,1)} %maximum_select_fusion.1.x_ref, bf16[8,832,1024]{2,1,0:T(8,128)(2,1)} %shard_map.87.w_ref), custom_call_target="tpu_custom_call" | custom-call | flops 1744830464 | bytes 6815744 | tf_op jit(solution)/shard_map/pallas_call | solution.py:160
  159.1 1.7 fusion.1
  160.8 1.6 collective-permute-start.26
  162.4 1.9 collective-permute-start.25
  164.3 11.3 %collective-permute-done.30 = bf16[256,1024]{1,0:T(8,128)(2,1)S(1)} collective-permute-done((bf16[256,1024]{1,0:T(8,128)(2,1)S(1)}, bf16[256,1024]{1,0:T(8,128)(2,1)S(1)}, u32[]{:S(2)}, u32[]{:S(2)}) %collective-permute-start.30) | collective-permute-done | bytes 524320 | tf_op jit(solution)/shard_map/ppermute | solution.py:21
  175.7 1.6 fusion.4
  177.2 1.6 collective-permute-start.31
  178.8 1.2 fusion.21
  180.1 6.8 %collective-permute-done.25 = bf16[256,1024]{1,0:T(8,128)(2,1)S(1)} collective-permute-done((bf16[256,1024]{1,0:T(8,128)(2,1)S(1)}, bf16[256,1024]{1,0:T(8,128)(2,1)S(1)}, u32[]{:S(2)}, u32[]{:S(2)}) %collective-permute-start.25) | collective-permute-done | bytes 524320 | tf_op jit(solution)/shard_map/ppermute | solution.py:21
  186.9 1.4 fusion.19
  188.3 8.1 %collective-permute-done.28 = bf16[256,1024]{1,0:T(8,128)(2,1)S(1)} collective-permute-done((bf16[256,1024]{1,0:T(8,128)(2,1)S(1)}, bf16[256,1024]{1,0:T(8,128)(2,1)S(1)}, u32[]{:S(2)}, u32[]{:S(2)}) %collective-permute-start.28) | collective-permute-done | bytes 524320 | tf_op jit(solution)/shard_map/ppermute | solution.py:21
  196.4 1.3 fusion.9
  197.7 1.0 pad_maximum_fusion
  (98 shorter events, 3.0 us)
Async XLA Ops:
  0.0 65.9 %copy-start = (f32[52,128]{1,0:T(8,128)S(1)}, f32[52,128]{1,0:T(8,128)}, u32[]{:S(2)}) copy-start(f32[52,128]{1,0:T(8,128)} %param.15) | copy-start | bytes 79876
  2.9 29.1 %collective-permute-start = (bf16[256,1024]{1,0:T(8,128)(2,1)}, bf16[256,1024]{1,0:T(8,128)(2,1)S(1)}, u32[]{:S(2)}, u32[]{:S(2)}) collective-permute-start(bf16[256,1024]{1,0:T(8,128)(2,1)} %get-tuple-element.33.refs_0_), channel_id=1, source_target_pairs={{0,4},{1,5},{2,6},{3,7},{4,0},{5,1},{6,2},{7,3},{8,12},{9,13},{10,... | collective-permute-start | bytes 1572872 | tf_op jit(solution)/shard_map/ppermute | solution.py:21
  5.9 26.1 %collective-permute-start.1 = (bf16[256,1024]{1,0:T(8,128)(2,1)}, bf16[256,1024]{1,0:T(8,128)(2,1)S(1)}, u32[]{:S(2)}, u32[]{:S(2)}) collective-permute-start(bf16[256,1024]{1,0:T(8,128)(2,1)} %get-tuple-element.33.refs_0_), channel_id=1, source_target_pairs={{0,2},{1,3},{2,0},{3,1},{4,6},{5,7},{6,4},{7,5},{8,10},{9,11},{10,... | collective-permute-start | bytes 1572872 | tf_op jit(solution)/shard_map/ppermute | solution.py:21
  7.4 24.6 %collective-permute-start.2 = (bf16[256,1024]{1,0:T(8,128)(2,1)}, bf16[256,1024]{1,0:T(8,128)(2,1)S(1)}, u32[]{:S(2)}, u32[]{:S(2)}) collective-permute-start(bf16[256,1024]{1,0:T(8,128)(2,1)} %get-tuple-element.33.refs_0_), channel_id=1, source_target_pairs={{0,1},{1,0},{2,3},{3,2},{4,5},{5,4},{6,7},{7,6},{8,9},{9,8},{10,11... | collective-permute-start | bytes 1572872 | tf_op jit(solution)/shard_map/ppermute | solution.py:21
  11.0 21.7 %copy-start.10 = (bf16[256,1024]{1,0:T(8,128)(2,1)S(1)}, bf16[256,1024]{1,0:T(8,128)(2,1)}, u32[]{:S(2)}) copy-start(bf16[256,1024]{1,0:T(8,128)(2,1)} %get-tuple-element.37.refs_0_) | copy-start | bytes 1572868
  32.0 4.9 %copy-start.8 = (bf16[256,1024]{1,0:T(8,128)(2,1)}, bf16[256,1024]{1,0:T(8,128)(2,1)S(1)}, u32[]{:S(2)}) copy-start(bf16[256,1024]{1,0:T(8,128)(2,1)S(1)} %collective-permute-done.refs_2_) | copy-start | bytes 1572868
  32.0 4.9 %copy-start.9 = (bf16[256,1024]{1,0:T(8,128)(2,1)}, bf16[256,1024]{1,0:T(8,128)(2,1)S(1)}, u32[]{:S(2)}) copy-start(bf16[256,1024]{1,0:T(8,128)(2,1)S(1)} %collective-permute-done.1.refs_4_) | copy-start | bytes 1572868
  32.0 1.1 copy-start.13
  32.0 2.1 %collective-permute-start.8 = (bf16[256,1024]{1,0:T(8,128)(2,1)S(1)}, bf16[256,1024]{1,0:T(8,128)(2,1)S(1)}, u32[]{:S(2)}, u32[]{:S(2)}) collective-permute-start(bf16[256,1024]{1,0:T(8,128)(2,1)S(1)} %collective-permute-done.refs_2_), channel_id=1, source_target_pairs={{0,1},{1,0},{2,3},{3,2},{4,5},{5,4},{6,7},{7,6},{8,9},{9,8},{10,11... | collective-permute-start | bytes 1572872 | tf_op jit(solution)/shard_map/ppermute | solution.py:21
  32.6 2.7 %collective-permute-start.9 = (bf16[256,1024]{1,0:T(8,128)(2,1)S(1)}, bf16[256,1024]{1,0:T(8,128)(2,1)S(1)}, u32[]{:S(2)}, u32[]{:S(2)}) collective-permute-start(bf16[256,1024]{1,0:T(8,128)(2,1)S(1)} %collective-permute-done.1.refs_4_), channel_id=1, source_target_pairs={{0,1},{1,0},{2,3},{3,2},{4,5},{5,4},{6,7},{7,6},{8,9},{9,8},{10,11... | collective-permute-start | bytes 1572872 | tf_op jit(solution)/shard_map/ppermute | solution.py:21
  32.7 17.1 %collective-permute-start.5 = (bf16[256,1024]{1,0:T(8,128)(2,1)S(1)}, bf16[256,1024]{1,0:T(8,128)(2,1)S(1)}, u32[]{:S(2)}, u32[]{:S(2)}) collective-permute-start(bf16[256,1024]{1,0:T(8,128)(2,1)S(1)} %copy-done.10), channel_id=1, source_target_pairs={{0,4},{1,5},{2,6},{3,7},{4,0},{5,1},{6,2},{7,3},{8,12},{9,13},{10,... | collective-permute-start | bytes 1572872 | tf_op jit(solution)/shard_map/ppermute | solution.py:21
  33.1 16.6 %collective-permute-start.6 = (bf16[256,1024]{1,0:T(8,128)(2,1)S(1)}, bf16[256,1024]{1,0:T(8,128)(2,1)S(1)}, u32[]{:S(2)}, u32[]{:S(2)}) collective-permute-start(bf16[256,1024]{1,0:T(8,128)(2,1)S(1)} %copy-done.10), channel_id=1, source_target_pairs={{0,2},{1,3},{2,0},{3,1},{4,6},{5,7},{6,4},{7,5},{8,10},{9,11},{10,... | collective-permute-start | bytes 1572872 | tf_op jit(solution)/shard_map/ppermute | solution.py:21
  33.4 19.6 %collective-permute-start.7 = (bf16[256,1024]{1,0:T(8,128)(2,1)S(1)}, bf16[256,1024]{1,0:T(8,128)(2,1)S(1)}, u32[]{:S(2)}, u32[]{:S(2)}) collective-permute-start(bf16[256,1024]{1,0:T(8,128)(2,1)S(1)} %copy-done.10), channel_id=1, source_target_pairs={{0,1},{1,0},{2,3},{3,2},{4,5},{5,4},{6,7},{7,6},{8,9},{9,8},{10,11... | collective-permute-start | bytes 1572872 | tf_op jit(solution)/shard_map/ppermute | solution.py:21
  34.2 2.8 %copy-start.14 = (bf16[256,1024]{1,0:T(8,128)(2,1)}, bf16[256,1024]{1,0:T(8,128)(2,1)S(1)}, u32[]{:S(2)}) copy-start(bf16[256,1024]{1,0:T(8,128)(2,1)S(1)} %collective-permute-done.8.refs_3_) | copy-start | bytes 1572868
  34.2 18.8 %collective-permute-start.3 = (bf16[128,1024]{1,0:T(8,128)(2,1)S(1)}, bf16[128,1024]{1,0:T(8,128)(2,1)}, u32[]{:S(2)}, u32[]{:S(2)}) collective-permute-start(bf16[128,1024]{1,0:T(8,128)(2,1)S(1)} %slice.78), channel_id=1, source_target_pairs={{0,2},{1,3},{2,0},{3,1},{4,6},{5,7},{6,4},{7,5},{8,10},{9,11},{10,... | collective-permute-start | bytes 786440 | tf_op jit(solution)/shard_map/ppermute | solution.py:21
  35.3 1.6 copy-start.15
  35.3 17.7 %collective-permute-start.4 = (bf16[128,1024]{1,0:T(8,128)(2,1)S(1)}, bf16[128,1024]{1,0:T(8,128)(2,1)}, u32[]{:S(2)}, u32[]{:S(2)}) collective-permute-start(bf16[128,1024]{1,0:T(8,128)(2,1)S(1)} %slice.79), channel_id=1, source_target_pairs={{0,4},{1,5},{2,6},{3,7},{4,0},{5,1},{6,2},{7,3},{8,12},{9,13},{10,... | collective-permute-start | bytes 786440 | tf_op jit(solution)/shard_map/ppermute | solution.py:21
  49.8 13.4 %copy-start.6 = (bf16[256,1024]{1,0:T(8,128)(2,1)}, bf16[256,1024]{1,0:T(8,128)(2,1)S(1)}, u32[]{:S(2)}) copy-start(bf16[256,1024]{1,0:T(8,128)(2,1)S(1)} %collective-permute-done.5.refs_2_) | copy-start | bytes 1572868
  49.8 13.4 %copy-start.7 = (bf16[256,1024]{1,0:T(8,128)(2,1)}, bf16[256,1024]{1,0:T(8,128)(2,1)S(1)}, u32[]{:S(2)}) copy-start(bf16[256,1024]{1,0:T(8,128)(2,1)S(1)} %collective-permute-done.6.refs_4_) | copy-start | bytes 1572868
  53.0 3.3 %copy-start.11 = (bf16[256,1024]{1,0:T(8,128)(2,1)}, bf16[256,1024]{1,0:T(8,128)(2,1)S(1)}, u32[]{:S(2)}) copy-start(bf16[256,1024]{1,0:T(8,128)(2,1)S(1)} %collective-permute-done.7.refs_1_) | copy-start | bytes 1572868
  53.0 1.8 collective-permute-start.14
  53.1 3.2 %collective-permute-start.15 = (bf16[128,1024]{1,0:T(8,128)(2,1)}, bf16[128,1024]{1,0:T(8,128)(2,1)S(1)}, u32[]{:S(2)}, u32[]{:S(2)}) collective-permute-start(bf16[128,1024]{1,0:T(8,128)(2,1)} %collective-permute-done.4.refs_1_), channel_id=1, source_target_pairs={{0,1},{1,0},{2,3},{3,2},{4,5},{5,4},{6,7},{7,6},{8,9},{9,8},{10,11... | collective-permute-start | bytes 786440 | tf_op jit(solution)/shard_map/ppermute | solution.py:21
  53.6 11.8 %collective-permute-start.12 = (bf16[256,1024]{1,0:T(8,128)(2,1)S(1)}, bf16[256,1024]{1,0:T(8,128)(2,1)S(1)}, u32[]{:S(2)}, u32[]{:S(2)}) collective-permute-start(bf16[256,1024]{1,0:T(8,128)(2,1)S(1)} %collective-permute-done.5.refs_2_), channel_id=1, source_target_pairs={{0,1},{1,0},{2,3},{3,2},{4,5},{5,4},{6,7},{7,6},{8,9},{9,8},{10,11... | collective-permute-start | bytes 1572872 | tf_op jit(solution)/shard_map/ppermute | solution.py:21
  53.6 11.7 %collective-permute-start.13 = (bf16[256,1024]{1,0:T(8,128)(2,1)S(1)}, bf16[256,1024]{1,0:T(8,128)(2,1)}, u32[]{:S(2)}, u32[]{:S(2)}) collective-permute-start(bf16[256,1024]{1,0:T(8,128)(2,1)S(1)} %collective-permute-done.6.refs_4_), channel_id=1, source_target_pairs={{0,1},{1,0},{2,3},{3,2},{4,5},{5,4},{6,7},{7,6},{8,9},{9,8},{10,11... | collective-permute-start | bytes 1572872 | tf_op jit(solution)/shard_map/ppermute | solution.py:21
  54.1 11.2 %collective-permute-start.10 = (bf16[128,1024]{1,0:T(8,128)(2,1)S(1)}, bf16[128,1024]{1,0:T(8,128)(2,1)}, u32[]{:S(2)}, u32[]{:S(2)}) collective-permute-start(bf16[128,1024]{1,0:T(8,128)(2,1)S(1)} %slice.80), channel_id=1, source_target_pairs={{0,2},{1,3},{2,0},{3,1},{4,6},{5,7},{6,4},{7,5},{8,10},{9,11},{10,... | collective-permute-start | bytes 786440 | tf_op jit(solution)/shard_map/ppermute | solution.py:21
  54.8 1.5 copy-start.19
  54.8 10.5 %collective-permute-start.11 = (bf16[128,1024]{1,0:T(8,128)(2,1)S(1)}, bf16[128,1024]{1,0:T(8,128)(2,1)}, u32[]{:S(2)}, u32[]{:S(2)}) collective-permute-start(bf16[128,1024]{1,0:T(8,128)(2,1)S(1)} %slice.81), channel_id=1, source_target_pairs={{0,4},{1,5},{2,6},{3,7},{4,0},{5,1},{6,2},{7,3},{8,12},{9,13},{10,... | collective-permute-start | bytes 786440 | tf_op jit(solution)/shard_map/ppermute | solution.py:21
  56.3 0.7 copy-start.20
  63.2 4.2 %copy-start.4 = (f32[1664,256]{1,0:T(8,128)S(1)}, f32[1664,256]{1,0:T(8,128)}, u32[]{:S(2)}) copy-start(f32[1664,256]{1,0:T(8,128)} %shard_map.85) | copy-start | bytes 5111812
  65.3 2.1 %copy-start.12 = (bf16[256,1024]{1,0:T(8,128)(2,1)}, bf16[256,1024]{1,0:T(8,128)(2,1)S(1)}, u32[]{:S(2)}) copy-start(bf16[256,1024]{1,0:T(8,128)(2,1)S(1)} %collective-permute-done.12.refs_3_) | copy-start | bytes 1572868
  65.4 4.8 %collective-permute-start.17 = (bf16[128,1024]{1,0:T(8,128)(2,1)}, bf16[128,1024]{1,0:T(8,128)(2,1)S(1)}, u32[]{:S(2)}, u32[]{:S(2)}) collective-permute-start(bf16[128,1024]{1,0:T(8,128)(2,1)} %collective-permute-done.10.refs_6_), channel_id=1, source_target_pairs={{0,1},{1,0},{2,3},{3,2},{4,5},{5,4},{6,7},{7,6},{8,9},{9,8},{10,11... | collective-permute-start | bytes 786440 | tf_op jit(solution)/shard_map/ppermute | solution.py:21
  65.4 4.7 %collective-permute-start.18 = (bf16[128,1024]{1,0:T(8,128)(2,1)}, bf16[128,1024]{1,0:T(8,128)(2,1)S(1)}, u32[]{:S(2)}, u32[]{:S(2)}) collective-permute-start(bf16[128,1024]{1,0:T(8,128)(2,1)} %collective-permute-done.11.refs_7_), channel_id=1, source_target_pairs={{0,1},{1,0},{2,3},{3,2},{4,5},{5,4},{6,7},{7,6},{8,9},{9,8},{10,11... | collective-permute-start | bytes 786440 | tf_op jit(solution)/shard_map/ppermute | solution.py:21
  66.0 1.5 copy-start.16
  67.5 21.9 %collective-permute-start.16 = (bf16[2,416,256]{2,1,0:T(8,128)(2,1)S(1)}, bf16[2,416,256]{2,1,0:T(8,128)(2,1)S(1)}, u32[]{:S(2)}, u32[]{:S(2)}) collective-permute-start(bf16[2,416,256]{2,1,0:T(8,128)(2,1)S(1)} %copy-done.16), channel_id=1, source_target_pairs={{0,8},{1,9},{2,10},{3,11},{4,12},{5,13},{6,14},{7,15},{8,0},{9,1},... | collective-permute-start | bytes 1277960 | tf_op jit(solution)/shard_map/ppermute | solution.py:26
  70.2 0.7 copy-start.17
  70.9 0.7 copy-start.18
  89.2 1.5 copy-start.5
  89.6 21.8 %collective-permute-start.19 = (bf16[416,256]{1,0:T(8,128)(2,1)S(1)}, bf16[416,256]{1,0:T(8,128)(2,1)S(1)}, u32[]{:S(2)}, u32[]{:S(2)}) collective-permute-start(bf16[416,256]{1,0:T(8,128)(2,1)S(1)} %fusion.25), channel_id=1, source_target_pairs={{0,8},{1,9},{2,10},{3,11},{4,12},{5,13},{6,14},{7,15},{8,0},{9,1},... | collective-permute-start | bytes 638984 | tf_op jit(solution)/shard_map/ppermute | solution.py:26
  90.7 31.4 %collective-permute-start.22 = (bf16[2,416,256]{2,1,0:T(8,128)(2,1)S(1)}, bf16[2,416,256]{2,1,0:T(8,128)(2,1)S(1)}, u32[]{:S(2)}, u32[]{:S(2)}) collective-permute-start(bf16[2,416,256]{2,1,0:T(8,128)(2,1)S(1)} %pad_maximum_fusion.2), channel_id=1, source_target_pairs={{0,8},{1,9},{2,10},{3,11},{4,12},{5,13},{6,14},{7,15},{8,0},{9,1},... | collective-permute-start | bytes 1277960 | tf_op jit(solution)/shard_map/ppermute | solution.py:26
  120.4 28.3 %collective-permute-start.20 = (bf16[3,256,1024]{2,1,0:T(8,128)(2,1)S(1)}, bf16[3,256,1024]{2,1,0:T(8,128)(2,1)}, u32[]{:S(2)}, u32[]{:S(2)}) collective-permute-start(bf16[3,256,1024]{2,1,0:T(8,128)(2,1)S(1)} %slice.107), channel_id=1, source_target_pairs={{0,1},{1,0},{2,3},{3,2},{4,5},{5,4},{6,7},{7,6},{8,9},{9,8},{10,11... | collective-permute-start | bytes 4718600 | tf_op jit(solution)/shard_map/ppermute | solution.py:21
  121.5 12.9 %collective-permute-start.21 = (bf16[256,1024]{1,0:T(8,128)(2,1)S(1)}, bf16[256,1024]{1,0:T(8,128)(2,1)S(1)}, u32[]{:S(2)}, u32[]{:S(2)}) collective-permute-start(bf16[256,1024]{1,0:T(8,128)(2,1)S(1)} %slice_bitcast_fusion.3), channel_id=1, source_target_pairs={{0,1},{1,0},{2,3},{3,2},{4,5},{5,4},{6,7},{7,6},{8,9},{9,8},{10,11... | collective-permute-start | bytes 1572872 | tf_op jit(solution)/shard_map/ppermute | solution.py:21
  122.3 11.1 %collective-permute-start.23 = (bf16[416,256]{1,0:T(8,128)(2,1)S(1)}, bf16[416,256]{1,0:T(8,128)(2,1)S(1)}, u32[]{:S(2)}, u32[]{:S(2)}) collective-permute-start(bf16[416,256]{1,0:T(8,128)(2,1)S(1)} %fusion.23), channel_id=1, source_target_pairs={{0,8},{1,9},{2,10},{3,11},{4,12},{5,13},{6,14},{7,15},{8,0},{9,1},... | collective-permute-start | bytes 638984 | tf_op jit(solution)/shard_map/ppermute | solution.py:26
  136.6 14.1 %collective-permute-start.24 = (bf16[256,1024]{1,0:T(8,128)(2,1)}, bf16[256,1024]{1,0:T(8,128)(2,1)S(1)}, u32[]{:S(2)}, u32[]{:S(2)}) collective-permute-start(bf16[256,1024]{1,0:T(8,128)(2,1)} %fusion.12), channel_id=1, source_target_pairs={{0,2},{1,3},{2,0},{3,1},{4,6},{5,7},{6,4},{7,5},{8,10},{9,11},{10,... | collective-permute-start | bytes 1572872 | tf_op jit(solution)/shard_map/ppermute | solution.py:21
  138.1 10.6 %copy-start.2 = (f32[4,256,1024]{2,1,0:T(8,128)S(1)}, f32[4,256,1024]{2,1,0:T(8,128)}, u32[]{:S(2)}) copy-start(f32[4,256,1024]{2,1,0:T(8,128)} %shard_map.88) | copy-start | bytes 12582916
  146.2 29.4 %collective-permute-start.27 = (bf16[3,256,1024]{2,1,0:T(8,128)(2,1)S(1)}, bf16[3,256,1024]{2,1,0:T(8,128)(2,1)}, u32[]{:S(2)}, u32[]{:S(2)}) collective-permute-start(bf16[3,256,1024]{2,1,0:T(8,128)(2,1)S(1)} %slice.118), channel_id=1, source_target_pairs={{0,1},{1,0},{2,3},{3,2},{4,5},{5,4},{6,7},{7,6},{8,9},{9,8},{10,11... | collective-permute-start | bytes 4718600 | tf_op jit(solution)/shard_map/ppermute | solution.py:21
  148.2 10.9 %collective-permute-start.29 = (bf16[256,1024]{1,0:T(8,128)(2,1)}, bf16[256,1024]{1,0:T(8,128)(2,1)}, u32[]{:S(2)}, u32[]{:S(2)}) collective-permute-start(bf16[256,1024]{1,0:T(8,128)(2,1)} %slice_bitcast_fusion.2), channel_id=1, source_target_pairs={{0,1},{1,0},{2,3},{3,2},{4,5},{5,4},{6,7},{7,6},{8,9},{9,8},{10,11... | collective-permute-start | bytes 1572872 | tf_op jit(solution)/shard_map/ppermute | solution.py:21
  159.1 19.8 %copy-start.3 = (f32[4,256,1024]{2,1,0:T(8,128)S(1)}, f32[4,256,1024]{2,1,0:T(8,128)}, u32[]{:S(2)}) copy-start(f32[4,256,1024]{2,1,0:T(8,128)} %shard_map.90) | copy-start | bytes 12582916
  160.7 14.9 %collective-permute-start.30 = (bf16[256,1024]{1,0:T(8,128)(2,1)S(1)}, bf16[256,1024]{1,0:T(8,128)(2,1)S(1)}, u32[]{:S(2)}, u32[]{:S(2)}) collective-permute-start(bf16[256,1024]{1,0:T(8,128)(2,1)S(1)} %fusion.1), channel_id=1, source_target_pairs={{0,4},{1,5},{2,6},{3,7},{4,0},{5,1},{6,2},{7,3},{8,12},{9,13},{10,... | collective-permute-start | bytes 1572872 | tf_op jit(solution)/shard_map/ppermute | solution.py:21
  160.8 19.3 %collective-permute-start.26 = (bf16[256,1024]{1,0:T(8,128)(2,1)S(1)}, bf16[256,1024]{1,0:T(8,128)(2,1)S(1)}, u32[]{:S(2)}, u32[]{:S(2)}) collective-permute-start(bf16[256,1024]{1,0:T(8,128)(2,1)S(1)} %fusion.20), channel_id=1, source_target_pairs={{0,2},{1,3},{2,0},{3,1},{4,6},{5,7},{6,4},{7,5},{8,10},{9,11},{10,... | collective-permute-start | bytes 1572872 | tf_op jit(solution)/shard_map/ppermute | solution.py:21
  162.4 24.5 %collective-permute-start.25 = (bf16[256,1024]{1,0:T(8,128)(2,1)S(1)}, bf16[256,1024]{1,0:T(8,128)(2,1)S(1)}, u32[]{:S(2)}, u32[]{:S(2)}) collective-permute-start(bf16[256,1024]{1,0:T(8,128)(2,1)S(1)} %fusion.15), channel_id=1, source_target_pairs={{0,4},{1,5},{2,6},{3,7},{4,0},{5,1},{6,2},{7,3},{8,12},{9,13},{10,... | collective-permute-start | bytes 1572872 | tf_op jit(solution)/shard_map/ppermute | solution.py:21
  177.2 11.0 %collective-permute-start.31 = (bf16[256,1024]{1,0:T(8,128)(2,1)S(1)}, bf16[256,1024]{1,0:T(8,128)(2,1)S(1)}, u32[]{:S(2)}, u32[]{:S(2)}) collective-permute-start(bf16[256,1024]{1,0:T(8,128)(2,1)S(1)} %fusion.4), channel_id=1, source_target_pairs={{0,2},{1,3},{2,0},{3,1},{4,6},{5,7},{6,4},{7,5},{8,10},{9,11},{10,... | collective-permute-start | bytes 1572872 | tf_op jit(solution)/shard_map/ppermute | solution.py:21
  180.0 16.3 %collective-permute-start.28 = (bf16[256,1024]{1,0:T(8,128)(2,1)S(1)}, bf16[256,1024]{1,0:T(8,128)(2,1)S(1)}, u32[]{:S(2)}, u32[]{:S(2)}) collective-permute-start(bf16[256,1024]{1,0:T(8,128)(2,1)S(1)} %fusion.21), channel_id=1, source_target_pairs={{0,4},{1,5},{2,6},{3,7},{4,0},{5,1},{6,2},{7,3},{8,12},{9,13},{10,... | collective-permute-start | bytes 1572872 | tf_op jit(solution)/shard_map/ppermute | solution.py:21
  186.9 11.8 %copy-start.1 = (f32[52,128]{1,0:T(8,128)S(1)}, f32[52,128]{1,0:T(8,128)}, u32[]{:S(2)}) copy-start(f32[52,128]{1,0:T(8,128)} %param.15) | copy-start | bytes 79876

commit v5 on v4

--- a/solution.py
+++ b/solution.py
@@ -187,14 +187,17 @@
     return first.astype(jnp.bfloat16), rest
 
 
-def forward(diagonal, rest, kept, by_y):
-    arrived = partner(diagonal, 2 if by_y else 4).astype(jnp.float32)
+def forward(diagonal, rest, kept, halves):
     far = kept[1] + rest[0].astype(jnp.float32)
     near = kept[2] + rest[1].astype(jnp.float32)
-    if by_y:
-        far = far + arrived
+    if halves:
+        half = diagonal.shape[0] // 2
+        upper = partner(diagonal[:half], 2).astype(jnp.float32)
+        lower = partner(diagonal[half:], 4).astype(jnp.float32)
+        far = jnp.concatenate((far[:half] + upper, far[half:]), 0)
+        near = jnp.concatenate((near[:half], near[half:] + lower), 0)
     else:
-        near = near + arrived
+        far = far + partner(diagonal, 2).astype(jnp.float32)
     return far.astype(jnp.bfloat16), near.astype(jnp.bfloat16)
 
 
@@ -314,11 +317,11 @@
     hidden_b = spread_hidden(piece_b)
     diagonal, hidden_b = tie(diagonal, hidden_b)
     to_pair_b = sent_product(hidden_b)
-    forward_a = forward(diagonal, rest_a, kept_a, True)
+    forward_a = forward(diagonal, rest_a, kept_a, False)
     *forward_a, hidden_b = tie(*forward_a, hidden_b)
     kept_b = kept_product(hidden_b)
     diagonal, rest_b = exchange_pair(to_pair_b, kept_b)
-    forward_b = forward(diagonal, rest_b, kept_b, False)
+    forward_b = forward(diagonal, rest_b, kept_b, True)
     out_a = collect(*forward_a, rest_a, kept_a)
     out_b = collect(*forward_b, rest_b, kept_b)
     return jnp.concatenate((out_a, out_b), 0)

time: 200 us -> 205 us (1.025)
  waiting for transfers between devices: 40.8 us -> 46.7 us
    ppermute x28 -> x29, waiting for transfers between devices: 30.7 us -> 35.2 us  [partner(): lax.ppermute(shard, 'gx', [(i, i ^ mask) for i in range(lax.axis_size('gx...]
    convert_element_type x4 -> x2, other arithmetic: 5.27 us -> 2.5 us  [forward(): return (far.astype(jnp.bfloat16), near.astype(jnp.bfloat16))]
    unnamed x48 -> x42, local copies, waits for them, and re-layouts: 6.4 us -> 4.24 us
    ppermute x28 -> x29, starting transfers between devices: 20.5 us -> 21 us  [partner(): lax.ppermute(shard, 'gx', [(i, i ^ mask) for i in range(lax.axis_size('gx...]
  transfers between devices with their start and end apart: 32 -> 33, of which waited for: 10 -> 10; matrix products, arithmetic and copies ran while one was open for 14% -> 13% of each run, Pallas kernels for 49% -> 47%
where the time goes in v5:
time: 205 us; the launch traced here: 203 us
  Pallas kernels  99.3 us (48%)
  waiting for transfers between devices  46.7 us (23%)
  starting transfers between devices  26.7 us (13%)
  other arithmetic  15.4 us (8%)
  local copies, waits for them, and re-layouts  14.9 us (7%)
    pallas_call x3, Pallas kernels, joined_product(): pl.pallas_call(kernel, grid_spec=pltpu.PrefetchScalarGridSpec(num_scalar_...  35.6 us
    ppermute x29, waiting for transfers between devices, partner(): lax.ppermute(shard, 'gx', [(i, i ^ mask) for i in range(lax.axis_size('gx...  35.2 us
    pallas_call x2, Pallas kernels, scale_rows(): pl.pallas_call(kernel, grid=(RO,), in_specs=[pl.BlockSpec((height, column...  33.6 us
    pallas_call x4, Pallas kernels, output_product(): pl.pallas_call(kernel, grid_spec=pltpu.PrefetchScalarGridSpec(num_scalar_...  27.2 us
    ppermute x29, starting transfers between devices, partner(): lax.ppermute(shard, 'gx', [(i, i ^ mask) for i in range(lax.axis_size('gx...  21 us
    ppermute x4, waiting for transfers between devices, from_behind(): lax.ppermute(shard, 'gx', [(i, (i + by) % devices) for i in range(devices)])  11.5 us
    ppermute x4, starting transfers between devices, from_behind(): lax.ppermute(shard, 'gx', [(i, (i + by) % devices) for i in range(devices)])  5.74 us
    unnamed x42, local copies, waits for them, and re-layouts  4.24 us
  transfers between devices with their start and end apart: 33, of which 10 were waited for; matrix products, arithmetic and copies ran while one was open for 13% of the time, Pallas kernels for 47%

profile of v5, /device:TPU:0, one launch (start us, length us, event | category | flops | bytes accessed | tf_op | source)
XLA Modules:
  0.0 203.5 jit_solution(7873828846993816638)
XLA Ops:
  0.0 2.9 %shard_map.82 = (bf16[256,1024]{1,0:T(8,128)(2,1)}, bf16[256,1024]{1,0:T(8,128)(2,1)}) custom-call(bf16[512,1024]{1,0:T(8,128)(2,1)} %x_ref.1, f32[8,512]{1,0:T(8,128)} %bitcast.129), custom_call_target="tpu_custom_call" | custom-call | flops 524288 | bytes 2097152 | tf_op jit(solution)/shard_map/pallas_call | solution.py:52
  2.9 3.0 %collective-permute-start = (bf16[256,1024]{1,0:T(8,128)(2,1)}, bf16[256,1024]{1,0:T(8,128)(2,1)S(1)}, u32[]{:S(2)}, u32[]{:S(2)}) collective-permute-start(bf16[256,1024]{1,0:T(8,128)(2,1)} %get-tuple-element.33.refs_0_), channel_id=1, source_target_pairs={{0,4},{1,5},{2,6},{3,7},{4,0},{5,1},{6,2},{7,3},{8,12},{9,13},{10,... | collective-permute-start | bytes 1572872 | tf_op jit(solution)/shard_map/ppermute | solution.py:21
  5.9 1.5 collective-permute-start.1
  7.5 0.8 dynamic-slice_bitcast_fusion.4
  8.6 1.1 copy.9
  9.9 1.1 copy.10
  11.1 20.9 %shard_map.83.refs_6_.refs_4_.refs_10_ = bf16[8,1664,1024]{2,1,0:T(8,128)(2,1)} custom-call(bf16[832,8192]{1,0:T(8,128)(2,1)} %bitcast.118, bf16[832,8192]{1,0:T(8,128)(2,1)} %bitcast.119, f32[13,8192]{1,0:T(8,128)} %bitcast.120, f32[13,8192]{1,0:T(8,128)} %bitcast.121), custom_call_target="tpu_custom_call" | custom-call | flops 13631488 | bytes 54525952 | tf_op jit(solution)/shard_map/pallas_call | solution.py:76
  32.0 0.6 collective-permute-start.8
  32.7 0.4 collective-permute-start.5
  33.1 0.3 collective-permute-start.6
  33.4 0.2 collective-permute-start.7
  33.7 0.5 collective-permute-done.8.refs_3_
  34.1 1.2 collective-permute-start.3
  35.3 1.6 collective-permute-start.4
  36.9 12.8 %shard_map.84.refs_5_ = f32[1664,256]{1,0:T(8,128)} custom-call(s32[1]{0:T(128)} %bitcast.slot_ref, bf16[256,1024]{1,0:T(8,128)(2,1)} %get-tuple-element.33.refs_0_, bf16[256,1024]{1,0:T(8,128)(2,1)} %copy-done.12, bf16[256,1024]{1,0:T(8,128)(2,1)} %copy-done.7, bf16[256,1024]{1,0:T(8,128)(2,1)} %copy-done.13, bf16[256,1024]{1,0:T(8,128)(2,1)} %copy-done.8, ...), custom_call_target="tpu_custom_call" | custom-call | flops 5234491392 | bytes 20447232 | tf_op jit(solution)/shard_map/pallas_call | solution.py:126
  49.8 3.2 %collective-permute-done.3.refs_0_ = bf16[128,1024]{1,0:T(8,128)(2,1)} collective-permute-done((bf16[128,1024]{1,0:T(8,128)(2,1)S(1)}, bf16[128,1024]{1,0:T(8,128)(2,1)}, u32[]{:S(2)}, u32[]{:S(2)}) %collective-permute-start.3) | collective-permute-done | bytes 262176 | tf_op jit(solution)/shard_map/ppermute | solution.py:21
  53.0 0.5 collective-permute-start.15
  53.6 0.4 collective-permute-start.13
  54.1 0.6 collective-permute-start.10
  54.8 1.5 collective-permute-start.11
  56.3 0.7 copy-done.17
  57.0 6.2 %shard_map.85 = f32[1664,256]{1,0:T(8,128)} custom-call(s32[1]{0:T(128)} %bitcast.slot_ref, bf16[128,1024]{1,0:T(8,128)(2,1)} %collective-permute-done.3.refs_0_, bf16[128,1024]{1,0:T(8,128)(2,1)} %collective-permute-done.4.refs_1_, bf16[128,1024]{1,0:T(8,128)(2,1)} %copy-done.16, bf16[128,1024]{1,0:T(8,128)(2,1)} %copy-done.17, ...), custom_call_target="tpu_custom_call" | custom-call | flops 1744830464 | bytes 6815744 | tf_op jit(solution)/shard_map/pallas_call | solution.py:126
  63.2 1.3 fusion.27
  64.5 0.8 pad_maximum_fusion.3
  65.4 0.5 collective-permute-start.18
  66.3 1.1 copy.11
  67.5 2.6 %collective-permute-start.16 = (bf16[2,416,256]{2,1,0:T(8,128)(2,1)S(1)}, bf16[2,416,256]{2,1,0:T(8,128)(2,1)S(1)}, u32[]{:S(2)}, u32[]{:S(2)}) collective-permute-start(bf16[2,416,256]{2,1,0:T(8,128)(2,1)S(1)} %copy-done.15), channel_id=1, source_target_pairs={{0,8},{1,9},{2,10},{3,11},{4,12},{5,13},{6,14},{7,15},{8,0},{9,1},... | collective-permute-start | bytes 1277960 | tf_op jit(solution)/shard_map/ppermute | solution.py:26
  70.1 16.6 %shard_map.86 = f32[1664,256]{1,0:T(8,128)} custom-call(s32[1]{0:T(128)} %bitcast.slot_ref, bf16[256,1024]{1,0:T(8,128)(2,1)} %get-tuple-element.37.refs_0_, bf16[256,1024]{1,0:T(8,128)(2,1)} %copy-done.10, bf16[256,1024]{1,0:T(8,128)(2,1)} %copy-done.5, bf16[256,1024]{1,0:T(8,128)(2,1)} %copy-done.11, bf16[256,1024]{1,0:T(8,128)(2,1)} %copy-done.6, ...), custom_call_target="tpu_custom_call" | custom-call | flops 6979321856 | bytes 27262976 | tf_op jit(solution)/shard_map/pallas_call | solution.py:126
  86.7 1.2 fusion.29
  88.0 1.4 collective-permute-done.16
  89.8 3.0 %collective-permute-start.22 = (bf16[2,416,256]{2,1,0:T(8,128)(2,1)S(1)}, bf16[2,416,256]{2,1,0:T(8,128)(2,1)S(1)}, u32[]{:S(2)}, u32[]{:S(2)}) collective-permute-start(bf16[2,416,256]{2,1,0:T(8,128)(2,1)S(1)} %pad_maximum_fusion.4), channel_id=1, source_target_pairs={{0,8},{1,9},{2,10},{3,11},{4,12},{5,13},{6,14},{7,15},{8,0},{9,1},... | collective-permute-start | bytes 1277960 | tf_op jit(solution)/shard_map/ppermute | solution.py:26
  92.7 12.7 %shard_map.87.w_ref = bf16[8,832,1024]{2,1,0:T(8,128)(2,1)} custom-call(bf16[832,8192]{1,0:T(8,128)(2,1)} %bitcast.117, f32[13,8192]{1,0:T(8,128)} %bitcast.122), custom_call_target="tpu_custom_call" | custom-call | flops 6815744 | bytes 27262976 | tf_op jit(solution)/shard_map/pallas_call | solution.py:76
  105.4 5.5 %collective-permute-done.19 = bf16[416,256]{1,0:T(8,128)(2,1)S(1)} collective-permute-done((bf16[416,256]{1,0:T(8,128)(2,1)S(1)}, bf16[416,256]{1,0:T(8,128)(2,1)S(1)}, u32[]{:S(2)}, u32[]{:S(2)}) %collective-permute-start.19) | collective-permute-done | bytes 213024 | tf_op jit(solution)/shard_map/ppermute | solution.py:26
  110.9 0.9 maximum_select_fusion.x_ref
  111.9 6.5 %shard_map.89 = bf16[4,256,1024]{2,1,0:T(8,128)(2,1)} custom-call(s32[1]{0:T(128)} %bitcast.slot_ref, bf16[832,256]{1,0:T(8,128)(2,1)} %maximum_select_fusion.x_ref, bf16[8,832,1024]{2,1,0:T(8,128)(2,1)} %shard_map.87.w_ref), custom_call_target="tpu_custom_call" | custom-call | flops 1744830464 | bytes 6815744 | tf_op jit(solution)/shard_map/pallas_call | solution.py:160
  118.3 1.5 slice.149
  119.9 1.1 slice_bitcast_fusion.5
  121.0 0.5 collective-permute-start.20
  121.8 7.1 %shard_map.88 = f32[4,256,1024]{2,1,0:T(8,128)} custom-call(s32[1]{0:T(128)} %bitcast.slot_ref, bf16[832,256]{1,0:T(8,128)(2,1)} %maximum_select_fusion.x_ref, bf16[8,832,1024]{2,1,0:T(8,128)(2,1)} %shard_map.87.w_ref), custom_call_target="tpu_custom_call" | custom-call | flops 1744830464 | bytes 6815744 | tf_op jit(solution)/shard_map/pallas_call | solution.py:160
  128.9 4.5 %collective-permute-done.23 = bf16[416,256]{1,0:T(8,128)(2,1)S(1)} collective-permute-done((bf16[416,256]{1,0:T(8,128)(2,1)S(1)}, bf16[416,256]{1,0:T(8,128)(2,1)S(1)}, u32[]{:S(2)}, u32[]{:S(2)}) %collective-permute-start.23) | collective-permute-done | bytes 213024 | tf_op jit(solution)/shard_map/ppermute | solution.py:26
  133.4 0.9 maximum_select_fusion.1.x_ref
  134.4 2.2 %fusion.8 = bf16[256,1024]{1,0:T(8,128)(2,1)} fusion(f32[4,256,1024]{2,1,0:T(8,128)} %shard_map.88, bf16[256,1024]{1,0:T(8,128)(2,1)S(1)} %collective-permute-done.21), kind=kLoop, calls=%fused_computation.14 | loop fusion | flops 786432 | bytes 2097152 | tf_op jit(solution)/shard_map/convert_element_type | solution.py:187
  136.6 6.6 %shard_map.91 = bf16[4,256,1024]{2,1,0:T(8,128)(2,1)} custom-call(s32[1]{0:T(128)} %bitcast.slot_ref, bf16[832,256]{1,0:T(8,128)(2,1)} %maximum_select_fusion.1.x_ref, bf16[8,832,1024]{2,1,0:T(8,128)(2,1)} %shard_map.87.w_ref), custom_call_target="tpu_custom_call" | custom-call | flops 1744830464 | bytes 6815744 | tf_op jit(solution)/shard_map/pallas_call | solution.py:160
  143.2 2.7 %slice.160 = bf16[3,256,1024]{2,1,0:T(8,128)(2,1)} slice(bf16[4,256,1024]{2,1,0:T(8,128)(2,1)} %shard_map.91), slice={[1:4], [0:256], [0:1024]} | slice | bytes 3145728 | tf_op jit(solution)/shard_map/slice | solution.py:186
  145.9 1.5 collective-permute-start.24
  147.3 1.1 slice_bitcast_fusion.3
  148.4 0.3 collective-permute-start.28
  148.7 1.2 fusion.16
  149.9 10.5 %collective-permute-done.24 = bf16[256,1024]{1,0:T(8,128)(2,1)S(1)} collective-permute-done((bf16[256,1024]{1,0:T(8,128)(2,1)}, bf16[256,1024]{1,0:T(8,128)(2,1)S(1)}, u32[]{:S(2)}, u32[]{:S(2)}) %collective-permute-start.24) | collective-permute-done | bytes 524320 | tf_op jit(solution)/shard_map/ppermute | solution.py:21
  160.4 1.3 fusion.11
  161.7 7.1 %shard_map.90 = f32[4,256,1024]{2,1,0:T(8,128)} custom-call(s32[1]{0:T(128)} %bitcast.slot_ref, bf16[832,256]{1,0:T(8,128)(2,1)} %maximum_select_fusion.1.x_ref, bf16[8,832,1024]{2,1,0:T(8,128)(2,1)} %shard_map.87.w_ref), custom_call_target="tpu_custom_call" | custom-call | flops 1744830464 | bytes 6815744 | tf_op jit(solution)/shard_map/pallas_call | solution.py:160
  168.8 1.5 fusion.1
  170.4 1.5 collective-permute-start.29
  171.9 0.6 collective-permute-start.26
  172.5 1.9 collective-permute-start.25
  174.4 1.9 slice_add_fusion.1
  176.3 3.3 %collective-permute-done.31 = bf16[128,1024]{1,0:T(8,128)(2,1)S(1)} collective-permute-done((bf16[128,1024]{1,0:T(8,128)(2,1)S(1)}, bf16[128,1024]{1,0:T(8,128)(2,1)S(1)}, u32[]{:S(2)}, u32[]{:S(2)}) %collective-permute-start.31) | collective-permute-done | bytes 262176 | tf_op jit(solution)/shard_map/ppermute | solution.py:21
  179.7 1.5 collective-permute-start.32
  181.4 0.4 collective-permute-start.30
  181.9 9.0 %collective-permute-done.26 = bf16[256,1024]{1,0:T(8,128)(2,1)S(1)} collective-permute-done((bf16[256,1024]{1,0:T(8,128)(2,1)S(1)}, bf16[256,1024]{1,0:T(8,128)(2,1)S(1)}, u32[]{:S(2)}, u32[]{:S(2)}) %collective-permute-start.26) | collective-permute-done | bytes 524320 | tf_op jit(solution)/shard_map/ppermute | solution.py:21
  190.9 1.4 fusion.15
  192.3 8.6 %collective-permute-done.32 = bf16[256,1024]{1,0:T(8,128)(2,1)S(1)} collective-permute-done((bf16[256,1024]{1,0:T(8,128)(2,1)S(1)}, bf16[256,1024]{1,0:T(8,128)(2,1)S(1)}, u32[]{:S(2)}, u32[]{:S(2)}) %collective-permute-start.32) | collective-permute-done | bytes 524320 | tf_op jit(solution)/shard_map/ppermute | solution.py:21
  200.8 1.6 fusion.5
  202.4 1.0 pad_maximum_fusion
  (100 shorter events, 2.6 us)
Async XLA Ops:
  0.0 65.9 %copy-start = (f32[52,128]{1,0:T(8,128)S(1)}, f32[52,128]{1,0:T(8,128)}, u32[]{:S(2)}) copy-start(f32[52,128]{1,0:T(8,128)} %param.15) | copy-start | bytes 79876
  2.9 29.1 %collective-permute-start = (bf16[256,1024]{1,0:T(8,128)(2,1)}, bf16[256,1024]{1,0:T(8,128)(2,1)S(1)}, u32[]{:S(2)}, u32[]{:S(2)}) collective-permute-start(bf16[256,1024]{1,0:T(8,128)(2,1)} %get-tuple-element.33.refs_0_), channel_id=1, source_target_pairs={{0,4},{1,5},{2,6},{3,7},{4,0},{5,1},{6,2},{7,3},{8,12},{9,13},{10,... | collective-permute-start | bytes 1572872 | tf_op jit(solution)/shard_map/ppermute | solution.py:21
  5.9 26.1 %collective-permute-start.1 = (bf16[256,1024]{1,0:T(8,128)(2,1)}, bf16[256,1024]{1,0:T(8,128)(2,1)S(1)}, u32[]{:S(2)}, u32[]{:S(2)}) collective-permute-start(bf16[256,1024]{1,0:T(8,128)(2,1)} %get-tuple-element.33.refs_0_), channel_id=1, source_target_pairs={{0,2},{1,3},{2,0},{3,1},{4,6},{5,7},{6,4},{7,5},{8,10},{9,11},{10,... | collective-permute-start | bytes 1572872 | tf_op jit(solution)/shard_map/ppermute | solution.py:21
  7.5 24.6 %collective-permute-start.2 = (bf16[256,1024]{1,0:T(8,128)(2,1)}, bf16[256,1024]{1,0:T(8,128)(2,1)S(1)}, u32[]{:S(2)}, u32[]{:S(2)}) collective-permute-start(bf16[256,1024]{1,0:T(8,128)(2,1)} %get-tuple-element.33.refs_0_), channel_id=1, source_target_pairs={{0,1},{1,0},{2,3},{3,2},{4,5},{5,4},{6,7},{7,6},{8,9},{9,8},{10,11... | collective-permute-start | bytes 1572872 | tf_op jit(solution)/shard_map/ppermute | solution.py:21
  11.1 21.6 %copy-start.9 = (bf16[256,1024]{1,0:T(8,128)(2,1)S(1)}, bf16[256,1024]{1,0:T(8,128)(2,1)}, u32[]{:S(2)}) copy-start(bf16[256,1024]{1,0:T(8,128)(2,1)} %get-tuple-element.37.refs_0_) | copy-start | bytes 1572868
  32.0 4.9 %copy-start.7 = (bf16[256,1024]{1,0:T(8,128)(2,1)}, bf16[256,1024]{1,0:T(8,128)(2,1)S(1)}, u32[]{:S(2)}) copy-start(bf16[256,1024]{1,0:T(8,128)(2,1)S(1)} %collective-permute-done.refs_2_) | copy-start | bytes 1572868
  32.0 4.9 %copy-start.8 = (bf16[256,1024]{1,0:T(8,128)(2,1)}, bf16[256,1024]{1,0:T(8,128)(2,1)S(1)}, u32[]{:S(2)}) copy-start(bf16[256,1024]{1,0:T(8,128)(2,1)S(1)} %collective-permute-done.1.refs_4_) | copy-start | bytes 1572868
  32.0 1.1 copy-start.12
  32.0 2.1 %collective-permute-start.8 = (bf16[256,1024]{1,0:T(8,128)(2,1)S(1)}, bf16[256,1024]{1,0:T(8,128)(2,1)S(1)}, u32[]{:S(2)}, u32[]{:S(2)}) collective-permute-start(bf16[256,1024]{1,0:T(8,128)(2,1)S(1)} %collective-permute-done.refs_2_), channel_id=1, source_target_pairs={{0,1},{1,0},{2,3},{3,2},{4,5},{5,4},{6,7},{7,6},{8,9},{9,8},{10,11... | collective-permute-start | bytes 1572872 | tf_op jit(solution)/shard_map/ppermute | solution.py:21
  32.6 2.7 %collective-permute-start.9 = (bf16[256,1024]{1,0:T(8,128)(2,1)S(1)}, bf16[256,1024]{1,0:T(8,128)(2,1)S(1)}, u32[]{:S(2)}, u32[]{:S(2)}) collective-permute-start(bf16[256,1024]{1,0:T(8,128)(2,1)S(1)} %collective-permute-done.1.refs_4_), channel_id=1, source_target_pairs={{0,1},{1,0},{2,3},{3,2},{4,5},{5,4},{6,7},{7,6},{8,9},{9,8},{10,11... | collective-permute-start | bytes 1572872 | tf_op jit(solution)/shard_map/ppermute | solution.py:21
  32.7 17.0 %collective-permute-start.5 = (bf16[256,1024]{1,0:T(8,128)(2,1)S(1)}, bf16[256,1024]{1,0:T(8,128)(2,1)S(1)}, u32[]{:S(2)}, u32[]{:S(2)}) collective-permute-start(bf16[256,1024]{1,0:T(8,128)(2,1)S(1)} %copy-done.9), channel_id=1, source_target_pairs={{0,4},{1,5},{2,6},{3,7},{4,0},{5,1},{6,2},{7,3},{8,12},{9,13},{10,... | collective-permute-start | bytes 1572872 | tf_op jit(solution)/shard_map/ppermute | solution.py:21
  33.1 16.6 %collective-permute-start.6 = (bf16[256,1024]{1,0:T(8,128)(2,1)S(1)}, bf16[256,1024]{1,0:T(8,128)(2,1)S(1)}, u32[]{:S(2)}, u32[]{:S(2)}) collective-permute-start(bf16[256,1024]{1,0:T(8,128)(2,1)S(1)} %copy-done.9), channel_id=1, source_target_pairs={{0,2},{1,3},{2,0},{3,1},{4,6},{5,7},{6,4},{7,5},{8,10},{9,11},{10,... | collective-permute-start | bytes 1572872 | tf_op jit(solution)/shard_map/ppermute | solution.py:21
  33.4 19.6 %collective-permute-start.7 = (bf16[256,1024]{1,0:T(8,128)(2,1)S(1)}, bf16[256,1024]{1,0:T(8,128)(2,1)S(1)}, u32[]{:S(2)}, u32[]{:S(2)}) collective-permute-start(bf16[256,1024]{1,0:T(8,128)(2,1)S(1)} %copy-done.9), channel_id=1, source_target_pairs={{0,1},{1,0},{2,3},{3,2},{4,5},{5,4},{6,7},{7,6},{8,9},{9,8},{10,11... | collective-permute-start | bytes 1572872 | tf_op jit(solution)/shard_map/ppermute | solution.py:21
  34.1 2.8 %copy-start.13 = (bf16[256,1024]{1,0:T(8,128)(2,1)}, bf16[256,1024]{1,0:T(8,128)(2,1)S(1)}, u32[]{:S(2)}) copy-start(bf16[256,1024]{1,0:T(8,128)(2,1)S(1)} %collective-permute-done.8.refs_3_) | copy-start | bytes 1572868
  34.1 18.8 %collective-permute-start.3 = (bf16[128,1024]{1,0:T(8,128)(2,1)S(1)}, bf16[128,1024]{1,0:T(8,128)(2,1)}, u32[]{:S(2)}, u32[]{:S(2)}) collective-permute-start(bf16[128,1024]{1,0:T(8,128)(2,1)S(1)} %slice.110), channel_id=1, source_target_pairs={{0,2},{1,3},{2,0},{3,1},{4,6},{5,7},{6,4},{7,5},{8,10},{9,11},{10,... | collective-permute-start | bytes 786440 | tf_op jit(solution)/shard_map/ppermute | solution.py:21
  35.3 1.6 copy-start.14
  35.3 17.6 %collective-permute-start.4 = (bf16[128,1024]{1,0:T(8,128)(2,1)S(1)}, bf16[128,1024]{1,0:T(8,128)(2,1)}, u32[]{:S(2)}, u32[]{:S(2)}) collective-permute-start(bf16[128,1024]{1,0:T(8,128)(2,1)S(1)} %slice.111), channel_id=1, source_target_pairs={{0,4},{1,5},{2,6},{3,7},{4,0},{5,1},{6,2},{7,3},{8,12},{9,13},{10,... | collective-permute-start | bytes 786440 | tf_op jit(solution)/shard_map/ppermute | solution.py:21
  49.7 13.5 %copy-start.5 = (bf16[256,1024]{1,0:T(8,128)(2,1)}, bf16[256,1024]{1,0:T(8,128)(2,1)S(1)}, u32[]{:S(2)}) copy-start(bf16[256,1024]{1,0:T(8,128)(2,1)S(1)} %collective-permute-done.5.refs_2_) | copy-start | bytes 1572868
  49.7 13.4 %copy-start.6 = (bf16[256,1024]{1,0:T(8,128)(2,1)}, bf16[256,1024]{1,0:T(8,128)(2,1)S(1)}, u32[]{:S(2)}) copy-start(bf16[256,1024]{1,0:T(8,128)(2,1)S(1)} %collective-permute-done.6.refs_4_) | copy-start | bytes 1572868
  52.9 3.3 %copy-start.10 = (bf16[256,1024]{1,0:T(8,128)(2,1)}, bf16[256,1024]{1,0:T(8,128)(2,1)S(1)}, u32[]{:S(2)}) copy-start(bf16[256,1024]{1,0:T(8,128)(2,1)S(1)} %collective-permute-done.7.refs_1_) | copy-start | bytes 1572868
  53.0 1.8 collective-permute-start.14
  53.0 3.2 %collective-permute-start.15 = (bf16[128,1024]{1,0:T(8,128)(2,1)}, bf16[128,1024]{1,0:T(8,128)(2,1)S(1)}, u32[]{:S(2)}, u32[]{:S(2)}) collective-permute-start(bf16[128,1024]{1,0:T(8,128)(2,1)} %collective-permute-done.4.refs_1_), channel_id=1, source_target_pairs={{0,1},{1,0},{2,3},{3,2},{4,5},{5,4},{6,7},{7,6},{8,9},{9,8},{10,11... | collective-permute-start | bytes 786440 | tf_op jit(solution)/shard_map/ppermute | solution.py:21
  53.5 11.8 %collective-permute-start.12 = (bf16[256,1024]{1,0:T(8,128)(2,1)S(1)}, bf16[256,1024]{1,0:T(8,128)(2,1)S(1)}, u32[]{:S(2)}, u32[]{:S(2)}) collective-permute-start(bf16[256,1024]{1,0:T(8,128)(2,1)S(1)} %collective-permute-done.5.refs_2_), channel_id=1, source_target_pairs={{0,1},{1,0},{2,3},{3,2},{4,5},{5,4},{6,7},{7,6},{8,9},{9,8},{10,11... | collective-permute-start | bytes 1572872 | tf_op jit(solution)/shard_map/ppermute | solution.py:21
  53.6 11.7 %collective-permute-start.13 = (bf16[256,1024]{1,0:T(8,128)(2,1)S(1)}, bf16[256,1024]{1,0:T(8,128)(2,1)}, u32[]{:S(2)}, u32[]{:S(2)}) collective-permute-start(bf16[256,1024]{1,0:T(8,128)(2,1)S(1)} %collective-permute-done.6.refs_4_), channel_id=1, source_target_pairs={{0,1},{1,0},{2,3},{3,2},{4,5},{5,4},{6,7},{7,6},{8,9},{9,8},{10,11... | collective-permute-start | bytes 1572872 | tf_op jit(solution)/shard_map/ppermute | solution.py:21
  54.1 11.2 %collective-permute-start.10 = (bf16[128,1024]{1,0:T(8,128)(2,1)S(1)}, bf16[128,1024]{1,0:T(8,128)(2,1)}, u32[]{:S(2)}, u32[]{:S(2)}) collective-permute-start(bf16[128,1024]{1,0:T(8,128)(2,1)S(1)} %slice.112), channel_id=1, source_target_pairs={{0,2},{1,3},{2,0},{3,1},{4,6},{5,7},{6,4},{7,5},{8,10},{9,11},{10,... | collective-permute-start | bytes 786440 | tf_op jit(solution)/shard_map/ppermute | solution.py:21
  54.8 1.5 copy-start.16
  54.8 10.5 %collective-permute-start.11 = (bf16[128,1024]{1,0:T(8,128)(2,1)S(1)}, bf16[128,1024]{1,0:T(8,128)(2,1)}, u32[]{:S(2)}, u32[]{:S(2)}) collective-permute-start(bf16[128,1024]{1,0:T(8,128)(2,1)S(1)} %slice.113), channel_id=1, source_target_pairs={{0,4},{1,5},{2,6},{3,7},{4,0},{5,1},{6,2},{7,3},{8,12},{9,13},{10,... | collective-permute-start | bytes 786440 | tf_op jit(solution)/shard_map/ppermute | solution.py:21
  56.3 0.7 copy-start.17
  63.2 4.2 %copy-start.3 = (f32[1664,256]{1,0:T(8,128)S(1)}, f32[1664,256]{1,0:T(8,128)}, u32[]{:S(2)}) copy-start(f32[1664,256]{1,0:T(8,128)} %shard_map.85) | copy-start | bytes 5111812
  65.3 2.1 %copy-start.11 = (bf16[256,1024]{1,0:T(8,128)(2,1)}, bf16[256,1024]{1,0:T(8,128)(2,1)S(1)}, u32[]{:S(2)}) copy-start(bf16[256,1024]{1,0:T(8,128)(2,1)S(1)} %collective-permute-done.12.refs_3_) | copy-start | bytes 1572868
  65.3 4.8 %collective-permute-start.17 = (bf16[128,1024]{1,0:T(8,128)(2,1)}, bf16[128,1024]{1,0:T(8,128)(2,1)}, u32[]{:S(2)}, u32[]{:S(2)}) collective-permute-start(bf16[128,1024]{1,0:T(8,128)(2,1)} %collective-permute-done.10.refs_6_), channel_id=1, source_target_pairs={{0,1},{1,0},{2,3},{3,2},{4,5},{5,4},{6,7},{7,6},{8,9},{9,8},{10,11... | collective-permute-start | bytes 786440 | tf_op jit(solution)/shard_map/ppermute | solution.py:21
  65.4 4.7 %collective-permute-start.18 = (bf16[128,1024]{1,0:T(8,128)(2,1)}, bf16[128,1024]{1,0:T(8,128)(2,1)}, u32[]{:S(2)}, u32[]{:S(2)}) collective-permute-start(bf16[128,1024]{1,0:T(8,128)(2,1)} %collective-permute-done.11.refs_7_), channel_id=1, source_target_pairs={{0,1},{1,0},{2,3},{3,2},{4,5},{5,4},{6,7},{7,6},{8,9},{9,8},{10,11... | collective-permute-start | bytes 786440 | tf_op jit(solution)/shard_map/ppermute | solution.py:21
  66.0 1.4 copy-start.15
  67.5 21.9 %collective-permute-start.16 = (bf16[2,416,256]{2,1,0:T(8,128)(2,1)S(1)}, bf16[2,416,256]{2,1,0:T(8,128)(2,1)S(1)}, u32[]{:S(2)}, u32[]{:S(2)}) collective-permute-start(bf16[2,416,256]{2,1,0:T(8,128)(2,1)S(1)} %copy-done.15), channel_id=1, source_target_pairs={{0,8},{1,9},{2,10},{3,11},{4,12},{5,13},{6,14},{7,15},{8,0},{9,1},... | collective-permute-start | bytes 1277960 | tf_op jit(solution)/shard_map/ppermute | solution.py:26
  87.9 1.8 copy-start.4
  89.6 21.3 %collective-permute-start.19 = (bf16[416,256]{1,0:T(8,128)(2,1)S(1)}, bf16[416,256]{1,0:T(8,128)(2,1)S(1)}, u32[]{:S(2)}, u32[]{:S(2)}) collective-permute-start(bf16[416,256]{1,0:T(8,128)(2,1)S(1)} %fusion.24), channel_id=1, source_target_pairs={{0,8},{1,9},{2,10},{3,11},{4,12},{5,13},{6,14},{7,15},{8,0},{9,1},... | collective-permute-start | bytes 638984 | tf_op jit(solution)/shard_map/ppermute | solution.py:26
  89.8 31.8 %collective-permute-start.22 = (bf16[2,416,256]{2,1,0:T(8,128)(2,1)S(1)}, bf16[2,416,256]{2,1,0:T(8,128)(2,1)S(1)}, u32[]{:S(2)}, u32[]{:S(2)}) collective-permute-start(bf16[2,416,256]{2,1,0:T(8,128)(2,1)S(1)} %pad_maximum_fusion.4), channel_id=1, source_target_pairs={{0,8},{1,9},{2,10},{3,11},{4,12},{5,13},{6,14},{7,15},{8,0},{9,1},... | collective-permute-start | bytes 1277960 | tf_op jit(solution)/shard_map/ppermute | solution.py:26
  120.9 13.5 %collective-permute-start.21 = (bf16[256,1024]{1,0:T(8,128)(2,1)S(1)}, bf16[256,1024]{1,0:T(8,128)(2,1)S(1)}, u32[]{:S(2)}, u32[]{:S(2)}) collective-permute-start(bf16[256,1024]{1,0:T(8,128)(2,1)S(1)} %slice_bitcast_fusion.5), channel_id=1, source_target_pairs={{0,1},{1,0},{2,3},{3,2},{4,5},{5,4},{6,7},{7,6},{8,9},{9,8},{10,11... | collective-permute-start | bytes 1572872 | tf_op jit(solution)/shard_map/ppermute | solution.py:21
  121.0 27.7 %collective-permute-start.20 = (bf16[3,256,1024]{2,1,0:T(8,128)(2,1)S(1)}, bf16[3,256,1024]{2,1,0:T(8,128)(2,1)}, u32[]{:S(2)}, u32[]{:S(2)}) collective-permute-start(bf16[3,256,1024]{2,1,0:T(8,128)(2,1)S(1)} %slice.149), channel_id=1, source_target_pairs={{0,1},{1,0},{2,3},{3,2},{4,5},{5,4},{6,7},{7,6},{8,9},{9,8},{10,11... | collective-permute-start | bytes 4718600 | tf_op jit(solution)/shard_map/ppermute | solution.py:21
  121.7 11.7 %collective-permute-start.23 = (bf16[416,256]{1,0:T(8,128)(2,1)S(1)}, bf16[416,256]{1,0:T(8,128)(2,1)S(1)}, u32[]{:S(2)}, u32[]{:S(2)}) collective-permute-start(bf16[416,256]{1,0:T(8,128)(2,1)S(1)} %fusion.22), channel_id=1, source_target_pairs={{0,8},{1,9},{2,10},{3,11},{4,12},{5,13},{6,14},{7,15},{8,0},{9,1},... | collective-permute-start | bytes 638984 | tf_op jit(solution)/shard_map/ppermute | solution.py:26
  136.6 12.1 %copy-start.2 = (f32[4,256,1024]{2,1,0:T(8,128)S(1)}, f32[4,256,1024]{2,1,0:T(8,128)}, u32[]{:S(2)}) copy-start(f32[4,256,1024]{2,1,0:T(8,128)} %shard_map.88) | copy-start | bytes 12582916
  145.8 28.6 %collective-permute-start.27 = (bf16[3,256,1024]{2,1,0:T(8,128)(2,1)}, bf16[3,256,1024]{2,1,0:T(8,128)(2,1)S(1)}, u32[]{:S(2)}, u32[]{:S(2)}) collective-permute-start(bf16[3,256,1024]{2,1,0:T(8,128)(2,1)} %slice.160), channel_id=1, source_target_pairs={{0,1},{1,0},{2,3},{3,2},{4,5},{5,4},{6,7},{7,6},{8,9},{9,8},{10,11... | collective-permute-start | bytes 4718600 | tf_op jit(solution)/shard_map/ppermute | solution.py:21
  145.9 14.5 %collective-permute-start.24 = (bf16[256,1024]{1,0:T(8,128)(2,1)}, bf16[256,1024]{1,0:T(8,128)(2,1)S(1)}, u32[]{:S(2)}, u32[]{:S(2)}) collective-permute-start(bf16[256,1024]{1,0:T(8,128)(2,1)} %fusion.8), channel_id=1, source_target_pairs={{0,2},{1,3},{2,0},{3,1},{4,6},{5,7},{6,4},{7,5},{8,10},{9,11},{10,... | collective-permute-start | bytes 1572872 | tf_op jit(solution)/shard_map/ppermute | solution.py:21
  148.4 20.4 %collective-permute-start.28 = (bf16[256,1024]{1,0:T(8,128)(2,1)S(1)}, bf16[256,1024]{1,0:T(8,128)(2,1)}, u32[]{:S(2)}, u32[]{:S(2)}) collective-permute-start(bf16[256,1024]{1,0:T(8,128)(2,1)S(1)} %slice_bitcast_fusion.3), channel_id=1, source_target_pairs={{0,1},{1,0},{2,3},{3,2},{4,5},{5,4},{6,7},{7,6},{8,9},{9,8},{10,11... | collective-permute-start | bytes 1572872 | tf_op jit(solution)/shard_map/ppermute | solution.py:21
  170.3 9.3 %collective-permute-start.31 = (bf16[128,1024]{1,0:T(8,128)(2,1)S(1)}, bf16[128,1024]{1,0:T(8,128)(2,1)S(1)}, u32[]{:S(2)}, u32[]{:S(2)}) collective-permute-start(bf16[128,1024]{1,0:T(8,128)(2,1)S(1)} %get-tuple-element.72), channel_id=1, source_target_pairs={{0,4},{1,5},{2,6},{3,7},{4,0},{5,1},{6,2},{7,3},{8,12},{9,13},{10,... | collective-permute-start | bytes 786440 | tf_op jit(solution)/shard_map/ppermute | solution.py:21
  170.4 10.9 %collective-permute-start.29 = (bf16[128,1024]{1,0:T(8,128)(2,1)S(1)}, bf16[128,1024]{1,0:T(8,128)(2,1)S(1)}, u32[]{:S(2)}, u32[]{:S(2)}) collective-permute-start(bf16[128,1024]{1,0:T(8,128)(2,1)S(1)} %get-tuple-element.71), channel_id=1, source_target_pairs={{0,2},{1,3},{2,0},{3,1},{4,6},{5,7},{6,4},{7,5},{8,10},{9,11},{10,... | collective-permute-start | bytes 786440 | tf_op jit(solution)/shard_map/ppermute | solution.py:21
  171.9 19.0 %collective-permute-start.26 = (bf16[256,1024]{1,0:T(8,128)(2,1)S(1)}, bf16[256,1024]{1,0:T(8,128)(2,1)S(1)}, u32[]{:S(2)}, u32[]{:S(2)}) collective-permute-start(bf16[256,1024]{1,0:T(8,128)(2,1)S(1)} %fusion.16), channel_id=1, source_target_pairs={{0,2},{1,3},{2,0},{3,1},{4,6},{5,7},{6,4},{7,5},{8,10},{9,11},{10,... | collective-permute-start | bytes 1572872 | tf_op jit(solution)/shard_map/ppermute | solution.py:21
  172.5 18.4 %collective-permute-start.25 = (bf16[256,1024]{1,0:T(8,128)(2,1)S(1)}, bf16[256,1024]{1,0:T(8,128)(2,1)S(1)}, u32[]{:S(2)}, u32[]{:S(2)}) collective-permute-start(bf16[256,1024]{1,0:T(8,128)(2,1)S(1)} %fusion.11), channel_id=1, source_target_pairs={{0,4},{1,5},{2,6},{3,7},{4,0},{5,1},{6,2},{7,3},{8,12},{9,13},{10,... | collective-permute-start | bytes 1572872 | tf_op jit(solution)/shard_map/ppermute | solution.py:21
  179.7 21.1 %collective-permute-start.32 = (bf16[256,1024]{1,0:T(8,128)(2,1)S(1)}, bf16[256,1024]{1,0:T(8,128)(2,1)S(1)}, u32[]{:S(2)}, u32[]{:S(2)}) collective-permute-start(bf16[256,1024]{1,0:T(8,128)(2,1)S(1)} %pad_maximum_fusion.2), channel_id=1, source_target_pairs={{0,2},{1,3},{2,0},{3,1},{4,6},{5,7},{6,4},{7,5},{8,10},{9,11},{10,... | collective-permute-start | bytes 1572872 | tf_op jit(solution)/shard_map/ppermute | solution.py:21
  181.4 19.4 %collective-permute-start.30 = (bf16[256,1024]{1,0:T(8,128)(2,1)S(1)}, bf16[256,1024]{1,0:T(8,128)(2,1)S(1)}, u32[]{:S(2)}, u32[]{:S(2)}) collective-permute-start(bf16[256,1024]{1,0:T(8,128)(2,1)S(1)} %pad_maximum_fusion.1), channel_id=1, source_target_pairs={{0,4},{1,5},{2,6},{3,7},{4,0},{5,1},{6,2},{7,3},{8,12},{9,13},{10,... | collective-permute-start | bytes 1572872 | tf_op jit(solution)/shard_map/ppermute | solution.py:21
  190.9 12.6 %copy-start.1 = (f32[52,128]{1,0:T(8,128)S(1)}, f32[52,128]{1,0:T(8,128)}, u32[]{:S(2)}) copy-start(f32[52,128]{1,0:T(8,128)} %param.15) | copy-start | bytes 79876
